TPU v7x, 256 devices: a whole 4x4x8 slice. The times are simulated.
256 devices in a mesh: blk: 32 (over z, y_hi, core), group: 8 (over y_lo, x).
Axes of the slice: x: 4, y: 4 (y_hi: 2, y_lo: 2; y = y_hi * 2 + y_lo), z: 8, core: 2. Of those that a mesh axis runs over, the one named last changes fastest.
Arguments:
- images: bfloat16 [32768, 1152], P(('blk', 'group')), may hold values from -6 to 6
- texts: bfloat16 [32768, 1152], P(('blk', 'group')), may hold values from -6 to 6
- logit_scale: float32 [1], replicated, may hold values from 1 to 4
- logit_bias: float32 [1], replicated, may hold values from -4 to -1
Outputs:
- grad_images: float32 [32768, 1152], P(('blk', 'group'))
- grad_texts: float32 [32768, 1152], P(('blk', 'group'))
- loss: float32 [1], replicated
All inputs are finite; a program needn't handle non-finite values.
Results may differ from a plain program's by a relative error of at most 0.0015.
Values may be sent and summed in bfloat16 or wider, within the bound.
No kernel may reach another device: no remote copies, remote signals or barrier semaphores. Data moves between devices by JAX's collectives and lax.ppermute only.
A program may use at most 64 MiB of HBM per device.

v0:
```python
import math

import jax
import jax.numpy as jnp
from jax import lax
from jax.sharding import PartitionSpec as P

STEPS = 8


def from_behind(value, axis, steps):
    count = lax.axis_size(axis)
    pairs = [(source, (source + steps) % count) for source in range(count)]
    return lax.ppermute(value, axis, pairs)


def body(images, texts, logit_scale, logit_bias):
    rows = images.shape[0]
    width = images.shape[1]
    groups = lax.axis_size("group")
    steps = STEPS
    gathered = lax.all_gather(images, "group", axis=0, tiled=True)
    block_rows = gathered.shape[0]
    member = lax.axis_index("group")
    factor = logit_scale[0] / math.sqrt(width)
    weight = factor / math.sqrt(steps * block_rows)
    row_ids = lax.broadcasted_iota(jnp.int32, (block_rows, rows), 0)
    col_ids = lax.broadcasted_iota(jnp.int32, (block_rows, rows), 1)
    positive = row_ids == col_ids + member * rows
    current = texts
    carried = jnp.zeros((rows, width), jnp.float32)
    image_acc = jnp.zeros((block_rows, width), jnp.float32)
    total = jnp.float32(0.0)
    for offset in range(steps):
        if offset > 0:
            current = from_behind(current, "blk", 1)
            carried = from_behind(carried, "blk", 1)
        logits = lax.dot_general(
            gathered, current, (((1,), (1,)), ((), ())), preferred_element_type=jnp.float32
        )
        logits = logits * factor + logit_bias[0]
        if offset == 0:
            signs = jnp.where(positive, 1.0, -1.0).astype(jnp.float32)
        else:
            signs = -jnp.ones((block_rows, rows), jnp.float32)
        total = total + jnp.sum(jax.nn.softplus(-signs * logits))
        coef = (-signs * jax.nn.sigmoid(-signs * logits) * weight).astype(jnp.bfloat16)
        image_term = jnp.dot(coef, current, preferred_element_type=jnp.float32)
        text_term = lax.dot_general(
            coef, gathered, (((0,), (0,)), ((), ())), preferred_element_type=jnp.float32
        )
        image_acc = image_acc + image_term
        carried = carried + text_term
    grad_images = lax.psum_scatter(image_acc, "group", scatter_dimension=0, tiled=True)
    grad_texts = from_behind(carried, "blk", -(steps - 1))
    pairs = rows * groups * lax.axis_size("blk")
    loss = (lax.psum(total, ("blk", "group")) / pairs).reshape(1)
    return (grad_images, grad_texts, loss)


def solution(mesh):
    return jax.shard_map(
        body,
        mesh=mesh,
        in_specs=(P(("blk", "group"), None), P(("blk", "group"), None), P(), P()),
        out_specs=(P(("blk", "group"), None), P(("blk", "group"), None), P()),
        check_vma=False,
    )
```

profile of v0, /device:TPU:1, one launch (start us, length us, event | category | flops | bytes accessed | tf_op | source)
XLA Modules:
  0.0 323.5 jit_solution(5944680558269863056)
XLA Ops:
  7.9 4.4 %collective-permute-start = (bf16[128,1152]{1,0:T(8,128)(2,1)}, bf16[128,1152]{1,0:T(8,128)(2,1)S(1)}, u32[]{:S(2)}, u32[]{:S(2)}) collective-permute-start(bf16[128,1152]{1,0:T(8,128)(2,1)} %param.5), channel_id=1, source_target_pairs={{0,8},{8,16},{16,24},{24,32},{32,40},{40,48},{48,56},{56,64},{64,7... | collective-permute-start | bytes 884744 | tf_op jit(solution)/shard_map/ppermute | solution.py:14
  12.3 4.0 %collective-permute-done = bf16[128,1152]{1,0:T(8,128)(2,1)S(1)} collective-permute-done((bf16[128,1152]{1,0:T(8,128)(2,1)}, bf16[128,1152]{1,0:T(8,128)(2,1)S(1)}, u32[]{:S(2)}, u32[]{:S(2)}) %collective-permute-start) | collective-permute-done | bytes 294944 | tf_op jit(solution)/shard_map/ppermute | solution.py:14
  16.3 3.9 %collective-permute-start.1 = (bf16[128,1152]{1,0:T(8,128)(2,1)S(1)}, bf16[128,1152]{1,0:T(8,128)(2,1)S(1)}, u32[]{:S(2)}, u32[]{:S(2)}) collective-permute-start(bf16[128,1152]{1,0:T(8,128)(2,1)S(1)} %collective-permute-done), channel_id=1, source_target_pairs={{0,8},{8,16},{16,24},{24,32},{32,40},{40,48},{48,56},{56,64},{64,7... | collective-permute-start | bytes 884744 | tf_op jit(solution)/shard_map/ppermute | solution.py:14
  20.2 3.7 %collective-permute-done.1 = bf16[128,1152]{1,0:T(8,128)(2,1)S(1)} collective-permute-done((bf16[128,1152]{1,0:T(8,128)(2,1)S(1)}, bf16[128,1152]{1,0:T(8,128)(2,1)S(1)}, u32[]{:S(2)}, u32[]{:S(2)}) %collective-permute-start.1) | collective-permute-done | bytes 294944 | tf_op jit(solution)/shard_map/ppermute | solution.py:14
  24.6 4.0 %collective-permute-start.2 = (bf16[128,1152]{1,0:T(8,128)(2,1)S(1)}, bf16[128,1152]{1,0:T(8,128)(2,1)S(1)}, u32[]{:S(2)}, u32[]{:S(2)}) collective-permute-start(bf16[128,1152]{1,0:T(8,128)(2,1)S(1)} %collective-permute-done.1), channel_id=1, source_target_pairs={{0,8},{8,16},{16,24},{24,32},{32,40},{40,48},{48,56},{56,64},{64,7... | collective-permute-start | bytes 884744 | tf_op jit(solution)/shard_map/ppermute | solution.py:14
  28.6 17.1 %collective-permute-done.2 = bf16[128,1152]{1,0:T(8,128)(2,1)S(1)} collective-permute-done((bf16[128,1152]{1,0:T(8,128)(2,1)S(1)}, bf16[128,1152]{1,0:T(8,128)(2,1)S(1)}, u32[]{:S(2)}, u32[]{:S(2)}) %collective-permute-start.2) | collective-permute-done | bytes 294944 | tf_op jit(solution)/shard_map/ppermute | solution.py:14
  46.4 4.0 %collective-permute-start.3 = (bf16[128,1152]{1,0:T(8,128)(2,1)S(1)}, bf16[128,1152]{1,0:T(8,128)(2,1)S(1)}, u32[]{:S(2)}, u32[]{:S(2)}) collective-permute-start(bf16[128,1152]{1,0:T(8,128)(2,1)S(1)} %collective-permute-done.2), channel_id=1, source_target_pairs={{0,8},{8,16},{16,24},{24,32},{32,40},{40,48},{48,56},{56,64},{64,7... | collective-permute-start | bytes 884744 | tf_op jit(solution)/shard_map/ppermute | solution.py:14
  50.4 5.2 %collective-permute-done.3 = bf16[128,1152]{1,0:T(8,128)(2,1)S(1)} collective-permute-done((bf16[128,1152]{1,0:T(8,128)(2,1)S(1)}, bf16[128,1152]{1,0:T(8,128)(2,1)S(1)}, u32[]{:S(2)}, u32[]{:S(2)}) %collective-permute-start.3) | collective-permute-done | bytes 294944 | tf_op jit(solution)/shard_map/ppermute | solution.py:14
  56.3 4.0 %collective-permute-start.4 = (bf16[128,1152]{1,0:T(8,128)(2,1)S(1)}, bf16[128,1152]{1,0:T(8,128)(2,1)S(1)}, u32[]{:S(2)}, u32[]{:S(2)}) collective-permute-start(bf16[128,1152]{1,0:T(8,128)(2,1)S(1)} %collective-permute-done.3), channel_id=1, source_target_pairs={{0,8},{8,16},{16,24},{24,32},{32,40},{40,48},{48,56},{56,64},{64,7... | collective-permute-start | bytes 884744 | tf_op jit(solution)/shard_map/ppermute | solution.py:14
  60.3 3.7 %collective-permute-done.4 = bf16[128,1152]{1,0:T(8,128)(2,1)S(1)} collective-permute-done((bf16[128,1152]{1,0:T(8,128)(2,1)S(1)}, bf16[128,1152]{1,0:T(8,128)(2,1)S(1)}, u32[]{:S(2)}, u32[]{:S(2)}) %collective-permute-start.4) | collective-permute-done | bytes 294944 | tf_op jit(solution)/shard_map/ppermute | solution.py:14
  63.9 4.0 %collective-permute-start.5 = (bf16[128,1152]{1,0:T(8,128)(2,1)S(1)}, bf16[128,1152]{1,0:T(8,128)(2,1)}, u32[]{:S(2)}, u32[]{:S(2)}) collective-permute-start(bf16[128,1152]{1,0:T(8,128)(2,1)S(1)} %collective-permute-done.4), channel_id=1, source_target_pairs={{0,8},{8,16},{16,24},{24,32},{32,40},{40,48},{48,56},{56,64},{64,7... | collective-permute-start | bytes 884744 | tf_op jit(solution)/shard_map/ppermute | solution.py:14
  69.2 2.4 collective-permute-done.5
  71.6 4.1 %collective-permute-start.6 = (bf16[128,1152]{1,0:T(8,128)(2,1)}, bf16[128,1152]{1,0:T(8,128)(2,1)}, u32[]{:S(2)}, u32[]{:S(2)}) collective-permute-start(bf16[128,1152]{1,0:T(8,128)(2,1)} %collective-permute-done.5), channel_id=1, source_target_pairs={{0,8},{8,16},{16,24},{24,32},{32,40},{40,48},{48,56},{56,64},{64,7... | collective-permute-start | bytes 884744 | tf_op jit(solution)/shard_map/ppermute | solution.py:14
  75.7 3.4 %fusion.9 = (f32[]{:T(128)}, f32[1024,128]{1,0:T(8,128)S(1)}) fusion(f32[]{:T(128)} %bitcast.36, f32[]{:T(128)} %bitcast, bf16[1024,1152]{1,0:T(8,128)(2,1)} %all-gather.2.cloned.1.call-done, bf16[128,1152]{1,0:T(8,128)(2,1)} %param.5, s32[128]{0:T(128)S(1)} %iota_add_fusion), kind=kOutput, calls=%fused_computation.33 | convolution fusion | flops 303693824 | bytes 3179020 | tf_op jit(solution)/shard_map/dot_general | solution.py:38
  89.3 2.8 fusion.15
  97.8 2.6 fusion.16
  101.2 4.1 %convolution_add_fusion = f32[1024,1152]{1,0:T(8,128)} fusion(f32[1024,1152]{1,0:T(8,128)S(1)} %convolution_add_fusion.1, bf16[128,1152]{1,0:T(8,128)(2,1)} %collective-permute-done.6, f32[1024,128]{1,0:T(8,128)S(1)} %get-tuple-element.18, f32[]{:T(128)} %bitcast.2), kind=kOutput, calls=%fused_computation | convolution fusion | flops 303824896 | bytes 10256388 | tf_op jit(solution)/shard_map/dot_general | solution.py:48
  107.1 6.8 %collective-permute-done.7 = f32[128,1152]{1,0:T(8,128)S(1)} collective-permute-done((f32[128,1152]{1,0:T(8,128)S(1)}, f32[128,1152]{1,0:T(8,128)S(1)}, u32[]{:S(2)}, u32[]{:S(2)}) %collective-permute-start.7) | collective-permute-done | bytes 589856 | tf_op jit(solution)/shard_map/ppermute | solution.py:14
  114.5 4.1 %collective-permute-start.8 = (f32[128,1152]{1,0:T(8,128)S(1)}, f32[128,1152]{1,0:T(8,128)S(1)}, u32[]{:S(2)}, u32[]{:S(2)}) collective-permute-start(f32[128,1152]{1,0:T(8,128)S(1)} %convolution_add_fusion.7), channel_id=1, source_target_pairs={{0,8},{8,16},{16,24},{24,32},{32,40},{40,48},{48,56},{56,64},{64,7... | collective-permute-start | bytes 1769480 | tf_op jit(solution)/shard_map/ppermute | solution.py:14
  119.2 50.5 %collective-permute-done.8 = f32[128,1152]{1,0:T(8,128)S(1)} collective-permute-done((f32[128,1152]{1,0:T(8,128)S(1)}, f32[128,1152]{1,0:T(8,128)S(1)}, u32[]{:S(2)}, u32[]{:S(2)}) %collective-permute-start.8) | collective-permute-done | bytes 589856 | tf_op jit(solution)/shard_map/ppermute | solution.py:14
  169.7 4.1 %collective-permute-start.9 = (f32[128,1152]{1,0:T(8,128)S(1)}, f32[128,1152]{1,0:T(8,128)S(1)}, u32[]{:S(2)}, u32[]{:S(2)}) collective-permute-start(f32[128,1152]{1,0:T(8,128)S(1)} %add.184), channel_id=1, source_target_pairs={{0,8},{8,16},{16,24},{24,32},{32,40},{40,48},{48,56},{56,64},{64,7... | collective-permute-start | bytes 1769480 | tf_op jit(solution)/shard_map/ppermute | solution.py:14
  174.4 6.2 %collective-permute-done.9 = f32[128,1152]{1,0:T(8,128)S(1)} collective-permute-done((f32[128,1152]{1,0:T(8,128)S(1)}, f32[128,1152]{1,0:T(8,128)S(1)}, u32[]{:S(2)}, u32[]{:S(2)}) %collective-permute-start.9) | collective-permute-done | bytes 589856 | tf_op jit(solution)/shard_map/ppermute | solution.py:14
  180.7 4.1 %collective-permute-start.10 = (f32[128,1152]{1,0:T(8,128)S(1)}, f32[128,1152]{1,0:T(8,128)S(1)}, u32[]{:S(2)}, u32[]{:S(2)}) collective-permute-start(f32[128,1152]{1,0:T(8,128)S(1)} %add.185), channel_id=1, source_target_pairs={{0,8},{8,16},{16,24},{24,32},{32,40},{40,48},{48,56},{56,64},{64,7... | collective-permute-start | bytes 1769480 | tf_op jit(solution)/shard_map/ppermute | solution.py:14
  185.3 6.3 %collective-permute-done.10 = f32[128,1152]{1,0:T(8,128)S(1)} collective-permute-done((f32[128,1152]{1,0:T(8,128)S(1)}, f32[128,1152]{1,0:T(8,128)S(1)}, u32[]{:S(2)}, u32[]{:S(2)}) %collective-permute-start.10) | collective-permute-done | bytes 589856 | tf_op jit(solution)/shard_map/ppermute | solution.py:14
  191.7 4.1 %collective-permute-start.11 = (f32[128,1152]{1,0:T(8,128)S(1)}, f32[128,1152]{1,0:T(8,128)S(1)}, u32[]{:S(2)}, u32[]{:S(2)}) collective-permute-start(f32[128,1152]{1,0:T(8,128)S(1)} %add.186), channel_id=1, source_target_pairs={{0,8},{8,16},{16,24},{24,32},{32,40},{40,48},{48,56},{56,64},{64,7... | collective-permute-start | bytes 1769480 | tf_op jit(solution)/shard_map/ppermute | solution.py:14
  196.3 6.3 %collective-permute-done.11 = f32[128,1152]{1,0:T(8,128)S(1)} collective-permute-done((f32[128,1152]{1,0:T(8,128)S(1)}, f32[128,1152]{1,0:T(8,128)S(1)}, u32[]{:S(2)}, u32[]{:S(2)}) %collective-permute-start.11) | collective-permute-done | bytes 589856 | tf_op jit(solution)/shard_map/ppermute | solution.py:14
  202.6 4.1 %collective-permute-start.12 = (f32[128,1152]{1,0:T(8,128)S(1)}, f32[128,1152]{1,0:T(8,128)S(1)}, u32[]{:S(2)}, u32[]{:S(2)}) collective-permute-start(f32[128,1152]{1,0:T(8,128)S(1)} %add.187), channel_id=1, source_target_pairs={{0,8},{8,16},{16,24},{24,32},{32,40},{40,48},{48,56},{56,64},{64,7... | collective-permute-start | bytes 1769480 | tf_op jit(solution)/shard_map/ppermute | solution.py:14
  207.3 6.3 %collective-permute-done.12 = f32[128,1152]{1,0:T(8,128)S(1)} collective-permute-done((f32[128,1152]{1,0:T(8,128)S(1)}, f32[128,1152]{1,0:T(8,128)S(1)}, u32[]{:S(2)}, u32[]{:S(2)}) %collective-permute-start.12) | collective-permute-done | bytes 589856 | tf_op jit(solution)/shard_map/ppermute | solution.py:14
  213.6 4.1 %collective-permute-start.13 = (f32[128,1152]{1,0:T(8,128)S(1)}, f32[128,1152]{1,0:T(8,128)S(1)}, u32[]{:S(2)}, u32[]{:S(2)}) collective-permute-start(f32[128,1152]{1,0:T(8,128)S(1)} %add.188), channel_id=1, source_target_pairs={{0,8},{8,16},{16,24},{24,32},{32,40},{40,48},{48,56},{56,64},{64,7... | collective-permute-start | bytes 1769480 | tf_op jit(solution)/shard_map/ppermute | solution.py:14
  218.2 6.3 %collective-permute-done.13 = f32[128,1152]{1,0:T(8,128)S(1)} collective-permute-done((f32[128,1152]{1,0:T(8,128)S(1)}, f32[128,1152]{1,0:T(8,128)S(1)}, u32[]{:S(2)}, u32[]{:S(2)}) %collective-permute-start.13) | collective-permute-done | bytes 589856 | tf_op jit(solution)/shard_map/ppermute | solution.py:14
  224.5 7.9 %collective-permute-start.14 = (f32[128,1152]{1,0:T(8,128)S(1)}, f32[128,1152]{1,0:T(8,128)S(1)}, u32[]{:S(2)}, u32[]{:S(2)}) collective-permute-start(f32[128,1152]{1,0:T(8,128)S(1)} %add.189), channel_id=1, source_target_pairs={{0,200},{8,208},{16,216},{24,224},{32,232},{40,240},{48,248},{56,0... | collective-permute-start | bytes 1769480 | tf_op jit(solution)/shard_map/ppermute | solution.py:14
  237.5 76.6 %psum.7 = f32[]{:T(128)} all-reduce(f32[]{:T(128)S(6)} %add.204), channel_id=1, replica_groups=mesh['blk'=32,'group'=8] {'blk','group'}, use_global_device_ids=true, to_apply=%region_9.10 | all-reduce | flops 1 | bytes 8 | tf_op jit(solution)/shard_map/psum | solution.py:57
  (83 shorter events, 26.4 us)
Async XLA Ops:
  7.2 68.5 %all-gather.2.cloned.1.call-start = ((), (), s32[]{:S(2)}) async-start(), calls=%async_computation.1 | async-start | bytes 2654208 | tf_op jit(solution)/shard_map/all_gather | solution.py:22
  7.9 306.8 %reduce-scatter.2.cloned.1.call-start = ((), (), s32[]{:S(2)}) async-start(), calls=%async_computation.2 | async-start | bytes 5308416 | tf_op jit(solution)/shard_map/reduce_scatter | solution.py:54
  7.9 8.4 %collective-permute-start = (bf16[128,1152]{1,0:T(8,128)(2,1)}, bf16[128,1152]{1,0:T(8,128)(2,1)S(1)}, u32[]{:S(2)}, u32[]{:S(2)}) collective-permute-start(bf16[128,1152]{1,0:T(8,128)(2,1)} %param.5), channel_id=1, source_target_pairs={{0,8},{8,16},{16,24},{24,32},{32,40},{40,48},{48,56},{56,64},{64,7... | collective-permute-start | bytes 884744 | tf_op jit(solution)/shard_map/ppermute | solution.py:14
  16.3 63.6 %copy-start.13 = (bf16[128,1152]{1,0:T(8,128)(2,1)}, bf16[128,1152]{1,0:T(8,128)(2,1)S(1)}, u32[]{:S(2)}) copy-start(bf16[128,1152]{1,0:T(8,128)(2,1)S(1)} %collective-permute-done) | copy-start | bytes 884740
  16.3 7.5 %collective-permute-start.1 = (bf16[128,1152]{1,0:T(8,128)(2,1)S(1)}, bf16[128,1152]{1,0:T(8,128)(2,1)S(1)}, u32[]{:S(2)}, u32[]{:S(2)}) collective-permute-start(bf16[128,1152]{1,0:T(8,128)(2,1)S(1)} %collective-permute-done), channel_id=1, source_target_pairs={{0,8},{8,16},{16,24},{24,32},{32,40},{40,48},{48,56},{56,64},{64,7... | collective-permute-start | bytes 884744 | tf_op jit(solution)/shard_map/ppermute | solution.py:14
  24.6 21.1 %collective-permute-start.2 = (bf16[128,1152]{1,0:T(8,128)(2,1)S(1)}, bf16[128,1152]{1,0:T(8,128)(2,1)S(1)}, u32[]{:S(2)}, u32[]{:S(2)}) collective-permute-start(bf16[128,1152]{1,0:T(8,128)(2,1)S(1)} %collective-permute-done.1), channel_id=1, source_target_pairs={{0,8},{8,16},{16,24},{24,32},{32,40},{40,48},{48,56},{56,64},{64,7... | collective-permute-start | bytes 884744 | tf_op jit(solution)/shard_map/ppermute | solution.py:14
  46.4 9.2 %collective-permute-start.3 = (bf16[128,1152]{1,0:T(8,128)(2,1)S(1)}, bf16[128,1152]{1,0:T(8,128)(2,1)S(1)}, u32[]{:S(2)}, u32[]{:S(2)}) collective-permute-start(bf16[128,1152]{1,0:T(8,128)(2,1)S(1)} %collective-permute-done.2), channel_id=1, source_target_pairs={{0,8},{8,16},{16,24},{24,32},{32,40},{40,48},{48,56},{56,64},{64,7... | collective-permute-start | bytes 884744 | tf_op jit(solution)/shard_map/ppermute | solution.py:14
  56.3 7.7 %collective-permute-start.4 = (bf16[128,1152]{1,0:T(8,128)(2,1)S(1)}, bf16[128,1152]{1,0:T(8,128)(2,1)S(1)}, u32[]{:S(2)}, u32[]{:S(2)}) collective-permute-start(bf16[128,1152]{1,0:T(8,128)(2,1)S(1)} %collective-permute-done.3), channel_id=1, source_target_pairs={{0,8},{8,16},{16,24},{24,32},{32,40},{40,48},{48,56},{56,64},{64,7... | collective-permute-start | bytes 884744 | tf_op jit(solution)/shard_map/ppermute | solution.py:14
  63.9 15.2 %copy-start.21 = (bf16[128,1152]{1,0:T(8,128)(2,1)}, bf16[128,1152]{1,0:T(8,128)(2,1)S(1)}, u32[]{:S(2)}) copy-start(bf16[128,1152]{1,0:T(8,128)(2,1)S(1)} %collective-permute-done.4) | copy-start | bytes 884740
  63.9 7.7 %collective-permute-start.5 = (bf16[128,1152]{1,0:T(8,128)(2,1)S(1)}, bf16[128,1152]{1,0:T(8,128)(2,1)}, u32[]{:S(2)}, u32[]{:S(2)}) collective-permute-start(bf16[128,1152]{1,0:T(8,128)(2,1)S(1)} %collective-permute-done.4), channel_id=1, source_target_pairs={{0,8},{8,16},{16,24},{24,32},{32,40},{40,48},{48,56},{56,64},{64,7... | collective-permute-start | bytes 884744 | tf_op jit(solution)/shard_map/ppermute | solution.py:14
  71.6 26.2 %collective-permute-start.6 = (bf16[128,1152]{1,0:T(8,128)(2,1)}, bf16[128,1152]{1,0:T(8,128)(2,1)}, u32[]{:S(2)}, u32[]{:S(2)}) collective-permute-start(bf16[128,1152]{1,0:T(8,128)(2,1)} %collective-permute-done.5), channel_id=1, source_target_pairs={{0,8},{8,16},{16,24},{24,32},{32,40},{40,48},{48,56},{56,64},{64,7... | collective-permute-start | bytes 884744 | tf_op jit(solution)/shard_map/ppermute | solution.py:14
  75.7 3.4 %copy-start.12 = (bf16[128,1152]{1,0:T(8,128)(2,1)S(1)}, bf16[128,1152]{1,0:T(8,128)(2,1)}, u32[]{:S(2)}) copy-start(bf16[128,1152]{1,0:T(8,128)(2,1)} %param.5) | copy-start | bytes 884740
  79.1 1.9 copy-start
  84.3 8.6 %copy-start.9 = (f32[1024,128]{1,0:T(8,128)}, f32[1024,128]{1,0:T(8,128)S(1)}, u32[]{:S(2)}) copy-start(f32[1024,128]{1,0:T(8,128)S(1)} %get-tuple-element.8) | copy-start | bytes 1572868
  84.3 1.7 copy-start.20
  86.0 7.7 %copy-start.7 = (f32[1024,128]{1,0:T(8,128)}, f32[1024,128]{1,0:T(8,128)S(1)}, u32[]{:S(2)}) copy-start(f32[1024,128]{1,0:T(8,128)S(1)} %get-tuple-element.10) | copy-start | bytes 1572868
  87.6 6.9 %copy-start.5 = (f32[1024,128]{1,0:T(8,128)}, f32[1024,128]{1,0:T(8,128)S(1)}, u32[]{:S(2)}) copy-start(f32[1024,128]{1,0:T(8,128)S(1)} %get-tuple-element.12) | copy-start | bytes 1572868
  89.2 6.0 %copy-start.3 = (f32[1024,128]{1,0:T(8,128)}, f32[1024,128]{1,0:T(8,128)S(1)}, u32[]{:S(2)}) copy-start(f32[1024,128]{1,0:T(8,128)S(1)} %get-tuple-element.14) | copy-start | bytes 1572868
  89.2 2.8 copy-start.14
  107.0 6.9 %collective-permute-start.7 = (f32[128,1152]{1,0:T(8,128)S(1)}, f32[128,1152]{1,0:T(8,128)S(1)}, u32[]{:S(2)}, u32[]{:S(2)}) collective-permute-start(f32[128,1152]{1,0:T(8,128)S(1)} %fusion.23), channel_id=1, source_target_pairs={{0,8},{8,16},{16,24},{24,32},{32,40},{40,48},{48,56},{56,64},{64,7... | collective-permute-start | bytes 1769480 | tf_op jit(solution)/shard_map/ppermute | solution.py:14
  114.0 4.6 %copy-start.10 = (f32[1024,128]{1,0:T(8,128)S(1)}, f32[1024,128]{1,0:T(8,128)}, u32[]{:S(2)}) copy-start(f32[1024,128]{1,0:T(8,128)} %copy-done.9) | copy-start | bytes 1572868
  114.5 59.3 %copy-start.8 = (f32[1024,128]{1,0:T(8,128)S(1)}, f32[1024,128]{1,0:T(8,128)}, u32[]{:S(2)}) copy-start(f32[1024,128]{1,0:T(8,128)} %copy-done.7) | copy-start | bytes 1572868
  114.5 55.1 %collective-permute-start.8 = (f32[128,1152]{1,0:T(8,128)S(1)}, f32[128,1152]{1,0:T(8,128)S(1)}, u32[]{:S(2)}, u32[]{:S(2)}) collective-permute-start(f32[128,1152]{1,0:T(8,128)S(1)} %convolution_add_fusion.7), channel_id=1, source_target_pairs={{0,8},{8,16},{16,24},{24,32},{32,40},{40,48},{48,56},{56,64},{64,7... | collective-permute-start | bytes 1769480 | tf_op jit(solution)/shard_map/ppermute | solution.py:14
  169.7 15.0 %copy-start.6 = (f32[1024,128]{1,0:T(8,128)S(1)}, f32[1024,128]{1,0:T(8,128)}, u32[]{:S(2)}) copy-start(f32[1024,128]{1,0:T(8,128)} %copy-done.5) | copy-start | bytes 1572868
  169.7 10.9 %collective-permute-start.9 = (f32[128,1152]{1,0:T(8,128)S(1)}, f32[128,1152]{1,0:T(8,128)S(1)}, u32[]{:S(2)}, u32[]{:S(2)}) collective-permute-start(f32[128,1152]{1,0:T(8,128)S(1)} %add.184), channel_id=1, source_target_pairs={{0,8},{8,16},{16,24},{24,32},{32,40},{40,48},{48,56},{56,64},{64,7... | collective-permute-start | bytes 1769480 | tf_op jit(solution)/shard_map/ppermute | solution.py:14
  180.7 15.0 %copy-start.4 = (f32[1024,128]{1,0:T(8,128)S(1)}, f32[1024,128]{1,0:T(8,128)}, u32[]{:S(2)}) copy-start(f32[1024,128]{1,0:T(8,128)} %copy-done.3) | copy-start | bytes 1572868
  180.7 10.9 %collective-permute-start.10 = (f32[128,1152]{1,0:T(8,128)S(1)}, f32[128,1152]{1,0:T(8,128)S(1)}, u32[]{:S(2)}, u32[]{:S(2)}) collective-permute-start(f32[128,1152]{1,0:T(8,128)S(1)} %add.185), channel_id=1, source_target_pairs={{0,8},{8,16},{16,24},{24,32},{32,40},{40,48},{48,56},{56,64},{64,7... | collective-permute-start | bytes 1769480 | tf_op jit(solution)/shard_map/ppermute | solution.py:14
  191.7 10.9 %collective-permute-start.11 = (f32[128,1152]{1,0:T(8,128)S(1)}, f32[128,1152]{1,0:T(8,128)S(1)}, u32[]{:S(2)}, u32[]{:S(2)}) collective-permute-start(f32[128,1152]{1,0:T(8,128)S(1)} %add.186), channel_id=1, source_target_pairs={{0,8},{8,16},{16,24},{24,32},{32,40},{40,48},{48,56},{56,64},{64,7... | collective-permute-start | bytes 1769480 | tf_op jit(solution)/shard_map/ppermute | solution.py:14
  202.6 15.0 %copy-start.2 = (f32[1024,128]{1,0:T(8,128)S(1)}, f32[1024,128]{1,0:T(8,128)}, u32[]{:S(2)}) copy-start(f32[1024,128]{1,0:T(8,128)} %copy-done.1) | copy-start | bytes 1572868
  202.6 10.9 %collective-permute-start.12 = (f32[128,1152]{1,0:T(8,128)S(1)}, f32[128,1152]{1,0:T(8,128)S(1)}, u32[]{:S(2)}, u32[]{:S(2)}) collective-permute-start(f32[128,1152]{1,0:T(8,128)S(1)} %add.187), channel_id=1, source_target_pairs={{0,8},{8,16},{16,24},{24,32},{32,40},{40,48},{48,56},{56,64},{64,7... | collective-permute-start | bytes 1769480 | tf_op jit(solution)/shard_map/ppermute | solution.py:14
  213.6 10.9 %collective-permute-start.13 = (f32[128,1152]{1,0:T(8,128)S(1)}, f32[128,1152]{1,0:T(8,128)S(1)}, u32[]{:S(2)}, u32[]{:S(2)}) collective-permute-start(f32[128,1152]{1,0:T(8,128)S(1)} %add.188), channel_id=1, source_target_pairs={{0,8},{8,16},{16,24},{24,32},{32,40},{40,48},{48,56},{56,64},{64,7... | collective-permute-start | bytes 1769480 | tf_op jit(solution)/shard_map/ppermute | solution.py:14
  224.5 90.2 %collective-permute-start.14 = (f32[128,1152]{1,0:T(8,128)S(1)}, f32[128,1152]{1,0:T(8,128)S(1)}, u32[]{:S(2)}, u32[]{:S(2)}) collective-permute-start(f32[128,1152]{1,0:T(8,128)S(1)} %add.189), channel_id=1, source_target_pairs={{0,200},{8,208},{16,216},{24,224},{32,232},{40,240},{48,248},{56,0... | collective-permute-start | bytes 1769480 | tf_op jit(solution)/shard_map/ppermute | solution.py:14
  (8 other events, 8.7 us)
Sparse Core Ops, SparseCore 0:
  9.8 43.7 all-gather.1
  105.5 64.6 reduce-scatter.1
where the time goes:
time: 324 us
  waiting for transfers between devices  125 us (39%)
  blocking collectives  76.6 us (24%)
  starting transfers between devices  60.7 us (19%)
  matrix products  33.3 us (10%)
  between operations  22.5 us (7%)
  local copies, waits for them, and re-layouts  4.87 us (2%)
    ppermute x15, waiting for transfers between devices, from_behind(): return lax.ppermute(value, axis, pairs)  125 us
    psum x1, blocking collectives, body(): loss = (lax.psum(total, ('blk', 'group')) / pairs).reshape(1)  76.6 us
    ppermute x15, starting transfers between devices, from_behind(): return lax.ppermute(value, axis, pairs)  60.6 us
    dot_general x8, matrix products, body(): lax.dot_general(gathered, current, (((1,), (1,)), ((), ())), preferred_el...  17.1 us
    dot_general x8, matrix products, body(): image_term = jnp.dot(coef, current, preferred_element_type=jnp.float32)  10.6 us
  transfers between devices with their start and end apart: 17, of which 13 were waited for; matrix products, arithmetic and copies ran while one was open for 8% of the time, Pallas kernels for 0%

commit v1 on v0

v1 whole, which is shorter than its diff:
```python
import math

import jax
import jax.numpy as jnp
from jax import lax
from jax.experimental import pallas as pl
from jax.experimental.pallas import tpu as pltpu
from jax.sharding import PartitionSpec as P

STEPS = 8
TILE = 256
CODE_SCALE = 2.0**36
CODE_FLOOR = 2.0**-126


def encode(value):
    scaled = value * CODE_SCALE
    return (scaled * scaled * scaled).astype(jnp.bfloat16)


def decode(code):
    wide = code.astype(jnp.float32)
    size = jnp.abs(wide)
    root = jnp.exp2(jnp.log2(jnp.maximum(size, CODE_FLOOR)) * (1.0 / 3.0)) * (1.0 / CODE_SCALE)
    root = jnp.where(size < CODE_FLOOR, 0.0, root)
    return jnp.where(wide < 0, -root, root)


def shift_blk(value, even, odd):
    count = lax.axis_size("blk")
    pairs = [(s, (s + (odd if s % 2 else even)) % count) for s in range(count)]
    return lax.ppermute(value, "blk", pairs)


def swap_core(value):
    return shift_blk(value, 1, -1)


def shift_group(value, over_y, over_x):
    pairs = [(s, ((s // 4 + over_y) % 2) * 4 + (s + over_x) % 4) for s in range(8)]
    return lax.ppermute(value, "group", pairs)


def sum_over(value, axis, first, count):
    size = lax.axis_size(axis)
    terms = [value] + [
        lax.ppermute(value, axis, [(s, s ^ (first * j)) for s in range(size)]) for j in range(1, count)
    ]
    while len(terms) > 1:
        terms = [a + b for a, b in zip(terms[::2], terms[1::2])]
    return terms[0]


def kernel(scalars, *refs):
    image_refs, text_refs = refs[:8], refs[8:16]
    gi_own, gi_codes = refs[16], refs[17:24]
    gt_wide, gt_codes = refs[24:28], refs[28:32]
    loss_ref = refs[32]
    images, texts, text_acc, coef, gi_wide, gi_stage, gt_stage, loss_acc, in_sems, out_sems = refs[33:]
    rows = image_refs[0].shape[0]
    total = 8 * rows
    width = images.shape[1]

    def fetch(i):
        source, place = (image_refs[i], images) if i < 8 else (text_refs[i - 8], texts)
        return pltpu.make_async_copy(source, place.at[pl.ds((i % 8) * rows, rows), :], in_sems.at[i])

    for i in range(8):
        fetch(8 + i).start()
    for i in range(8):
        fetch(i).start()
    for i in range(16):
        fetch(i).wait()
    factor, bias, weight = scalars[0], scalars[1], scalars[2]
    loss_acc[...] = jnp.zeros_like(loss_acc)
    text_acc[...] = jnp.zeros_like(text_acc)

    def step(ic, _):
        at = pl.ds(pl.multiple_of(ic * TILE, TILE), TILE)
        left = images[at, :]
        for tc in range(total // TILE):
            right = texts[tc * TILE : (tc + 1) * TILE, :]
            logits = lax.dot_general(left, right, (((1,), (1,)), ((), ())), preferred_element_type=jnp.float32)
            logits = logits * factor + bias
            if tc == 0:
                row = lax.broadcasted_iota(jnp.int32, (TILE, TILE), 0) + ic * TILE
                col = lax.broadcasted_iota(jnp.int32, (TILE, TILE), 1)
                positive = jnp.logical_and(row == col, col < rows)
                logits = jnp.where(positive, -logits, logits)
            small = jnp.exp(-jnp.abs(logits))
            log1p = jnp.log(1.0 + small)
            part = jnp.exp(jnp.minimum(logits, 0.0) - log1p) * weight
            if tc == 0:
                part = jnp.where(positive, -part, part)
            coef[:, tc * TILE : (tc + 1) * TILE] = part.astype(jnp.bfloat16)
            exact = jnp.where(small < 2.0**-9, small * (1.0 - 0.5 * small), log1p)
            terms = jnp.maximum(logits, 0.0) + exact
            loss_acc[...] += jnp.sum(terms.reshape(TILE // 8, 8, TILE), axis=0)
        c = coef[...]
        grad = jnp.dot(c, texts[...], preferred_element_type=jnp.float32)

        @pl.when(ic == 0)
        def _():
            gi_wide[...] = grad[:rows]

        gi_stage[at, :] = encode(grad)
        for tc in range(total // TILE):
            place = slice(tc * TILE, (tc + 1) * TILE)
            text_acc[place, :] += lax.dot_general(
                c[:, place], left, (((0,), (0,)), ((), ())), preferred_element_type=jnp.float32
            )
        return 0

    lax.fori_loop(0, total // TILE, step, 0)
    loss_ref[...] = loss_acc[...]
    copies = [pltpu.make_async_copy(gi_wide, gi_own, out_sems.at[0])]
    for i in range(7):
        copies.append(pltpu.make_async_copy(gi_stage.at[pl.ds((i + 1) * rows, rows), :], gi_codes[i], out_sems.at[1 + i]))
    for i in range(4):
        copies.append(pltpu.make_async_copy(text_acc.at[pl.ds(i * rows, rows), :], gt_wide[i], out_sems.at[8 + i]))
    for i in range(4):
        gt_stage[i * rows : (i + 1) * rows, :] = encode(text_acc[(4 + i) * rows : (5 + i) * rows, :])
        copies.append(pltpu.make_async_copy(gt_stage.at[pl.ds(i * rows, rows), :], gt_codes[i], out_sems.at[12 + i]))
    for copy in copies:
        copy.start()
    for copy in copies:
        copy.wait()


def multiply(scalars, image_shares, text_shares):
    rows, width = image_shares[0].shape
    total = 8 * rows
    any_space = pl.BlockSpec(memory_space=pl.ANY)
    wide = jax.ShapeDtypeStruct((rows, width), jnp.float32)
    code = jax.ShapeDtypeStruct((rows, width), jnp.bfloat16)
    return pl.pallas_call(
        kernel,
        out_shape=[wide] + [code] * 7 + [wide] * 4 + [code] * 4 + [jax.ShapeDtypeStruct((8, TILE), jnp.float32)],
        in_specs=[pl.BlockSpec(memory_space=pltpu.SMEM)] + [any_space] * 16,
        out_specs=[any_space] * 16 + [pl.BlockSpec(memory_space=pltpu.VMEM)],
        scratch_shapes=[
            pltpu.VMEM((total, width), jnp.bfloat16),
            pltpu.VMEM((total, width), jnp.bfloat16),
            pltpu.VMEM((total, width), jnp.float32),
            pltpu.VMEM((TILE, total), jnp.bfloat16),
            pltpu.VMEM((rows, width), jnp.float32),
            pltpu.VMEM((total, width), jnp.bfloat16),
            pltpu.VMEM((4 * rows, width), jnp.bfloat16),
            pltpu.VMEM((8, TILE), jnp.float32),
            pltpu.SemaphoreType.DMA((16,)),
            pltpu.SemaphoreType.DMA((16,)),
        ],
        compiler_params=pltpu.CompilerParams(vmem_limit_bytes=40 * 1024 * 1024),
        cost_estimate=pl.CostEstimate(
            flops=6 * total * total * width, bytes_accessed=16 * total * width, transcendentals=3 * total * total
        ),
        name="pairs",
    )(scalars, *image_shares, *text_shares)


def body(images, texts, logit_scale, logit_bias):
    rows, width = images.shape
    core = lax.axis_index("blk") % 2
    factor = logit_scale[0] / math.sqrt(width)
    weight = factor / math.sqrt(STEPS * 8 * rows)
    scalars = jnp.stack([factor, logit_bias[0], weight])

    across = shift_group(images, 1, 0)
    behind1 = shift_blk(texts, 2, 2)
    behind2 = shift_blk(texts, 4, 4)
    direct = [shift_group(images, 0, d) for d in (1, -1, 2)]
    relayed = [shift_group(across, 0, d) for d in (1, -1, 2)]
    behind3 = shift_blk(behind1, 4, 4)
    extra = shift_blk(jnp.where(core == 0, texts, behind2), 1, 3)
    siblings = [swap_core(b) for b in (behind1, behind2, behind3)]
    image_shares = [images, across] + direct + relayed
    text_shares = [texts, behind1, behind2, behind3, extra] + siblings
    out = multiply(scalars, image_shares, text_shares)
    gi_own, gi_codes = out[0], out[1:8]
    gt_own, gt1, gt2, gt3 = out[8:12]
    gt_extra, gt_sib1, gt_sib2, gt_sib3 = out[12:16]

    loss = jnp.sum(out[16]).reshape(1, 1)

    gt3 = gt3 + decode(swap_core(gt_sib3))
    from3 = shift_blk(encode(gt3), -4, -4)
    from_extra = decode(shift_blk(gt_extra, -3, -1))
    gt1 = gt1 + decode(swap_core(gt_sib1)) + decode(from3)
    gt2 = gt2 + decode(swap_core(gt_sib2)) + jnp.where(core == 1, from_extra, 0.0)
    from1 = shift_blk(encode(gt1), -2, -2)
    from2 = shift_blk(encode(gt2), -4, -4)

    moves = [(1, 0)] + [(0, -d) for d in (1, -1, 2)] + [(1, -d) for d in (1, -1, 2)]
    back = [shift_group(g, y, x) for g, (y, x) in zip(gi_codes, moves)]

    loss = sum_over(loss, "group", 1, 8)
    loss = sum_over(loss, "blk", 4, 8)
    loss = sum_over(loss, "blk", 1, 4)
    pairs = rows * lax.axis_size("group") * lax.axis_size("blk")
    loss = loss.reshape(1) / pairs

    grad_texts = gt_own + jnp.where(core == 0, from_extra, 0.0) + decode(from1) + decode(from2)
    grad_images = gi_own
    for code in back:
        grad_images = grad_images + decode(code)
    return (grad_images, grad_texts, loss)


def solution(mesh):
    return jax.shard_map(
        body,
        mesh=mesh,
        in_specs=(P(("blk", "group"), None), P(("blk", "group"), None), P(), P()),
        out_specs=(P(("blk", "group"), None), P(("blk", "group"), None), P()),
        check_vma=False,
    )
```

time: 324 us -> 195 us (0.60)
  blocking collectives: 76.6 us -> 0 us
  waiting for transfers between devices: 125 us -> 53.6 us
  matrix products: 33.3 us -> 0 us
  starting transfers between devices: 60.7 us -> 89.8 us
  Pallas kernels: 0 us -> 17.2 us
  between operations: 22.5 us -> 14.2 us
  local copies, waits for them, and re-layouts: 4.87 us -> 12.8 us
  other arithmetic: 0.37 us -> 6.92 us
    psum x1 -> x0, blocking collectives: 76.6 us -> none  [body(): loss = (lax.psum(total, ('blk', 'group')) / pairs).reshape(1)]
    ppermute x15 -> x45, waiting for transfers between devices: 125 us -> 53.6 us  [the longest x14 24.1 us: shift_group(): return lax.ppermute(value, 'group', pairs)]
    dot_general x24 -> x0, matrix products: 33.3 us -> none  [the longest x8 17.1 us: body(): lax.dot_general(gathered, current, (((1,), (1,)), ((), ())), preferred_el...]
    ppermute x15 -> x45, starting transfers between devices: 60.6 us -> 89.8 us  [the longest x17 52.9 us: sum_over(): lax.ppermute(value, axis, [(s, s ^ first * j) for s in range(size)])]
    pallas_call x0 -> x1, Pallas kernels: none -> 17.2 us  [multiply(): pl.pallas_call(kernel, out_shape=[wide] + [code] * 7 + [wide] * 4 + [code...]
    unnamed x47 -> x42, local copies, waits for them, and re-layouts: 4.87 us -> 12.8 us
    add x7 -> x2, other arithmetic: 0.37 us -> 4.52 us  [the longest x1 2.82 us: body(): grad_images = grad_images + decode(code)]
  transfers between devices with their start and end apart: 17 -> 45, of which waited for: 13 -> 16; matrix products, arithmetic and copies ran while one was open for 8% -> 3% of each run, Pallas kernels for 0% -> 0%
where the time goes in v1:
time: 195 us
  starting transfers between devices  89.8 us (46%)
  waiting for transfers between devices  53.6 us (27%)
  Pallas kernels  17.2 us (9%)
  between operations  14.2 us (7%)
  local copies, waits for them, and re-layouts  12.8 us (7%)
  other arithmetic  6.92 us (4%)
    ppermute x17, starting transfers between devices, sum_over(): lax.ppermute(value, axis, [(s, s ^ first * j) for s in range(size)])  52.9 us
    ppermute x14, waiting for transfers between devices, shift_group(): return lax.ppermute(value, 'group', pairs)  24.1 us
    ppermute x14, waiting for transfers between devices, shift_blk(): return lax.ppermute(value, 'blk', pairs)  23.1 us
    ppermute x14, starting transfers between devices, shift_blk(): return lax.ppermute(value, 'blk', pairs)  21.4 us
    pallas_call x1, Pallas kernels, multiply(): pl.pallas_call(kernel, out_shape=[wide] + [code] * 7 + [wide] * 4 + [code...  17.2 us
    ppermute x14, starting transfers between devices, shift_group(): return lax.ppermute(value, 'group', pairs)  15.6 us
    unnamed x42, local copies, waits for them, and re-layouts  12.8 us
    ppermute x17, waiting for transfers between devices, sum_over(): lax.ppermute(value, axis, [(s, s ^ first * j) for s in range(size)])  6.37 us
  transfers between devices with their start and end apart: 45, of which 16 were waited for; matrix products, arithmetic and copies ran while one was open for 3% of the time, Pallas kernels for 0%

profile of v1, /device:TPU:1, one launch (start us, length us, event | category | flops | bytes accessed | tf_op | source)
XLA Modules:
  0.0 194.7 jit_solution(16962036198270933662)
XLA Ops:
  0.6 2.5 %collective-permute-start.8 = (bf16[128,1152]{1,0:T(8,128)(2,1)}, bf16[128,1152]{1,0:T(8,128)(2,1)S(1)}, u32[]{:S(2)}, u32[]{:S(2)}) collective-permute-start(bf16[128,1152]{1,0:T(8,128)(2,1)} %refs_8_.1), channel_id=1, source_target_pairs={{0,32},{8,40},{16,48},{24,56},{32,64},{40,72},{48,80},{56,88},{64,... | collective-permute-start | bytes 884744 | tf_op jit(solution)/shard_map/ppermute | solution.py:32
  3.2 2.9 %collective-permute-start.7 = (bf16[128,1152]{1,0:T(8,128)(2,1)}, bf16[128,1152]{1,0:T(8,128)(2,1)S(1)}, u32[]{:S(2)}, u32[]{:S(2)}) collective-permute-start(bf16[128,1152]{1,0:T(8,128)(2,1)} %refs_8_.1), channel_id=1, source_target_pairs={{0,16},{8,24},{16,32},{24,40},{32,48},{40,56},{48,64},{56,72},{64,... | collective-permute-start | bytes 884744 | tf_op jit(solution)/shard_map/ppermute | solution.py:32
  6.1 2.5 %collective-permute-start.2 = (bf16[128,1152]{1,0:T(8,128)(2,1)}, bf16[128,1152]{1,0:T(8,128)(2,1)S(1)}, u32[]{:S(2)}, u32[]{:S(2)}) collective-permute-start(bf16[128,1152]{1,0:T(8,128)(2,1)} %refs_0_.1), channel_id=1, source_target_pairs={{0,3},{1,0},{2,1},{3,2},{4,7},{5,4},{6,5},{7,6},{8,11},{9,8},{10,9... | collective-permute-start | bytes 884744 | tf_op jit(solution)/shard_map/ppermute | solution.py:41
  9.0 5.1 %collective-permute-done.8.refs_10_ = bf16[128,1152]{1,0:T(8,128)(2,1)S(1)} collective-permute-done((bf16[128,1152]{1,0:T(8,128)(2,1)}, bf16[128,1152]{1,0:T(8,128)(2,1)S(1)}, u32[]{:S(2)}, u32[]{:S(2)}) %collective-permute-start.8) | collective-permute-done | bytes 294944 | tf_op jit(solution)/shard_map/ppermute | solution.py:32
  14.1 2.7 %collective-permute-start.3 = (bf16[128,1152]{1,0:T(8,128)(2,1)}, bf16[128,1152]{1,0:T(8,128)(2,1)S(1)}, u32[]{:S(2)}, u32[]{:S(2)}) collective-permute-start(bf16[128,1152]{1,0:T(8,128)(2,1)} %refs_0_.1), channel_id=1, source_target_pairs={{0,2},{1,3},{2,0},{3,1},{4,6},{5,7},{6,4},{7,5},{8,10},{9,11},{10,... | collective-permute-start | bytes 884744 | tf_op jit(solution)/shard_map/ppermute | solution.py:41
  16.8 6.2 %collective-permute-done.7.refs_9_ = bf16[128,1152]{1,0:T(8,128)(2,1)S(1)} collective-permute-done((bf16[128,1152]{1,0:T(8,128)(2,1)}, bf16[128,1152]{1,0:T(8,128)(2,1)S(1)}, u32[]{:S(2)}, u32[]{:S(2)}) %collective-permute-start.7) | collective-permute-done | bytes 294944 | tf_op jit(solution)/shard_map/ppermute | solution.py:32
  25.8 2.6 %collective-permute-start.11 = (bf16[128,1152]{1,0:T(8,128)(2,1)S(1)}, bf16[128,1152]{1,0:T(8,128)(2,1)S(1)}, u32[]{:S(2)}, u32[]{:S(2)}) collective-permute-start(bf16[128,1152]{1,0:T(8,128)(2,1)S(1)} %collective-permute-done.7.refs_9_), channel_id=1, source_target_pairs={{0,8},{8,0},{16,24},{24,16},{32,40},{40,32},{48,56},{56,48},{64,72... | collective-permute-start | bytes 884744 | tf_op jit(solution)/shard_map/ppermute | solution.py:32
  31.5 5.5 %collective-permute-done.9.refs_11_ = bf16[128,1152]{1,0:T(8,128)(2,1)S(1)} collective-permute-done((bf16[128,1152]{1,0:T(8,128)(2,1)S(1)}, bf16[128,1152]{1,0:T(8,128)(2,1)S(1)}, u32[]{:S(2)}, u32[]{:S(2)}) %collective-permute-start.9) | collective-permute-done | bytes 294944 | tf_op jit(solution)/shard_map/ppermute | solution.py:32
  39.4 4.3 %collective-permute-done.5.refs_6_ = bf16[128,1152]{1,0:T(8,128)(2,1)S(1)} collective-permute-done((bf16[128,1152]{1,0:T(8,128)(2,1)S(1)}, bf16[128,1152]{1,0:T(8,128)(2,1)S(1)}, u32[]{:S(2)}, u32[]{:S(2)}) %collective-permute-start.5) | collective-permute-done | bytes 294944 | tf_op jit(solution)/shard_map/ppermute | solution.py:41
  49.5 17.2 %pairs.1 = (f32[128,1152]{1,0:T(8,128)S(1)}, bf16[128,1152]{1,0:T(8,128)(2,1)S(1)}, bf16[128,1152]{1,0:T(8,128)(2,1)S(1)}, bf16[128,1152]{1,0:T(8,128)(2,1)S(1)}...) custom-call(f32[3]{0:T(128)S(1)} %pad_maximum_fusion.scalars, ...), custom_call_target="tpu_custom_call" | custom-call | flops 7247757312 | bytes 18874368 | tf_op jit(solution)/shard_map/pairs/pallas_call | solution.py:136
  75.3 2.9 %collective-permute-start.32 = (f32[1,1]{1,0:T(1,128)}, f32[1,1]{1,0:T(1,128)}, u32[]{:S(2)}, u32[]{:S(2)}) collective-permute-start(f32[1,1]{1,0:T(1,128)} %bitcast), channel_id=1, source_target_pairs={{0,5},{1,4},{2,7},{3,6},{4,1},{5,0},{6,3},{7,2},{8,13},{9,12},{10,... | collective-permute-start | bytes 20 | tf_op jit(solution)/shard_map/ppermute | solution.py:47
  81.4 2.3 %collective-permute-start.28 = (f32[1,1]{1,0:T(1,128)}, f32[1,1]{1,0:T(1,128)}, u32[]{:S(2)}, u32[]{:S(2)}) collective-permute-start(f32[1,1]{1,0:T(1,128)} %bitcast), channel_id=1, source_target_pairs={{0,1},{1,0},{2,3},{3,2},{4,5},{5,4},{6,7},{7,6},{8,9},{9,8},{10,11... | collective-permute-start | bytes 20 | tf_op jit(solution)/shard_map/ppermute | solution.py:47
  89.9 2.9 %collective-permute-start.41 = (f32[1,1]{1,0:T(1,128)}, f32[1,1]{1,0:T(1,128)}, u32[]{:S(2)}, u32[]{:S(2)}) collective-permute-start(f32[1,1]{1,0:T(1,128)} %add.122), channel_id=1, source_target_pairs={{0,224},{8,232},{16,240},{24,248},{32,192},{40,200},{48,208},{56,2... | collective-permute-start | bytes 20 | tf_op jit(solution)/shard_map/ppermute | solution.py:47
  93.5 6.1 %collective-permute-start.40 = (f32[1,1]{1,0:T(1,128)}, f32[1,1]{1,0:T(1,128)}, u32[]{:S(2)}, u32[]{:S(2)}) collective-permute-start(f32[1,1]{1,0:T(1,128)} %add.122), channel_id=1, source_target_pairs={{0,192},{8,200},{16,208},{24,216},{32,224},{40,232},{48,240},{56,2... | collective-permute-start | bytes 20 | tf_op jit(solution)/shard_map/ppermute | solution.py:47
  99.8 5.4 %collective-permute-start.39 = (f32[1,1]{1,0:T(1,128)}, f32[1,1]{1,0:T(1,128)}, u32[]{:S(2)}, u32[]{:S(2)}) collective-permute-start(f32[1,1]{1,0:T(1,128)} %add.122), channel_id=1, source_target_pairs={{0,160},{8,168},{16,176},{24,184},{32,128},{40,136},{48,144},{56,1... | collective-permute-start | bytes 20 | tf_op jit(solution)/shard_map/ppermute | solution.py:47
  106.3 3.6 %collective-permute-start.38 = (f32[1,1]{1,0:T(1,128)}, f32[1,1]{1,0:T(1,128)}, u32[]{:S(2)}, u32[]{:S(2)}) collective-permute-start(f32[1,1]{1,0:T(1,128)} %add.122), channel_id=1, source_target_pairs={{0,128},{8,136},{16,144},{24,152},{32,160},{40,168},{48,176},{56,1... | collective-permute-start | bytes 20 | tf_op jit(solution)/shard_map/ppermute | solution.py:47
  109.9 2.8 %collective-permute-done.38 = f32[1,1]{1,0:T(1,128)} collective-permute-done((f32[1,1]{1,0:T(1,128)}, f32[1,1]{1,0:T(1,128)}, u32[]{:S(2)}, u32[]{:S(2)}) %collective-permute-start.38) | collective-permute-done | bytes 36 | tf_op jit(solution)/shard_map/ppermute | solution.py:47
  115.2 4.6 %collective-permute-start.37 = (f32[1,1]{1,0:T(1,128)}, f32[1,1]{1,0:T(1,128)}, u32[]{:S(2)}, u32[]{:S(2)}) collective-permute-start(f32[1,1]{1,0:T(1,128)} %add.122), channel_id=1, source_target_pairs={{0,96},{8,104},{16,112},{24,120},{32,64},{40,72},{48,80},{56,88},{... | collective-permute-start | bytes 20 | tf_op jit(solution)/shard_map/ppermute | solution.py:47
  121.3 2.4 %collective-permute-done.36 = f32[1,1]{1,0:T(1,128)} collective-permute-done((f32[1,1]{1,0:T(1,128)}, f32[1,1]{1,0:T(1,128)}, u32[]{:S(2)}, u32[]{:S(2)}) %collective-permute-start.36) | collective-permute-done | bytes 36 | tf_op jit(solution)/shard_map/ppermute | solution.py:47
  124.9 11.9 %collective-permute-start.42 = (f32[1,1]{1,0:T(1,128)}, f32[1,1]{1,0:T(1,128)}, u32[]{:S(2)}, u32[]{:S(2)}) collective-permute-start(f32[1,1]{1,0:T(1,128)} %add.129), channel_id=1, source_target_pairs={{0,8},{8,0},{16,24},{24,16},{32,40},{40,32},{48,56},{56,48},{64,72... | collective-permute-start | bytes 20 | tf_op jit(solution)/shard_map/ppermute | solution.py:47
  136.8 3.9 %collective-permute-start.44 = (f32[1,1]{1,0:T(1,128)}, f32[1,1]{1,0:T(1,128)}, u32[]{:S(2)}, u32[]{:S(2)}) collective-permute-start(f32[1,1]{1,0:T(1,128)} %add.129), channel_id=1, source_target_pairs={{0,24},{8,16},{16,8},{24,0},{32,56},{40,48},{48,40},{56,32},{64,88... | collective-permute-start | bytes 20 | tf_op jit(solution)/shard_map/ppermute | solution.py:47
  141.4 3.7 %collective-permute-start.43 = (f32[1,1]{1,0:T(1,128)}, f32[1,1]{1,0:T(1,128)}, u32[]{:S(2)}, u32[]{:S(2)}) collective-permute-start(f32[1,1]{1,0:T(1,128)} %add.129), channel_id=1, source_target_pairs={{0,16},{8,24},{16,0},{24,8},{32,48},{40,56},{48,32},{56,40},{64,80... | collective-permute-start | bytes 20 | tf_op jit(solution)/shard_map/ppermute | solution.py:47
  149.0 2.9 %collective-permute-done.21 = bf16[128,1152]{1,0:T(8,128)(2,1)S(1)} collective-permute-done((bf16[128,1152]{1,0:T(8,128)(2,1)}, bf16[128,1152]{1,0:T(8,128)(2,1)S(1)}, u32[]{:S(2)}, u32[]{:S(2)}) %collective-permute-start.21) | collective-permute-done | bytes 294944 | tf_op jit(solution)/shard_map/ppermute | solution.py:32
  152.0 2.6 %collective-permute-start.24 = (bf16[128,1152]{1,0:T(8,128)(2,1)S(1)}, bf16[128,1152]{1,0:T(8,128)(2,1)S(1)}, u32[]{:S(2)}, u32[]{:S(2)}) collective-permute-start(bf16[128,1152]{1,0:T(8,128)(2,1)S(1)} %fusion.115), channel_id=1, source_target_pairs={{0,224},{8,232},{16,240},{24,248},{32,0},{40,8},{48,16},{56,24},{6... | collective-permute-start | bytes 884744 | tf_op jit(solution)/shard_map/ppermute | solution.py:32
  157.0 2.3 %collective-permute-start.18 = (bf16[128,1152]{1,0:T(8,128)(2,1)S(1)}, bf16[128,1152]{1,0:T(8,128)(2,1)S(1)}, u32[]{:S(2)}, u32[]{:S(2)}) collective-permute-start(bf16[128,1152]{1,0:T(8,128)(2,1)S(1)} %get-tuple-element.25), channel_id=1, source_target_pairs={{0,7},{1,4},{2,5},{3,6},{4,3},{5,0},{6,1},{7,2},{8,15},{9,12},{10,... | collective-permute-start | bytes 884744 | tf_op jit(solution)/shard_map/ppermute | solution.py:41
  160.5 2.1 %collective-permute-start.20 = (bf16[128,1152]{1,0:T(8,128)(2,1)S(1)}, bf16[128,1152]{1,0:T(8,128)(2,1)S(1)}, u32[]{:S(2)}, u32[]{:S(2)}) collective-permute-start(bf16[128,1152]{1,0:T(8,128)(2,1)S(1)} %get-tuple-element.27), channel_id=1, source_target_pairs={{0,6},{1,7},{2,4},{3,5},{4,2},{5,3},{6,0},{7,1},{8,14},{9,15},{10,... | collective-permute-start | bytes 884744 | tf_op jit(solution)/shard_map/ppermute | solution.py:41
  163.3 3.5 %collective-permute-start.27 = (bf16[128,1152]{1,0:T(8,128)(2,1)S(1)}, bf16[128,1152]{1,0:T(8,128)(2,1)S(1)}, u32[]{:S(2)}, u32[]{:S(2)}) collective-permute-start(bf16[128,1152]{1,0:T(8,128)(2,1)S(1)} %fusion.116), channel_id=1, source_target_pairs={{0,224},{8,232},{16,240},{24,248},{32,0},{40,8},{48,16},{56,24},{6... | collective-permute-start | bytes 884744 | tf_op jit(solution)/shard_map/ppermute | solution.py:32
  166.8 2.1 %collective-permute-start.25 = (bf16[128,1152]{1,0:T(8,128)(2,1)S(1)}, bf16[128,1152]{1,0:T(8,128)(2,1)S(1)}, u32[]{:S(2)}, u32[]{:S(2)}) collective-permute-start(bf16[128,1152]{1,0:T(8,128)(2,1)S(1)} %fusion.117), channel_id=1, source_target_pairs={{0,240},{8,248},{16,0},{24,8},{32,16},{40,24},{48,32},{56,40},{64,... | collective-permute-start | bytes 884744 | tf_op jit(solution)/shard_map/ppermute | solution.py:32
  168.9 9.9 %collective-permute-done.18 = bf16[128,1152]{1,0:T(8,128)(2,1)S(1)} collective-permute-done((bf16[128,1152]{1,0:T(8,128)(2,1)S(1)}, bf16[128,1152]{1,0:T(8,128)(2,1)S(1)}, u32[]{:S(2)}, u32[]{:S(2)}) %collective-permute-start.18) | collective-permute-done | bytes 294944 | tf_op jit(solution)/shard_map/ppermute | solution.py:41
  178.8 7.9 %collective-permute-done.20 = bf16[128,1152]{1,0:T(8,128)(2,1)S(1)} collective-permute-done((bf16[128,1152]{1,0:T(8,128)(2,1)S(1)}, bf16[128,1152]{1,0:T(8,128)(2,1)S(1)}, u32[]{:S(2)}, u32[]{:S(2)}) %collective-permute-start.20) | collective-permute-done | bytes 294944 | tf_op jit(solution)/shard_map/ppermute | solution.py:41
  186.7 2.8 %fusion.104 = f32[128,1152]{1,0:T(8,128)} fusion(f32[128,1152]{1,0:T(8,128)S(1)} %copy-done.20, bf16[128,1152]{1,0:T(8,128)(2,1)S(1)} %collective-permute-done.14, bf16[128,1152]{1,0:T(8,128)(2,1)S(1)} %collective-permute-done.15, bf16[128,1152]{1,0:T(8,128)(2,1)S(1)} %collective-permute-done.16, bf16[128,1152]{1,0:T(8,128)(2,1)S(1)} %collective-permute-done.17, ...), kind=kLoop, calls=%fused_computation.149 | loop fusion | flops 11354112 | bytes 3244032 | tf_op jit(solution)/shard_map/add | solution.py:205
  189.6 2.3 %collective-permute-done.25 = bf16[128,1152]{1,0:T(8,128)(2,1)S(1)} collective-permute-done((bf16[128,1152]{1,0:T(8,128)(2,1)S(1)}, bf16[128,1152]{1,0:T(8,128)(2,1)S(1)}, u32[]{:S(2)}, u32[]{:S(2)}) %collective-permute-start.25) | collective-permute-done | bytes 294944 | tf_op jit(solution)/shard_map/ppermute | solution.py:32
  (109 shorter events, 38.0 us)
Async XLA Ops:
  0.6 13.4 %collective-permute-start.8 = (bf16[128,1152]{1,0:T(8,128)(2,1)}, bf16[128,1152]{1,0:T(8,128)(2,1)S(1)}, u32[]{:S(2)}, u32[]{:S(2)}) collective-permute-start(bf16[128,1152]{1,0:T(8,128)(2,1)} %refs_8_.1), channel_id=1, source_target_pairs={{0,32},{8,40},{16,48},{24,56},{32,64},{40,72},{48,80},{56,88},{64,... | collective-permute-start | bytes 884744 | tf_op jit(solution)/shard_map/ppermute | solution.py:32
  3.2 19.9 %collective-permute-start.7 = (bf16[128,1152]{1,0:T(8,128)(2,1)}, bf16[128,1152]{1,0:T(8,128)(2,1)S(1)}, u32[]{:S(2)}, u32[]{:S(2)}) collective-permute-start(bf16[128,1152]{1,0:T(8,128)(2,1)} %refs_8_.1), channel_id=1, source_target_pairs={{0,16},{8,24},{16,32},{24,40},{32,48},{40,56},{48,64},{56,72},{64,... | collective-permute-start | bytes 884744 | tf_op jit(solution)/shard_map/ppermute | solution.py:32
  6.1 17.0 %collective-permute-start.2 = (bf16[128,1152]{1,0:T(8,128)(2,1)}, bf16[128,1152]{1,0:T(8,128)(2,1)S(1)}, u32[]{:S(2)}, u32[]{:S(2)}) collective-permute-start(bf16[128,1152]{1,0:T(8,128)(2,1)} %refs_0_.1), channel_id=1, source_target_pairs={{0,3},{1,0},{2,1},{3,2},{4,7},{5,4},{6,5},{7,6},{8,11},{9,8},{10,9... | collective-permute-start | bytes 884744 | tf_op jit(solution)/shard_map/ppermute | solution.py:41
  8.6 16.5 %collective-permute-start.1 = (bf16[128,1152]{1,0:T(8,128)(2,1)}, bf16[128,1152]{1,0:T(8,128)(2,1)S(1)}, u32[]{:S(2)}, u32[]{:S(2)}) collective-permute-start(bf16[128,1152]{1,0:T(8,128)(2,1)} %refs_0_.1), channel_id=1, source_target_pairs={{0,1},{1,2},{2,3},{3,0},{4,5},{5,6},{6,7},{7,4},{8,9},{9,10},{10,1... | collective-permute-start | bytes 884744 | tf_op jit(solution)/shard_map/ppermute | solution.py:41
  8.6 17.2 %collective-permute-start = (bf16[128,1152]{1,0:T(8,128)(2,1)}, bf16[128,1152]{1,0:T(8,128)(2,1)S(1)}, u32[]{:S(2)}, u32[]{:S(2)}) collective-permute-start(bf16[128,1152]{1,0:T(8,128)(2,1)} %refs_0_.1), channel_id=1, source_target_pairs={{0,4},{1,5},{2,6},{3,7},{4,0},{5,1},{6,2},{7,3},{8,12},{9,13},{10,... | collective-permute-start | bytes 884744 | tf_op jit(solution)/shard_map/ppermute | solution.py:41
  14.1 15.0 %collective-permute-start.3 = (bf16[128,1152]{1,0:T(8,128)(2,1)}, bf16[128,1152]{1,0:T(8,128)(2,1)S(1)}, u32[]{:S(2)}, u32[]{:S(2)}) collective-permute-start(bf16[128,1152]{1,0:T(8,128)(2,1)} %refs_0_.1), channel_id=1, source_target_pairs={{0,2},{1,3},{2,0},{3,1},{4,6},{5,7},{6,4},{7,5},{8,10},{9,11},{10,... | collective-permute-start | bytes 884744 | tf_op jit(solution)/shard_map/ppermute | solution.py:41
  23.8 6.4 %collective-permute-start.12 = (bf16[128,1152]{1,0:T(8,128)(2,1)S(1)}, bf16[128,1152]{1,0:T(8,128)(2,1)S(1)}, u32[]{:S(2)}, u32[]{:S(2)}) collective-permute-start(bf16[128,1152]{1,0:T(8,128)(2,1)S(1)} %collective-permute-done.8.refs_10_), channel_id=1, source_target_pairs={{0,8},{8,0},{16,24},{24,16},{32,40},{40,32},{48,56},{56,48},{64,72... | collective-permute-start | bytes 884744 | tf_op jit(solution)/shard_map/ppermute | solution.py:32
  25.8 11.2 %collective-permute-start.9 = (bf16[128,1152]{1,0:T(8,128)(2,1)S(1)}, bf16[128,1152]{1,0:T(8,128)(2,1)S(1)}, u32[]{:S(2)}, u32[]{:S(2)}) collective-permute-start(bf16[128,1152]{1,0:T(8,128)(2,1)S(1)} %collective-permute-done.7.refs_9_), channel_id=1, source_target_pairs={{0,32},{8,40},{16,48},{24,56},{32,64},{40,72},{48,80},{56,88},{64,... | collective-permute-start | bytes 884744 | tf_op jit(solution)/shard_map/ppermute | solution.py:32
  25.8 13.6 %collective-permute-start.11 = (bf16[128,1152]{1,0:T(8,128)(2,1)S(1)}, bf16[128,1152]{1,0:T(8,128)(2,1)S(1)}, u32[]{:S(2)}, u32[]{:S(2)}) collective-permute-start(bf16[128,1152]{1,0:T(8,128)(2,1)S(1)} %collective-permute-done.7.refs_9_), channel_id=1, source_target_pairs={{0,8},{8,0},{16,24},{24,16},{32,40},{40,32},{48,56},{56,48},{64,72... | collective-permute-start | bytes 884744 | tf_op jit(solution)/shard_map/ppermute | solution.py:32
  29.1 10.3 %collective-permute-start.6 = (bf16[128,1152]{1,0:T(8,128)(2,1)S(1)}, bf16[128,1152]{1,0:T(8,128)(2,1)S(1)}, u32[]{:S(2)}, u32[]{:S(2)}) collective-permute-start(bf16[128,1152]{1,0:T(8,128)(2,1)S(1)} %collective-permute-done.refs_1_), channel_id=1, source_target_pairs={{0,2},{1,3},{2,0},{3,1},{4,6},{5,7},{6,4},{7,5},{8,10},{9,11},{10,... | collective-permute-start | bytes 884744 | tf_op jit(solution)/shard_map/ppermute | solution.py:41
  29.3 14.4 %collective-permute-start.5 = (bf16[128,1152]{1,0:T(8,128)(2,1)S(1)}, bf16[128,1152]{1,0:T(8,128)(2,1)S(1)}, u32[]{:S(2)}, u32[]{:S(2)}) collective-permute-start(bf16[128,1152]{1,0:T(8,128)(2,1)S(1)} %collective-permute-done.refs_1_), channel_id=1, source_target_pairs={{0,3},{1,0},{2,1},{3,2},{4,7},{5,4},{6,5},{7,6},{8,11},{9,8},{10,9... | collective-permute-start | bytes 884744 | tf_op jit(solution)/shard_map/ppermute | solution.py:41
  30.1 15.5 %collective-permute-start.4 = (bf16[128,1152]{1,0:T(8,128)(2,1)S(1)}, bf16[128,1152]{1,0:T(8,128)(2,1)S(1)}, u32[]{:S(2)}, u32[]{:S(2)}) collective-permute-start(bf16[128,1152]{1,0:T(8,128)(2,1)S(1)} %collective-permute-done.refs_1_), channel_id=1, source_target_pairs={{0,1},{1,2},{2,3},{3,0},{4,5},{5,6},{6,7},{7,4},{8,9},{9,10},{10,1... | collective-permute-start | bytes 884744 | tf_op jit(solution)/shard_map/ppermute | solution.py:41
  37.0 8.7 %collective-permute-start.13 = (bf16[128,1152]{1,0:T(8,128)(2,1)S(1)}, bf16[128,1152]{1,0:T(8,128)(2,1)S(1)}, u32[]{:S(2)}, u32[]{:S(2)}) collective-permute-start(bf16[128,1152]{1,0:T(8,128)(2,1)S(1)} %collective-permute-done.9.refs_11_), channel_id=1, source_target_pairs={{0,8},{8,0},{16,24},{24,16},{32,40},{40,32},{48,56},{56,48},{64,72... | collective-permute-start | bytes 884744 | tf_op jit(solution)/shard_map/ppermute | solution.py:32
  72.6 75.9 %collective-permute-start.23 = (bf16[128,1152]{1,0:T(8,128)(2,1)}, bf16[128,1152]{1,0:T(8,128)(2,1)S(1)}, u32[]{:S(2)}, u32[]{:S(2)}) collective-permute-start(bf16[128,1152]{1,0:T(8,128)(2,1)} %get-tuple-element.33), channel_id=1, source_target_pairs={{0,8},{8,0},{16,24},{24,16},{32,40},{40,32},{48,56},{56,48},{64,72... | collective-permute-start | bytes 884744 | tf_op jit(solution)/shard_map/ppermute | solution.py:32
  79.2 8.6 %collective-permute-start.30 = (f32[1,1]{1,0:T(1,128)}, f32[1,1]{1,0:T(1,128)}, u32[]{:S(2)}, u32[]{:S(2)}) collective-permute-start(f32[1,1]{1,0:T(1,128)} %bitcast), channel_id=1, source_target_pairs={{0,3},{1,2},{2,1},{3,0},{4,7},{5,6},{6,5},{7,4},{8,11},{9,10},{10,... | collective-permute-start | bytes 20 | tf_op jit(solution)/shard_map/ppermute | solution.py:47
  80.0 8.6 %collective-permute-start.29 = (f32[1,1]{1,0:T(1,128)}, f32[1,1]{1,0:T(1,128)}, u32[]{:S(2)}, u32[]{:S(2)}) collective-permute-start(f32[1,1]{1,0:T(1,128)} %bitcast), channel_id=1, source_target_pairs={{0,2},{1,3},{2,0},{3,1},{4,6},{5,7},{6,4},{7,5},{8,10},{9,11},{10,... | collective-permute-start | bytes 20 | tf_op jit(solution)/shard_map/ppermute | solution.py:47
  83.7 71.5 %collective-permute-start.14 = (bf16[128,1152]{1,0:T(8,128)(2,1)}, bf16[128,1152]{1,0:T(8,128)(2,1)S(1)}, u32[]{:S(2)}, u32[]{:S(2)}) collective-permute-start(bf16[128,1152]{1,0:T(8,128)(2,1)} %copy-done.8), channel_id=1, source_target_pairs={{0,4},{1,5},{2,6},{3,7},{4,0},{5,1},{6,2},{7,3},{8,12},{9,13},{10,... | collective-permute-start | bytes 884744 | tf_op jit(solution)/shard_map/ppermute | solution.py:41
  85.8 71.2 %collective-permute-start.15 = (bf16[128,1152]{1,0:T(8,128)(2,1)}, bf16[128,1152]{1,0:T(8,128)(2,1)S(1)}, u32[]{:S(2)}, u32[]{:S(2)}) collective-permute-start(bf16[128,1152]{1,0:T(8,128)(2,1)} %copy-done.7), channel_id=1, source_target_pairs={{0,3},{1,0},{2,1},{3,2},{4,7},{5,4},{6,5},{7,6},{8,11},{9,8},{10,9... | collective-permute-start | bytes 884744 | tf_op jit(solution)/shard_map/ppermute | solution.py:41
  87.8 75.4 %collective-permute-start.16 = (bf16[128,1152]{1,0:T(8,128)(2,1)}, bf16[128,1152]{1,0:T(8,128)(2,1)S(1)}, u32[]{:S(2)}, u32[]{:S(2)}) collective-permute-start(bf16[128,1152]{1,0:T(8,128)(2,1)} %copy-done.4), channel_id=1, source_target_pairs={{0,1},{1,2},{2,3},{3,0},{4,5},{5,6},{6,7},{7,4},{8,9},{9,10},{10,1... | collective-permute-start | bytes 884744 | tf_op jit(solution)/shard_map/ppermute | solution.py:41
  93.5 6.3 %collective-permute-start.40 = (f32[1,1]{1,0:T(1,128)}, f32[1,1]{1,0:T(1,128)}, u32[]{:S(2)}, u32[]{:S(2)}) collective-permute-start(f32[1,1]{1,0:T(1,128)} %add.122), channel_id=1, source_target_pairs={{0,192},{8,200},{16,208},{24,216},{32,224},{40,232},{48,240},{56,2... | collective-permute-start | bytes 20 | tf_op jit(solution)/shard_map/ppermute | solution.py:47
  99.8 6.6 %collective-permute-start.39 = (f32[1,1]{1,0:T(1,128)}, f32[1,1]{1,0:T(1,128)}, u32[]{:S(2)}, u32[]{:S(2)}) collective-permute-start(f32[1,1]{1,0:T(1,128)} %add.122), channel_id=1, source_target_pairs={{0,160},{8,168},{16,176},{24,184},{32,128},{40,136},{48,144},{56,1... | collective-permute-start | bytes 20 | tf_op jit(solution)/shard_map/ppermute | solution.py:47
  106.3 6.3 %collective-permute-start.38 = (f32[1,1]{1,0:T(1,128)}, f32[1,1]{1,0:T(1,128)}, u32[]{:S(2)}, u32[]{:S(2)}) collective-permute-start(f32[1,1]{1,0:T(1,128)} %add.122), channel_id=1, source_target_pairs={{0,128},{8,136},{16,144},{24,152},{32,160},{40,168},{48,176},{56,1... | collective-permute-start | bytes 20 | tf_op jit(solution)/shard_map/ppermute | solution.py:47
  124.9 11.9 %collective-permute-start.42 = (f32[1,1]{1,0:T(1,128)}, f32[1,1]{1,0:T(1,128)}, u32[]{:S(2)}, u32[]{:S(2)}) collective-permute-start(f32[1,1]{1,0:T(1,128)} %add.129), channel_id=1, source_target_pairs={{0,8},{8,0},{16,24},{24,16},{32,40},{40,32},{48,56},{56,48},{64,72... | collective-permute-start | bytes 20 | tf_op jit(solution)/shard_map/ppermute | solution.py:47
  145.3 6.7 %collective-permute-start.21 = (bf16[128,1152]{1,0:T(8,128)(2,1)}, bf16[128,1152]{1,0:T(8,128)(2,1)S(1)}, u32[]{:S(2)}, u32[]{:S(2)}) collective-permute-start(bf16[128,1152]{1,0:T(8,128)(2,1)} %copy-done.10), channel_id=1, source_target_pairs={{0,232},{8,0},{16,248},{24,16},{32,8},{40,32},{48,24},{56,48},{64,... | collective-permute-start | bytes 884744 | tf_op jit(solution)/shard_map/ppermute | solution.py:32
  151.9 7.4 %collective-permute-start.22 = (bf16[128,1152]{1,0:T(8,128)(2,1)S(1)}, bf16[128,1152]{1,0:T(8,128)(2,1)S(1)}, u32[]{:S(2)}, u32[]{:S(2)}) collective-permute-start(bf16[128,1152]{1,0:T(8,128)(2,1)S(1)} %copy-done.6), channel_id=1, source_target_pairs={{0,8},{8,0},{16,24},{24,16},{32,40},{40,32},{48,56},{56,48},{64,72... | collective-permute-start | bytes 884744 | tf_op jit(solution)/shard_map/ppermute | solution.py:32
  152.0 8.5 %collective-permute-start.24 = (bf16[128,1152]{1,0:T(8,128)(2,1)S(1)}, bf16[128,1152]{1,0:T(8,128)(2,1)S(1)}, u32[]{:S(2)}, u32[]{:S(2)}) collective-permute-start(bf16[128,1152]{1,0:T(8,128)(2,1)S(1)} %fusion.115), channel_id=1, source_target_pairs={{0,224},{8,232},{16,240},{24,248},{32,0},{40,8},{48,16},{56,24},{6... | collective-permute-start | bytes 884744 | tf_op jit(solution)/shard_map/ppermute | solution.py:32
  155.5 11.2 %collective-permute-start.17 = (bf16[128,1152]{1,0:T(8,128)(2,1)S(1)}, bf16[128,1152]{1,0:T(8,128)(2,1)S(1)}, u32[]{:S(2)}, u32[]{:S(2)}) collective-permute-start(bf16[128,1152]{1,0:T(8,128)(2,1)S(1)} %copy-done.3), channel_id=1, source_target_pairs={{0,2},{1,3},{2,0},{3,1},{4,6},{5,7},{6,4},{7,5},{8,10},{9,11},{10,... | collective-permute-start | bytes 884744 | tf_op jit(solution)/shard_map/ppermute | solution.py:41
  157.0 21.8 %collective-permute-start.18 = (bf16[128,1152]{1,0:T(8,128)(2,1)S(1)}, bf16[128,1152]{1,0:T(8,128)(2,1)S(1)}, u32[]{:S(2)}, u32[]{:S(2)}) collective-permute-start(bf16[128,1152]{1,0:T(8,128)(2,1)S(1)} %get-tuple-element.25), channel_id=1, source_target_pairs={{0,7},{1,4},{2,5},{3,6},{4,3},{5,0},{6,1},{7,2},{8,15},{9,12},{10,... | collective-permute-start | bytes 884744 | tf_op jit(solution)/shard_map/ppermute | solution.py:41
  159.3 19.5 %collective-permute-start.19 = (bf16[128,1152]{1,0:T(8,128)(2,1)S(1)}, bf16[128,1152]{1,0:T(8,128)(2,1)S(1)}, u32[]{:S(2)}, u32[]{:S(2)}) collective-permute-start(bf16[128,1152]{1,0:T(8,128)(2,1)S(1)} %get-tuple-element.26), channel_id=1, source_target_pairs={{0,5},{1,6},{2,7},{3,4},{4,1},{5,2},{6,3},{7,0},{8,13},{9,14},{10,... | collective-permute-start | bytes 884744 | tf_op jit(solution)/shard_map/ppermute | solution.py:41
  160.5 26.2 %collective-permute-start.20 = (bf16[128,1152]{1,0:T(8,128)(2,1)S(1)}, bf16[128,1152]{1,0:T(8,128)(2,1)S(1)}, u32[]{:S(2)}, u32[]{:S(2)}) collective-permute-start(bf16[128,1152]{1,0:T(8,128)(2,1)S(1)} %get-tuple-element.27), channel_id=1, source_target_pairs={{0,6},{1,7},{2,4},{3,5},{4,2},{5,3},{6,0},{7,1},{8,14},{9,15},{10,... | collective-permute-start | bytes 884744 | tf_op jit(solution)/shard_map/ppermute | solution.py:41
  163.3 26.3 %collective-permute-start.27 = (bf16[128,1152]{1,0:T(8,128)(2,1)S(1)}, bf16[128,1152]{1,0:T(8,128)(2,1)S(1)}, u32[]{:S(2)}, u32[]{:S(2)}) collective-permute-start(bf16[128,1152]{1,0:T(8,128)(2,1)S(1)} %fusion.116), channel_id=1, source_target_pairs={{0,224},{8,232},{16,240},{24,248},{32,0},{40,8},{48,16},{56,24},{6... | collective-permute-start | bytes 884744 | tf_op jit(solution)/shard_map/ppermute | solution.py:32
  166.8 25.1 %collective-permute-start.25 = (bf16[128,1152]{1,0:T(8,128)(2,1)S(1)}, bf16[128,1152]{1,0:T(8,128)(2,1)S(1)}, u32[]{:S(2)}, u32[]{:S(2)}) collective-permute-start(bf16[128,1152]{1,0:T(8,128)(2,1)S(1)} %fusion.117), channel_id=1, source_target_pairs={{0,240},{8,248},{16,0},{24,8},{32,16},{40,24},{48,32},{56,40},{64,... | collective-permute-start | bytes 884744 | tf_op jit(solution)/shard_map/ppermute | solution.py:32
  (34 other events, 173.6 us)

commit v2 on v0

v2 whole, which is shorter than its diff:
```python
import math

import jax
import jax.numpy as jnp
from jax import lax
from jax.experimental import pallas as pl
from jax.experimental.pallas import tpu as pltpu
from jax.sharding import PartitionSpec as P

STEPS = 8
TILE = 256
VMEM_LIMIT = 60 * 1024 * 1024
CODE_SCALE = 2.0**56
CODE_FLOOR = 2.0**-126
HINT = pl.CostEstimate(flops=1, bytes_accessed=1, transcendentals=0)


def encode(value):
    scaled = value * CODE_SCALE
    return (scaled * jnp.abs(scaled)).astype(jnp.bfloat16)


def decode(code):
    wide = code.astype(jnp.float32)
    return wide * lax.rsqrt(jnp.maximum(jnp.abs(wide), CODE_FLOOR)) * (1.0 / CODE_SCALE)


def shift_blk(value, even, odd, name):
    count = lax.axis_size("blk")
    pairs = [(s, (s + (odd if s % 2 else even)) % count) for s in range(count)]
    with jax.named_scope(name):
        return lax.ppermute(value, "blk", pairs)


def swap_core(value, name):
    return shift_blk(value, 1, -1, name)


def swap_y(value, name):
    with jax.named_scope(name):
        return lax.ppermute(value, "group", [(s, (s + 4) % 8) for s in range(8)])


def ring_x(value, steps, name):
    pairs = []
    for b in range(lax.axis_size("blk")):
        for g in range(8):
            x = g % 4 + (-steps if b % 2 else steps)
            pairs.append((b * 8 + g, b * 8 + g // 4 * 4 + x % 4))
    with jax.named_scope(name):
        return lax.ppermute(value, ("blk", "group"), pairs)


def sum_over(value, axis):
    copies = jnp.broadcast_to(value[None], (lax.axis_size(axis), *value.shape))
    with jax.named_scope(f"loss_{axis}"):
        return jnp.sum(lax.all_to_all(copies, axis, 0, 0), axis=0)


def after(value, *others):
    return lax.optimization_barrier((value, *others))[0]


def any_specs(count):
    return [pl.BlockSpec(memory_space=pl.ANY)] * count


def params():
    return pltpu.CompilerParams(vmem_limit_bytes=VMEM_LIMIT)


def fetch_all(pairs, sems):
    copies = [pltpu.make_async_copy(source, target, sems.at[i]) for i, (source, target) in enumerate(pairs)]
    for c in copies:
        c.start()
    return copies


def share_slots(refs, place):
    rows = refs[0].shape[0]
    return [(r, place.at[pl.ds(i * rows, rows), :]) for i, r in enumerate(refs)]


def pairs_kernel(scale, bias_ref, *refs):
    image_refs, text_refs = refs[:8], refs[8:16]
    coef_ref, loss_ref, outs = refs[16], refs[17], refs[18:23]
    images, texts, coef, acc, stage, loss_acc, in_sems, out_sems = refs[23:]
    rows, width = image_refs[0].shape
    total = 8 * rows
    factor = scale[0] * (1.0 / math.sqrt(width))
    weight = factor * (1.0 / math.sqrt(STEPS * total))
    bias = bias_ref[0]
    slots = share_slots(text_refs, texts) + share_slots(image_refs, images)
    copies = [pltpu.make_async_copy(source, target, in_sems.at[i]) for i, (source, target) in enumerate(slots)]
    for i in (0, 1, 10, 11, 2, 3, 4, 5, 6, 7, 12, 13, 14, 15, 8, 9):
        copies[i].start()
    waited = set()
    sends = []
    loss_acc[...] = jnp.zeros_like(loss_acc)
    for it in (1, 2, 3, 0):
        place = pl.ds(it * TILE, TILE)
        for jt in range(total // TILE):
            for i in (8 + 2 * it, 9 + 2 * it, 2 * jt, 2 * jt + 1):
                if i not in waited:
                    copies[i].wait()
                    waited.add(i)
            left = images[place, :]
            right = texts[jt * TILE : (jt + 1) * TILE, :]
            logits = lax.dot_general(left, right, (((1,), (1,)), ((), ())), preferred_element_type=jnp.float32)
            logits = logits * factor + bias
            mixed = it == 0 and jt == 0
            if mixed:
                row = lax.broadcasted_iota(jnp.int32, (TILE, TILE), 0)
                col = lax.broadcasted_iota(jnp.int32, (TILE, TILE), 1)
                positive = jnp.logical_and(row == col, col < rows)
                logits = jnp.where(positive, -logits, logits)
            small = jnp.exp(-jnp.abs(logits))
            log1p = jnp.log(1.0 + small)
            part = jnp.exp(jnp.minimum(logits, 0.0) - log1p) * weight
            if mixed:
                part = jnp.where(positive, -part, part)
            coef[place, jt * TILE : (jt + 1) * TILE] = part.astype(jnp.bfloat16)
            exact = jnp.where(small < 2.0**-9, small * (1.0 - 0.5 * small), log1p)
            terms = jnp.maximum(logits, 0.0) + exact
            loss_acc[...] += jnp.sum(terms.reshape(TILE // 8, 8, TILE), axis=0)
        sends.append(pltpu.make_async_copy(coef.at[place, :], coef_ref.at[place, :], out_sems.at[5 + it]))
        sends[-1].start()
        product = jnp.dot(coef[place, :], texts[...], preferred_element_type=jnp.float32)
        if it == 0:
            acc[...] = product
            for i in range(2):
                sends.append(pltpu.make_async_copy(acc.at[pl.ds(i * rows, rows), :], outs[i], out_sems.at[i]))
                sends[-1].start()
        else:
            stage[place, :] = encode(product)
            sends.append(pltpu.make_async_copy(stage.at[place, :], outs[1 + it], out_sems.at[1 + it]))
            sends[-1].start()
    loss_ref[...] = loss_acc[:, : TILE // 2] + loss_acc[:, TILE // 2 :]
    for s in sends:
        s.wait()


def pairs_part(logit_scale, logit_bias, image_shares, text_shares):
    rows, width = image_shares[0].shape
    total = 8 * rows
    wide = jax.ShapeDtypeStruct((rows, width), jnp.float32)
    return pl.pallas_call(
        pairs_kernel,
        out_shape=[jax.ShapeDtypeStruct((total, total), jnp.bfloat16), jax.ShapeDtypeStruct((8, TILE // 2), jnp.float32)]
        + [wide] * 2
        + [jax.ShapeDtypeStruct((TILE, width), jnp.bfloat16)] * 3,
        in_specs=[pl.BlockSpec(memory_space=pltpu.SMEM)] * 2 + any_specs(16),
        out_specs=any_specs(1) + [pl.BlockSpec(memory_space=pltpu.VMEM)] + any_specs(5),
        scratch_shapes=[
            pltpu.VMEM((total, width), jnp.bfloat16),
            pltpu.VMEM((total, width), jnp.bfloat16),
            pltpu.VMEM((total, total), jnp.bfloat16),
            pltpu.VMEM((TILE, width), jnp.float32),
            pltpu.VMEM((total, width), jnp.bfloat16),
            pltpu.VMEM((8, TILE), jnp.float32),
            pltpu.SemaphoreType.DMA((16,)),
            pltpu.SemaphoreType.DMA((9,)),
        ],
        compiler_params=params(),
        cost_estimate=HINT,
        name="pairs_part",
    )(logit_scale, logit_bias, *image_shares, *text_shares)


def texts_kernel(coef_ref, *refs):
    image_refs, outs = refs[:8], refs[8:16]
    images, coef, acc, stage, in_sems, out_sems = refs[16:]
    rows = image_refs[0].shape[0]
    tiles = 8 * rows // TILE
    order = (2, 3, 1, 0)
    copies = [
        pltpu.make_async_copy(source, target, in_sems.at[i])
        for i, (source, target) in enumerate(
            [(coef_ref.at[:, pl.ds(i * TILE, TILE)], coef.at[:, pl.ds(i * TILE, TILE)]) for i in range(tiles)]
            + share_slots(image_refs, images)
        )
    ]
    for i in (order[0], *range(tiles, tiles + 8), *order[1:]):
        copies[i].start()
    for c in copies[tiles:]:
        c.wait()
    sends = []
    for jt in order:
        copies[jt].wait()
        place = slice(jt * TILE, (jt + 1) * TILE)
        acc[place, :] = lax.dot_general(
            coef[:, place], images[...], (((0,), (0,)), ((), ())), preferred_element_type=jnp.float32
        )
        for i in (2 * jt, 2 * jt + 1):
            part = pl.ds(i * rows, rows)
            if i < 7:
                sends.append(pltpu.make_async_copy(acc.at[part, :], outs[i], out_sems.at[i]))
            else:
                stage[...] = encode(acc[part, :])
                sends.append(pltpu.make_async_copy(stage, outs[i], out_sems.at[i]))
            sends[-1].start()
    for s in sends:
        s.wait()


def texts_part(coef, image_shares):
    rows, width = image_shares[0].shape
    total = 8 * rows
    wide = jax.ShapeDtypeStruct((rows, width), jnp.float32)
    return pl.pallas_call(
        texts_kernel,
        out_shape=[wide] * 7 + [jax.ShapeDtypeStruct((rows, width), jnp.bfloat16)],
        in_specs=any_specs(9),
        out_specs=any_specs(8),
        scratch_shapes=[
            pltpu.VMEM((total, width), jnp.bfloat16),
            pltpu.VMEM((total, total), jnp.bfloat16),
            pltpu.VMEM((total, width), jnp.float32),
            pltpu.VMEM((rows, width), jnp.bfloat16),
            pltpu.SemaphoreType.DMA((12,)),
            pltpu.SemaphoreType.DMA((8,)),
        ],
        compiler_params=params(),
        cost_estimate=HINT,
        name="texts_part",
    )(coef, *image_shares)


def body(images, texts, logit_scale, logit_bias):
    rows, width = images.shape
    core = lax.axis_index("blk") % 2
    across = swap_y(images, "across")
    behind2 = shift_blk(texts, 4, 4, "behind2")
    behind1 = shift_blk(texts, 2, 2, "behind1")
    near = [images]
    far = [across]
    for name, group in (("near", near), ("far", far)):
        first = ring_x(group[0], 1, f"{name}1")
        group += [first, ring_x(first, 1, f"{name}2"), ring_x(group[0], 3, f"{name}3")]
    extra = shift_blk(jnp.where(core == 0, texts, behind2), 1, 3, "extra")
    behind3 = shift_blk(behind2, 2, 2, "behind3")
    sib1, sib2, sib3 = [swap_core(b, "sibling") for b in (behind1, behind2, behind3)]
    image_shares = [s for pair in zip(near, far) for s in pair]
    text_shares = [texts, behind1, behind2, behind3, sib1, sib2, sib3, extra]

    coef, loss, gi_own, gi_across, *gi_codes = pairs_part(logit_scale, logit_bias, image_shares, text_shares)
    back = [ring_x(code, -(i + 1), f"back_x{i + 1}") for i, code in enumerate(gi_codes)]
    gt_own, gt1, gt2, gt3, gt_sib1, gt_sib2, gt_sib3, gt_extra = texts_part(coef, image_shares)

    gt1 = gt1 + swap_core(gt_sib1, "back_sib1")
    gt2 = gt2 + swap_core(gt_sib2, "back_sib2")
    gt3 = gt3 + swap_core(gt_sib3, "back_sib3")
    code13 = jnp.concatenate([encode(gt1), encode(gt3)])
    from_extra = decode(shift_blk(gt_extra, -3, -1, "back_extra"))
    gt2 = gt2 + jnp.where(core == 1, from_extra, 0.0)
    code13, gt2, from_extra = lax.optimization_barrier((code13, gt2, from_extra))
    from13 = shift_blk(code13, -2, -2, "back13")
    code2 = encode(gt2 + decode(from13[rows:]))
    from2 = shift_blk(code2, -4, -4, "back2")

    for code in back:
        gi_own = gi_own + decode(code[:rows])
        gi_across = gi_across + decode(code[rows:])
    code_across = encode(gi_across)
    last = swap_y(code_across, "back_across")
    grad_images = gi_own + decode(last)

    loss = sum_over(after(loss, code13), "blk")
    loss = jnp.sum(sum_over(after(loss, code2, code_across), "group"))
    pairs = rows * lax.axis_size("group") * lax.axis_size("blk")
    loss = loss.reshape(1) / pairs

    grad_texts = gt_own + jnp.where(core == 0, from_extra, 0.0) + decode(from13[:rows]) + decode(from2)
    return (grad_images, grad_texts, loss)


def solution(mesh):
    return jax.shard_map(
        body,
        mesh=mesh,
        in_specs=(P(("blk", "group"), None), P(("blk", "group"), None), P(), P()),
        out_specs=(P(("blk", "group"), None), P(("blk", "group"), None), P()),
        check_vma=False,
    )
```

time: 324 us -> 119 us (0.37)
  waiting for transfers between devices: 125 us -> 37.3 us
  blocking collectives: 76.6 us -> 0 us
  matrix products: 33.3 us -> 0 us
  Pallas kernels: 0 us -> 19.2 us
  starting transfers between devices: 60.7 us -> 41.7 us
  between operations: 22.5 us -> 4.04 us
  other arithmetic: 0.37 us -> 12.3 us
    ppermute x15 -> x24, waiting for transfers between devices: 125 us -> 34.5 us  [the longest x13 23.5 us: shift_blk(): return lax.ppermute(value, 'blk', pairs)]
    psum x1 -> x0, blocking collectives: 76.6 us -> none  [body(): loss = (lax.psum(total, ('blk', 'group')) / pairs).reshape(1)]
    dot_general x24 -> x0, matrix products: 33.3 us -> none  [the longest x8 17.1 us: body(): lax.dot_general(gathered, current, (((1,), (1,)), ((), ())), preferred_el...]
    ppermute x15 -> x24, starting transfers between devices: 60.6 us -> 30.4 us  [the longest x13 16.3 us: shift_blk(): return lax.ppermute(value, 'blk', pairs)]
    pallas_call x0 -> x2, Pallas kernels: none -> 19.2 us  [the longest x1 12.7 us: pairs_part(): pl.pallas_call(pairs_kernel, out_shape=[jax.ShapeDtypeStruct((total, tota...]
    all_to_all x0 -> x2, starting transfers between devices: none -> 11.3 us  [sum_over(): return jnp.sum(lax.all_to_all(copies, axis, 0, 0), axis=0)]
    convert_element_type x0 -> x4, other arithmetic: none -> 4.32 us  [encode(): return (scaled * jnp.abs(scaled)).astype(jnp.bfloat16)]
    add x7 -> x2, other arithmetic: 0.37 us -> 4.56 us  [the longest x1 2.38 us: body(): grad_images = gi_own + decode(last)]
  transfers between devices with their start and end apart: 17 -> 26, of which waited for: 13 -> 9; matrix products, arithmetic and copies ran while one was open for 8% -> 10% of each run, Pallas kernels for 0% -> 0%
where the time goes in v2:
time: 119 us; the launch traced here: 117 us
  starting transfers between devices  41.7 us (35%)
  waiting for transfers between devices  37.3 us (31%)
  Pallas kernels  19.2 us (16%)
  other arithmetic  12.3 us (10%)
  between operations  4.04 us (3%)
  local copies, waits for them, and re-layouts  2.87 us (2%)
    ppermute x13, waiting for transfers between devices, shift_blk(): return lax.ppermute(value, 'blk', pairs)  23.5 us
    ppermute x13, starting transfers between devices, shift_blk(): return lax.ppermute(value, 'blk', pairs)  16.3 us
    ppermute x9, starting transfers between devices, ring_x(): return lax.ppermute(value, ('blk', 'group'), pairs)  13.2 us
    pallas_call x1, Pallas kernels, pairs_part(): pl.pallas_call(pairs_kernel, out_shape=[jax.ShapeDtypeStruct((total, tota...  12.7 us
    all_to_all x2, starting transfers between devices, sum_over(): return jnp.sum(lax.all_to_all(copies, axis, 0, 0), axis=0)  11.3 us
    ppermute x9, waiting for transfers between devices, ring_x(): return lax.ppermute(value, ('blk', 'group'), pairs)  11 us
    pallas_call x1, Pallas kernels, texts_part(): pl.pallas_call(texts_kernel, out_shape=[wide] * 7 + [jax.ShapeDtypeStruct...  6.49 us
    convert_element_type x4, other arithmetic, encode(): return (scaled * jnp.abs(scaled)).astype(jnp.bfloat16)  4.32 us
  transfers between devices with their start and end apart: 26, of which 9 were waited for; matrix products, arithmetic and copies ran while one was open for 10% of the time, Pallas kernels for 0%

profile of v2, /device:TPU:1, one launch (start us, length us, event | category | flops | bytes accessed | tf_op | source)
XLA Modules:
  0.0 117.4 jit_solution(14098832252690609077)
XLA Ops:
  0.6 2.5 %collective-permute-start.8 = (bf16[128,1152]{1,0:T(8,128)(2,1)}, bf16[128,1152]{1,0:T(8,128)(2,1)S(1)}, u32[]{:S(2)}, u32[]{:S(2)}) collective-permute-start(bf16[128,1152]{1,0:T(8,128)(2,1)} %refs_8_.1), channel_id=1, source_target_pairs={{0,32},{8,40},{16,48},{24,56},{32,64},{40,72},{48,80},{56,88},{64,... | collective-permute-start | bytes 884744 | tf_op jit(solution)/shard_map/behind2/ppermute | solution.py:32
  3.2 2.9 %collective-permute-start.7 = (bf16[128,1152]{1,0:T(8,128)(2,1)}, bf16[128,1152]{1,0:T(8,128)(2,1)S(1)}, u32[]{:S(2)}, u32[]{:S(2)}) collective-permute-start(bf16[128,1152]{1,0:T(8,128)(2,1)} %refs_8_.1), channel_id=1, source_target_pairs={{0,16},{8,24},{16,32},{24,40},{32,48},{40,56},{48,64},{56,72},{64,... | collective-permute-start | bytes 884744 | tf_op jit(solution)/shard_map/behind1/ppermute | solution.py:32
  6.1 1.2 %collective-permute-start.5 = (bf16[128,1152]{1,0:T(8,128)(2,1)}, bf16[128,1152]{1,0:T(8,128)(2,1)S(1)}, u32[]{:S(2)}, u32[]{:S(2)}) collective-permute-start(bf16[128,1152]{1,0:T(8,128)(2,1)} %refs_0_.3), channel_id=1, source_target_pairs={{0,3},{1,0},{2,1},{3,2},{4,7},{5,4},{6,5},{7,6},{8,9},{9,10},{10,1... | collective-permute-start | bytes 884744 | tf_op jit(solution)/shard_map/near3/ppermute | solution.py:51
  7.3 1.5 %collective-permute-start.1 = (bf16[128,1152]{1,0:T(8,128)(2,1)}, bf16[128,1152]{1,0:T(8,128)(2,1)S(1)}, u32[]{:S(2)}, u32[]{:S(2)}) collective-permute-start(bf16[128,1152]{1,0:T(8,128)(2,1)} %refs_0_.3), channel_id=1, source_target_pairs={{0,1},{1,2},{2,3},{3,0},{4,5},{5,6},{6,7},{7,4},{8,11},{9,8},{10,9... | collective-permute-start | bytes 884744 | tf_op jit(solution)/shard_map/near1/ppermute | solution.py:51
  9.2 4.9 %collective-permute-done.8.refs_10_ = bf16[128,1152]{1,0:T(8,128)(2,1)S(1)} collective-permute-done((bf16[128,1152]{1,0:T(8,128)(2,1)}, bf16[128,1152]{1,0:T(8,128)(2,1)S(1)}, u32[]{:S(2)}, u32[]{:S(2)}) %collective-permute-start.8) | collective-permute-done | bytes 294944 | tf_op jit(solution)/shard_map/behind2/ppermute | solution.py:32
  14.1 8.9 %collective-permute-done.7.refs_9_ = bf16[128,1152]{1,0:T(8,128)(2,1)S(1)} collective-permute-done((bf16[128,1152]{1,0:T(8,128)(2,1)}, bf16[128,1152]{1,0:T(8,128)(2,1)S(1)}, u32[]{:S(2)}, u32[]{:S(2)}) %collective-permute-start.7) | collective-permute-done | bytes 294944 | tf_op jit(solution)/shard_map/behind1/ppermute | solution.py:32
  23.1 1.4 %collective-permute-start.11 = (bf16[128,1152]{1,0:T(8,128)(2,1)S(1)}, bf16[128,1152]{1,0:T(8,128)(2,1)S(1)}, u32[]{:S(2)}, u32[]{:S(2)}) collective-permute-start(bf16[128,1152]{1,0:T(8,128)(2,1)S(1)} %collective-permute-done.8.refs_10_), channel_id=1, source_target_pairs={{0,8},{8,0},{16,24},{24,16},{32,40},{40,32},{48,56},{56,48},{64,72... | collective-permute-start | bytes 884744 | tf_op jit(solution)/shard_map/sibling/ppermute | solution.py:32
  24.5 2.6 %collective-permute-start.2 = (bf16[128,1152]{1,0:T(8,128)(2,1)S(1)}, bf16[128,1152]{1,0:T(8,128)(2,1)S(1)}, u32[]{:S(2)}, u32[]{:S(2)}) collective-permute-start(bf16[128,1152]{1,0:T(8,128)(2,1)S(1)} %collective-permute-done.refs_1_), channel_id=1, source_target_pairs={{0,1},{1,2},{2,3},{3,0},{4,5},{5,6},{6,7},{7,4},{8,11},{9,8},{10,9... | collective-permute-start | bytes 884744 | tf_op jit(solution)/shard_map/far1/ppermute | solution.py:51
  27.9 1.9 %collective-permute-start.3 = (bf16[128,1152]{1,0:T(8,128)(2,1)S(1)}, bf16[128,1152]{1,0:T(8,128)(2,1)S(1)}, u32[]{:S(2)}, u32[]{:S(2)}) collective-permute-start(bf16[128,1152]{1,0:T(8,128)(2,1)S(1)} %collective-permute-done.1.refs_2_), channel_id=1, source_target_pairs={{0,1},{1,2},{2,3},{3,0},{4,5},{5,6},{6,7},{7,4},{8,11},{9,8},{10,9... | collective-permute-start | bytes 884744 | tf_op jit(solution)/shard_map/near2/ppermute | solution.py:51
  29.8 6.8 %collective-permute-done.9.refs_11_ = bf16[128,1152]{1,0:T(8,128)(2,1)S(1)} collective-permute-done((bf16[128,1152]{1,0:T(8,128)(2,1)S(1)}, bf16[128,1152]{1,0:T(8,128)(2,1)S(1)}, u32[]{:S(2)}, u32[]{:S(2)}) %collective-permute-start.9) | collective-permute-done | bytes 294944 | tf_op jit(solution)/shard_map/behind3/ppermute | solution.py:32
  37.5 2.5 %collective-permute-start.4 = (bf16[128,1152]{1,0:T(8,128)(2,1)S(1)}, bf16[128,1152]{1,0:T(8,128)(2,1)S(1)}, u32[]{:S(2)}, u32[]{:S(2)}) collective-permute-start(bf16[128,1152]{1,0:T(8,128)(2,1)S(1)} %collective-permute-done.2.refs_3_), channel_id=1, source_target_pairs={{0,1},{1,2},{2,3},{3,0},{4,5},{5,6},{6,7},{7,4},{8,11},{9,8},{10,9... | collective-permute-start | bytes 884744 | tf_op jit(solution)/shard_map/far2/ppermute | solution.py:51
  42.1 1.5 %collective-permute-done.4.refs_5_ = bf16[128,1152]{1,0:T(8,128)(2,1)S(1)} collective-permute-done((bf16[128,1152]{1,0:T(8,128)(2,1)S(1)}, bf16[128,1152]{1,0:T(8,128)(2,1)S(1)}, u32[]{:S(2)}, u32[]{:S(2)}) %collective-permute-start.4) | collective-permute-done | bytes 294944 | tf_op jit(solution)/shard_map/far2/ppermute | solution.py:51
  44.5 12.7 %pairs_part.1 = (bf16[1024,1024]{1,0:T(8,128)(2,1)}, f32[8,128]{1,0:T(8,128)}, f32[128,1152]{1,0:T(8,128)}, f32[128,1152]{1,0:T(8,128)}, bf16[256,1152]{1,0:T(8,...) custom-call(f32[1]{0:T(128)S(6)} %copy.7.scale, f32[1]{0:T(128)S(6)} %copy.8.bias_ref, ...), custom_call_target="tpu_custom_call" | custom-call | flops 1 | bytes 1 | tf_op jit(solution)/shard_map/pairs_part/pallas_call | solution.py:147
  57.2 6.5 %texts_part.1 = (f32[128,1152]{1,0:T(8,128)}, f32[128,1152]{1,0:T(8,128)}, f32[128,1152]{1,0:T(8,128)}, f32[128,1152]{1,0:T(8,128)}, f32[128,1152]{1,0:T(8,128)}...) custom-call(bf16[1024,1024]{1,0:T(8,128)(2,1)} %get-tuple-element.28.coef_ref, ...), custom_call_target="tpu_custom_call" | custom-call | flops 1 | bytes 1 | tf_op jit(solution)/shard_map/texts_part/pallas_call | solution.py:210
  63.7 2.1 %collective-permute-start.18 = (f32[128,1152]{1,0:T(8,128)}, f32[128,1152]{1,0:T(8,128)S(1)}, u32[]{:S(2)}, u32[]{:S(2)}) collective-permute-start(f32[128,1152]{1,0:T(8,128)} %get-tuple-element.31), channel_id=1, source_target_pairs={{0,8},{8,0},{16,24},{24,16},{32,40},{40,32},{48,56},{56,48},{64,72... | collective-permute-start | bytes 1769480 | tf_op jit(solution)/shard_map/back_sib1/ppermute | solution.py:32
  66.0 2.7 %collective-permute-start.15 = (bf16[256,1152]{1,0:T(8,128)(2,1)}, bf16[256,1152]{1,0:T(8,128)(2,1)S(1)}, u32[]{:S(2)}, u32[]{:S(2)}) collective-permute-start(bf16[256,1152]{1,0:T(8,128)(2,1)} %get-tuple-element.25), channel_id=1, source_target_pairs={{0,2},{1,3},{2,0},{3,1},{4,6},{5,7},{6,4},{7,5},{8,10},{9,11},{10,... | collective-permute-start | bytes 1769480 | tf_op jit(solution)/shard_map/back_x2/ppermute | solution.py:51
  69.6 1.2 fusion.45
  70.8 1.6 %collective-permute-start.20 = (f32[128,1152]{1,0:T(8,128)S(1)}, f32[128,1152]{1,0:T(8,128)S(1)}, u32[]{:S(2)}, u32[]{:S(2)}) collective-permute-start(f32[128,1152]{1,0:T(8,128)S(1)} %copy-done.20), channel_id=1, source_target_pairs={{0,8},{8,0},{16,24},{24,16},{32,40},{40,32},{48,56},{56,48},{64,72... | collective-permute-start | bytes 1769480 | tf_op jit(solution)/shard_map/back_sib2/ppermute | solution.py:32
  73.4 2.9 %collective-permute-done.21 = bf16[128,1152]{1,0:T(8,128)(2,1)S(1)} collective-permute-done((bf16[128,1152]{1,0:T(8,128)(2,1)}, bf16[128,1152]{1,0:T(8,128)(2,1)S(1)}, u32[]{:S(2)}, u32[]{:S(2)}) %collective-permute-start.21) | collective-permute-done | bytes 294944 | tf_op jit(solution)/shard_map/back_extra/ppermute | solution.py:32
  76.5 2.8 %collective-permute-start.22 = (bf16[256,1152]{1,0:T(8,128)(2,1)}, bf16[256,1152]{1,0:T(8,128)(2,1)}, u32[]{:S(2)}, u32[]{:S(2)}) collective-permute-start(bf16[256,1152]{1,0:T(8,128)(2,1)} %pad_maximum_fusion), channel_id=1, source_target_pairs={{0,240},{8,248},{16,0},{24,8},{32,16},{40,24},{48,32},{56,40},{64,... | collective-permute-start | bytes 1769480 | tf_op jit(solution)/shard_map/back13/ppermute | solution.py:32
  79.9 5.8 %all-to-all-start = ((f32[32,8,128]{2,1,0:T(8,128)}), f32[32,8,128]{2,1,0:T(8,128)}, u32[]{:S(2)}, u32[]{:S(2)}) async-start(f32[32,8,128]{2,1,0:T(8,128)} %broadcast_in_dim.18), calls=%async_computation | async-start | bytes 262144 | tf_op jit(solution)/shard_map/loss_blk/all_to_all | solution.py:57
  85.7 6.4 %collective-permute-done.14 = bf16[256,1152]{1,0:T(8,128)(2,1)S(1)} collective-permute-done((bf16[256,1152]{1,0:T(8,128)(2,1)}, bf16[256,1152]{1,0:T(8,128)(2,1)S(1)}, u32[]{:S(2)}, u32[]{:S(2)}) %collective-permute-start.14) | collective-permute-done | bytes 589856 | tf_op jit(solution)/shard_map/back_x1/ppermute | solution.py:51
  92.7 2.4 %collective-permute-done.16 = bf16[256,1152]{1,0:T(8,128)(2,1)S(1)} collective-permute-done((bf16[256,1152]{1,0:T(8,128)(2,1)}, bf16[256,1152]{1,0:T(8,128)(2,1)S(1)}, u32[]{:S(2)}, u32[]{:S(2)}) %collective-permute-start.16) | collective-permute-done | bytes 589856 | tf_op jit(solution)/shard_map/back_x3/ppermute | solution.py:51
  95.2 1.2 %fusion.48 = bf16[128,1152]{1,0:T(8,128)(2,1)} fusion(f32[128,1152]{1,0:T(8,128)S(1)} %copy-done.9, bf16[256,1152]{1,0:T(8,128)(2,1)S(1)} %collective-permute-done.16, bf16[256,1152]{1,0:T(8,128)(2,1)S(1)} %collective-permute-done.15, bf16[256,1152]{1,0:T(8,128)(2,1)S(1)} %collective-permute-done.14), kind=kLoop, calls=%fused_computation.76 | loop fusion | flops 3244032 | bytes 1769472 | tf_op jit(solution)/shard_map/convert_element_type | solution.py:20
  96.8 0.9 reduce_sum.16
  97.7 1.9 %fusion.47 = bf16[128,1152]{1,0:T(8,128)(2,1)} fusion(f32[128,1152]{1,0:T(8,128)S(1)} %get-tuple-element.39, bf16[256,1152]{1,0:T(8,128)(2,1)} %collective-permute-done.22), kind=kLoop, calls=%fused_computation.73 | loop fusion | flops 1474560 | bytes 1179648 | tf_op jit(solution)/shard_map/convert_element_type | solution.py:20
  99.6 1.1 collective-permute-start.23
  101.3 5.5 %all-to-all-start.1 = ((f32[8,8,128]{2,1,0:T(8,128)}), f32[8,8,128]{2,1,0:T(8,128)}, u32[]{:S(2)}, u32[]{:S(2)}) async-start(f32[8,8,128]{2,1,0:T(8,128)} %broadcast_in_dim.19), calls=%async_computation.1 | async-start | bytes 65536 | tf_op jit(solution)/shard_map/loss_group/all_to_all | solution.py:57
  106.9 2.4 %fusion.6 = f32[128,1152]{1,0:T(8,128)} fusion(f32[128,1152]{1,0:T(8,128)S(1)} %copy-done.10, bf16[128,1152]{1,0:T(8,128)(2,1)} %collective-permute-done.17, bf16[256,1152]{1,0:T(8,128)(2,1)S(1)} %collective-permute-done.16, bf16[256,1152]{1,0:T(8,128)(2,1)S(1)} %collective-permute-done.15, bf16[256,1152]{1,0:T(8,128)(2,1)S(1)} %collective-permute-done.14), kind=kLoop, calls=%fused_computation.32 | loop fusion | flops 3538944 | bytes 2359296 | tf_op jit(solution)/shard_map/add | solution.py:266
  109.2 2.8 %all-to-all-done.1 = f32[8,8,128]{2,1,0:T(8,128)} async-done(((f32[8,8,128]{2,1,0:T(8,128)}), f32[8,8,128]{2,1,0:T(8,128)}, u32[]{:S(2)}, u32[]{:S(2)}) %all-to-all-start.1) | async-done | bytes 32800 | tf_op jit(solution)/shard_map/loss_group/all_to_all | solution.py:57
  112.0 1.4 %reduce_sum.20 = f32[]{:T(128)} reduce(f32[8,8,128]{2,1,0:T(8,128)} %all-to-all-done.1, f32[]{:T(128)} %constant.31.clone.1), dimensions={0,1,2}, to_apply=%region_1.2 | reduce | flops 8191 | bytes 32776 | tf_op jit(solution)/shard_map/reduce_sum | solution.py:269
  114.1 2.2 %fusion.36 = f32[128,1152]{1,0:T(8,128)} fusion(bf16[128,1152]{1,0:T(8,128)(2,1)} %collective-permute-done.23, f32[128,1152]{1,0:T(8,128)S(1)} %copy-done.8, f32[128,1152]{1,0:T(8,128)S(1)} %get-tuple-element.37, bf16[256,1152]{1,0:T(8,128)(2,1)} %collective-permute-done.22, pred[]{:T(512)S(6)} %eq.9), kind=kLoop, calls=%fused_computation.62 | loop fusion | flops 2064384 | bytes 2359297 | tf_op jit(solution)/shard_map/add | solution.py:273
  (77 shorter events, 8.4 us)
Async XLA Ops:
  0.6 13.4 %collective-permute-start.8 = (bf16[128,1152]{1,0:T(8,128)(2,1)}, bf16[128,1152]{1,0:T(8,128)(2,1)S(1)}, u32[]{:S(2)}, u32[]{:S(2)}) collective-permute-start(bf16[128,1152]{1,0:T(8,128)(2,1)} %refs_8_.1), channel_id=1, source_target_pairs={{0,32},{8,40},{16,48},{24,56},{32,64},{40,72},{48,80},{56,88},{64,... | collective-permute-start | bytes 884744 | tf_op jit(solution)/shard_map/behind2/ppermute | solution.py:32
  3.2 19.9 %collective-permute-start.7 = (bf16[128,1152]{1,0:T(8,128)(2,1)}, bf16[128,1152]{1,0:T(8,128)(2,1)S(1)}, u32[]{:S(2)}, u32[]{:S(2)}) collective-permute-start(bf16[128,1152]{1,0:T(8,128)(2,1)} %refs_8_.1), channel_id=1, source_target_pairs={{0,16},{8,24},{16,32},{24,40},{32,48},{40,56},{48,64},{56,72},{64,... | collective-permute-start | bytes 884744 | tf_op jit(solution)/shard_map/behind1/ppermute | solution.py:32
  6.1 18.3 %collective-permute-start.5 = (bf16[128,1152]{1,0:T(8,128)(2,1)}, bf16[128,1152]{1,0:T(8,128)(2,1)S(1)}, u32[]{:S(2)}, u32[]{:S(2)}) collective-permute-start(bf16[128,1152]{1,0:T(8,128)(2,1)} %refs_0_.3), channel_id=1, source_target_pairs={{0,3},{1,0},{2,1},{3,2},{4,7},{5,4},{6,5},{7,6},{8,9},{9,10},{10,1... | collective-permute-start | bytes 884744 | tf_op jit(solution)/shard_map/near3/ppermute | solution.py:51
  7.3 19.7 %collective-permute-start.1 = (bf16[128,1152]{1,0:T(8,128)(2,1)}, bf16[128,1152]{1,0:T(8,128)(2,1)S(1)}, u32[]{:S(2)}, u32[]{:S(2)}) collective-permute-start(bf16[128,1152]{1,0:T(8,128)(2,1)} %refs_0_.3), channel_id=1, source_target_pairs={{0,1},{1,2},{2,3},{3,0},{4,5},{5,6},{6,7},{7,4},{8,11},{9,8},{10,9... | collective-permute-start | bytes 884744 | tf_op jit(solution)/shard_map/near1/ppermute | solution.py:51
  8.8 15.7 %collective-permute-start = (bf16[128,1152]{1,0:T(8,128)(2,1)}, bf16[128,1152]{1,0:T(8,128)(2,1)S(1)}, u32[]{:S(2)}, u32[]{:S(2)}) collective-permute-start(bf16[128,1152]{1,0:T(8,128)(2,1)} %refs_0_.3), channel_id=1, source_target_pairs={{0,4},{1,5},{2,6},{3,7},{4,0},{5,1},{6,2},{7,3},{8,12},{9,13},{10,... | collective-permute-start | bytes 884744 | tf_op jit(solution)/shard_map/across/ppermute | solution.py:41
  14.1 29.6 %copy-start.7 = (bf16[128,1152]{1,0:T(8,128)(2,1)}, bf16[128,1152]{1,0:T(8,128)(2,1)S(1)}, u32[]{:S(2)}) copy-start(bf16[128,1152]{1,0:T(8,128)(2,1)S(1)} %collective-permute-done.8.refs_10_) | copy-start | bytes 884740
  14.1 12.9 %collective-permute-start.13 = (bf16[128,1152]{1,0:T(8,128)(2,1)S(1)}, bf16[128,1152]{1,0:T(8,128)(2,1)S(1)}, u32[]{:S(2)}, u32[]{:S(2)}) collective-permute-start(bf16[128,1152]{1,0:T(8,128)(2,1)S(1)} %broadcast_select_fusion), channel_id=1, source_target_pairs={{0,8},{8,32},{16,24},{24,48},{32,40},{40,64},{48,56},{56,80},{64,7... | collective-permute-start | bytes 884744 | tf_op jit(solution)/shard_map/extra/ppermute | solution.py:32
  23.1 20.6 %copy-start.13 = (bf16[128,1152]{1,0:T(8,128)(2,1)}, bf16[128,1152]{1,0:T(8,128)(2,1)S(1)}, u32[]{:S(2)}) copy-start(bf16[128,1152]{1,0:T(8,128)(2,1)S(1)} %collective-permute-done.7.refs_9_) | copy-start | bytes 884740
  23.1 4.8 %collective-permute-start.11 = (bf16[128,1152]{1,0:T(8,128)(2,1)S(1)}, bf16[128,1152]{1,0:T(8,128)(2,1)S(1)}, u32[]{:S(2)}, u32[]{:S(2)}) collective-permute-start(bf16[128,1152]{1,0:T(8,128)(2,1)S(1)} %collective-permute-done.8.refs_10_), channel_id=1, source_target_pairs={{0,8},{8,0},{16,24},{24,16},{32,40},{40,32},{48,56},{56,48},{64,72... | collective-permute-start | bytes 884744 | tf_op jit(solution)/shard_map/sibling/ppermute | solution.py:32
  24.4 19.2 %copy-start = (bf16[128,1152]{1,0:T(8,128)(2,1)}, bf16[128,1152]{1,0:T(8,128)(2,1)S(1)}, u32[]{:S(2)}) copy-start(bf16[128,1152]{1,0:T(8,128)(2,1)S(1)} %collective-permute-done.5.refs_6_) | copy-start | bytes 884740
  24.4 12.2 %collective-permute-start.9 = (bf16[128,1152]{1,0:T(8,128)(2,1)S(1)}, bf16[128,1152]{1,0:T(8,128)(2,1)S(1)}, u32[]{:S(2)}, u32[]{:S(2)}) collective-permute-start(bf16[128,1152]{1,0:T(8,128)(2,1)S(1)} %collective-permute-done.8.refs_10_), channel_id=1, source_target_pairs={{0,16},{8,24},{16,32},{24,40},{32,48},{40,56},{48,64},{56,72},{64,... | collective-permute-start | bytes 884744 | tf_op jit(solution)/shard_map/behind3/ppermute | solution.py:32
  24.5 19.2 %copy-start.2 = (bf16[128,1152]{1,0:T(8,128)(2,1)}, bf16[128,1152]{1,0:T(8,128)(2,1)S(1)}, u32[]{:S(2)}) copy-start(bf16[128,1152]{1,0:T(8,128)(2,1)S(1)} %collective-permute-done.refs_1_) | copy-start | bytes 884740
  24.5 13.0 %collective-permute-start.2 = (bf16[128,1152]{1,0:T(8,128)(2,1)S(1)}, bf16[128,1152]{1,0:T(8,128)(2,1)S(1)}, u32[]{:S(2)}, u32[]{:S(2)}) collective-permute-start(bf16[128,1152]{1,0:T(8,128)(2,1)S(1)} %collective-permute-done.refs_1_), channel_id=1, source_target_pairs={{0,1},{1,2},{2,3},{3,0},{4,5},{5,6},{6,7},{7,4},{8,11},{9,8},{10,9... | collective-permute-start | bytes 884744 | tf_op jit(solution)/shard_map/far1/ppermute | solution.py:51
  27.0 16.6 %copy-start.1 = (bf16[128,1152]{1,0:T(8,128)(2,1)}, bf16[128,1152]{1,0:T(8,128)(2,1)S(1)}, u32[]{:S(2)}) copy-start(bf16[128,1152]{1,0:T(8,128)(2,1)S(1)} %collective-permute-done.1.refs_2_) | copy-start | bytes 884740
  27.0 14.3 %collective-permute-start.6 = (bf16[128,1152]{1,0:T(8,128)(2,1)S(1)}, bf16[128,1152]{1,0:T(8,128)(2,1)S(1)}, u32[]{:S(2)}, u32[]{:S(2)}) collective-permute-start(bf16[128,1152]{1,0:T(8,128)(2,1)S(1)} %collective-permute-done.refs_1_), channel_id=1, source_target_pairs={{0,3},{1,0},{2,1},{3,2},{4,7},{5,4},{6,5},{7,6},{8,9},{9,10},{10,1... | collective-permute-start | bytes 884744 | tf_op jit(solution)/shard_map/far3/ppermute | solution.py:51
  27.0 14.2 %collective-permute-start.10 = (bf16[128,1152]{1,0:T(8,128)(2,1)S(1)}, bf16[128,1152]{1,0:T(8,128)(2,1)S(1)}, u32[]{:S(2)}, u32[]{:S(2)}) collective-permute-start(bf16[128,1152]{1,0:T(8,128)(2,1)S(1)} %collective-permute-done.7.refs_9_), channel_id=1, source_target_pairs={{0,8},{8,0},{16,24},{24,16},{32,40},{40,32},{48,56},{56,48},{64,72... | collective-permute-start | bytes 884744 | tf_op jit(solution)/shard_map/sibling/ppermute | solution.py:32
  27.9 13.4 %collective-permute-start.3 = (bf16[128,1152]{1,0:T(8,128)(2,1)S(1)}, bf16[128,1152]{1,0:T(8,128)(2,1)S(1)}, u32[]{:S(2)}, u32[]{:S(2)}) collective-permute-start(bf16[128,1152]{1,0:T(8,128)(2,1)S(1)} %collective-permute-done.1.refs_2_), channel_id=1, source_target_pairs={{0,1},{1,2},{2,3},{3,0},{4,5},{5,6},{6,7},{7,4},{8,11},{9,8},{10,9... | collective-permute-start | bytes 884744 | tf_op jit(solution)/shard_map/near2/ppermute | solution.py:51
  36.6 4.7 %collective-permute-start.12 = (bf16[128,1152]{1,0:T(8,128)(2,1)S(1)}, bf16[128,1152]{1,0:T(8,128)(2,1)S(1)}, u32[]{:S(2)}, u32[]{:S(2)}) collective-permute-start(bf16[128,1152]{1,0:T(8,128)(2,1)S(1)} %collective-permute-done.9.refs_11_), channel_id=1, source_target_pairs={{0,8},{8,0},{16,24},{24,16},{32,40},{40,32},{48,56},{56,48},{64,72... | collective-permute-start | bytes 884744 | tf_op jit(solution)/shard_map/sibling/ppermute | solution.py:32
  37.5 6.1 %collective-permute-start.4 = (bf16[128,1152]{1,0:T(8,128)(2,1)S(1)}, bf16[128,1152]{1,0:T(8,128)(2,1)S(1)}, u32[]{:S(2)}, u32[]{:S(2)}) collective-permute-start(bf16[128,1152]{1,0:T(8,128)(2,1)S(1)} %collective-permute-done.2.refs_3_), channel_id=1, source_target_pairs={{0,1},{1,2},{2,3},{3,0},{4,5},{5,6},{6,7},{7,4},{8,11},{9,8},{10,9... | collective-permute-start | bytes 884744 | tf_op jit(solution)/shard_map/far2/ppermute | solution.py:51
  63.7 5.9 %collective-permute-start.18 = (f32[128,1152]{1,0:T(8,128)}, f32[128,1152]{1,0:T(8,128)S(1)}, u32[]{:S(2)}, u32[]{:S(2)}) collective-permute-start(f32[128,1152]{1,0:T(8,128)} %get-tuple-element.31), channel_id=1, source_target_pairs={{0,8},{8,0},{16,24},{24,16},{32,40},{40,32},{48,56},{56,48},{64,72... | collective-permute-start | bytes 1769480 | tf_op jit(solution)/shard_map/back_sib1/ppermute | solution.py:32
  65.9 4.9 %collective-permute-start.19 = (f32[128,1152]{1,0:T(8,128)}, f32[128,1152]{1,0:T(8,128)S(1)}, u32[]{:S(2)}, u32[]{:S(2)}) collective-permute-start(f32[128,1152]{1,0:T(8,128)} %get-tuple-element.33), channel_id=1, source_target_pairs={{0,8},{8,0},{16,24},{24,16},{32,40},{40,32},{48,56},{56,48},{64,72... | collective-permute-start | bytes 1769480 | tf_op jit(solution)/shard_map/back_sib3/ppermute | solution.py:32
  66.0 26.1 %collective-permute-start.14 = (bf16[256,1152]{1,0:T(8,128)(2,1)}, bf16[256,1152]{1,0:T(8,128)(2,1)S(1)}, u32[]{:S(2)}, u32[]{:S(2)}) collective-permute-start(bf16[256,1152]{1,0:T(8,128)(2,1)} %get-tuple-element.24), channel_id=1, source_target_pairs={{0,3},{1,0},{2,1},{3,2},{4,7},{5,4},{6,5},{7,6},{8,9},{9,10},{10,1... | collective-permute-start | bytes 1769480 | tf_op jit(solution)/shard_map/back_x1/ppermute | solution.py:51
  66.0 26.8 %collective-permute-start.15 = (bf16[256,1152]{1,0:T(8,128)(2,1)}, bf16[256,1152]{1,0:T(8,128)(2,1)S(1)}, u32[]{:S(2)}, u32[]{:S(2)}) collective-permute-start(bf16[256,1152]{1,0:T(8,128)(2,1)} %get-tuple-element.25), channel_id=1, source_target_pairs={{0,2},{1,3},{2,0},{3,1},{4,6},{5,7},{6,4},{7,5},{8,10},{9,11},{10,... | collective-permute-start | bytes 1769480 | tf_op jit(solution)/shard_map/back_x2/ppermute | solution.py:51
  68.7 26.5 %collective-permute-start.16 = (bf16[256,1152]{1,0:T(8,128)(2,1)}, bf16[256,1152]{1,0:T(8,128)(2,1)S(1)}, u32[]{:S(2)}, u32[]{:S(2)}) collective-permute-start(bf16[256,1152]{1,0:T(8,128)(2,1)} %get-tuple-element.26), channel_id=1, source_target_pairs={{0,1},{1,2},{2,3},{3,0},{4,5},{5,6},{6,7},{7,4},{8,11},{9,8},{10,9... | collective-permute-start | bytes 1769480 | tf_op jit(solution)/shard_map/back_x3/ppermute | solution.py:51
  69.6 6.7 %collective-permute-start.21 = (bf16[128,1152]{1,0:T(8,128)(2,1)}, bf16[128,1152]{1,0:T(8,128)(2,1)S(1)}, u32[]{:S(2)}, u32[]{:S(2)}) collective-permute-start(bf16[128,1152]{1,0:T(8,128)(2,1)} %get-tuple-element.36), channel_id=1, source_target_pairs={{0,232},{8,0},{16,248},{24,16},{32,8},{40,32},{48,24},{56,48},{64,... | collective-permute-start | bytes 884744 | tf_op jit(solution)/shard_map/back_extra/ppermute | solution.py:32
  70.8 5.4 %collective-permute-start.20 = (f32[128,1152]{1,0:T(8,128)S(1)}, f32[128,1152]{1,0:T(8,128)S(1)}, u32[]{:S(2)}, u32[]{:S(2)}) collective-permute-start(f32[128,1152]{1,0:T(8,128)S(1)} %copy-done.20), channel_id=1, source_target_pairs={{0,8},{8,0},{16,24},{24,16},{32,40},{40,32},{48,56},{56,48},{64,72... | collective-permute-start | bytes 1769480 | tf_op jit(solution)/shard_map/back_sib2/ppermute | solution.py:32
  76.3 18.9 %copy-start.9 = (f32[128,1152]{1,0:T(8,128)S(1)}, f32[128,1152]{1,0:T(8,128)}, u32[]{:S(2)}) copy-start(f32[128,1152]{1,0:T(8,128)} %get-tuple-element.27) | copy-start | bytes 1769476
  76.5 21.3 %collective-permute-start.22 = (bf16[256,1152]{1,0:T(8,128)(2,1)}, bf16[256,1152]{1,0:T(8,128)(2,1)}, u32[]{:S(2)}, u32[]{:S(2)}) collective-permute-start(bf16[256,1152]{1,0:T(8,128)(2,1)} %pad_maximum_fusion), channel_id=1, source_target_pairs={{0,240},{8,248},{16,0},{24,8},{32,16},{40,24},{48,32},{56,40},{64,... | collective-permute-start | bytes 1769480 | tf_op jit(solution)/shard_map/back13/ppermute | solution.py:32
  79.9 16.9 %all-to-all-start = ((f32[32,8,128]{2,1,0:T(8,128)}), f32[32,8,128]{2,1,0:T(8,128)}, u32[]{:S(2)}, u32[]{:S(2)}) async-start(f32[32,8,128]{2,1,0:T(8,128)} %broadcast_in_dim.18), calls=%async_computation | async-start | bytes 262144 | tf_op jit(solution)/shard_map/loss_blk/all_to_all | solution.py:57
  96.4 10.5 %collective-permute-start.17 = (bf16[128,1152]{1,0:T(8,128)(2,1)}, bf16[128,1152]{1,0:T(8,128)(2,1)}, u32[]{:S(2)}, u32[]{:S(2)}) collective-permute-start(bf16[128,1152]{1,0:T(8,128)(2,1)} %fusion.48), channel_id=1, source_target_pairs={{0,4},{1,5},{2,6},{3,7},{4,0},{5,1},{6,2},{7,3},{8,12},{9,13},{10,... | collective-permute-start | bytes 884744 | tf_op jit(solution)/shard_map/back_across/ppermute | solution.py:41
  99.6 14.5 %collective-permute-start.23 = (bf16[128,1152]{1,0:T(8,128)(2,1)}, bf16[128,1152]{1,0:T(8,128)(2,1)}, u32[]{:S(2)}, u32[]{:S(2)}) collective-permute-start(bf16[128,1152]{1,0:T(8,128)(2,1)} %fusion.47), channel_id=1, source_target_pairs={{0,224},{8,232},{16,240},{24,248},{32,0},{40,8},{48,16},{56,24},{6... | collective-permute-start | bytes 884744 | tf_op jit(solution)/shard_map/back2/ppermute | solution.py:32
  101.3 10.7 %all-to-all-start.1 = ((f32[8,8,128]{2,1,0:T(8,128)}), f32[8,8,128]{2,1,0:T(8,128)}, u32[]{:S(2)}, u32[]{:S(2)}) async-start(f32[8,8,128]{2,1,0:T(8,128)} %broadcast_in_dim.19), calls=%async_computation.1 | async-start | bytes 65536 | tf_op jit(solution)/shard_map/loss_group/all_to_all | solution.py:57
  (15 other events, 92.5 us)

commit v3 on v2

v3 whole, which is shorter than its diff:
```python
import math

import jax
import jax.numpy as jnp
from jax import lax
from jax.experimental import pallas as pl
from jax.experimental.pallas import tpu as pltpu
from jax.sharding import PartitionSpec as P

STEPS = 8
TILE = 256
VMEM_LIMIT = 60 * 1024 * 1024
CODE_SCALE = 2.0**56
CODE_FLOOR = 2.0**-126
HINT = pl.CostEstimate(flops=1, bytes_accessed=1, transcendentals=0)


def encode(value):
    scaled = value * CODE_SCALE
    return (scaled * jnp.abs(scaled)).astype(jnp.bfloat16)


def decode(code):
    wide = code.astype(jnp.float32)
    return wide * lax.rsqrt(jnp.maximum(jnp.abs(wide), CODE_FLOOR)) * (1.0 / CODE_SCALE)


def shift_blk(value, even, odd, name):
    count = lax.axis_size("blk")
    pairs = [(s, (s + (odd if s % 2 else even)) % count) for s in range(count)]
    with jax.named_scope(name):
        return lax.ppermute(value, "blk", pairs)


def swap_core(value, name):
    return shift_blk(value, 1, -1, name)


def swap_y(value, name):
    with jax.named_scope(name):
        return lax.ppermute(value, "group", [(s, (s + 4) % 8) for s in range(8)])


def ring_x(value, steps, name):
    pairs = []
    for b in range(lax.axis_size("blk")):
        for g in range(8):
            x = g % 4 + (-steps if b % 2 else steps)
            pairs.append((b * 8 + g, b * 8 + g // 4 * 4 + x % 4))
    with jax.named_scope(name):
        return lax.ppermute(value, ("blk", "group"), pairs)


def sum_over(value, axis):
    with jax.named_scope(f"loss_{axis}"):
        return jnp.sum(lax.all_to_all(value, axis, 0, 0), axis=0)


def after(value, *others):
    return lax.optimization_barrier((value, *others))[0]


def any_specs(count):
    return [pl.BlockSpec(memory_space=pl.ANY)] * count


def params():
    return pltpu.CompilerParams(vmem_limit_bytes=VMEM_LIMIT)


def fetch_all(pairs, sems):
    copies = [pltpu.make_async_copy(source, target, sems.at[i]) for i, (source, target) in enumerate(pairs)]
    for c in copies:
        c.start()
    return copies


def share_slots(refs, place):
    rows = refs[0].shape[0]
    return [(r, place.at[pl.ds(i * rows, rows), :]) for i, r in enumerate(refs)]


def pairs_kernel(scale, bias_ref, *refs):
    image_refs, text_refs = refs[:8], refs[8:16]
    loss_ref, wide_refs, code_refs = refs[16], refs[17:19], refs[19:22]
    text_own_ref, text_mid_ref, text_sib_ref, text_extra_ref = refs[22:26]
    images, texts, coef, acc, stage, text_acc, text_stage, loss_acc, in_sems, out_sems = refs[26:]
    rows, width = image_refs[0].shape
    total = 8 * rows
    factor = scale[0] * (1.0 / math.sqrt(width))
    weight = factor * (1.0 / math.sqrt(STEPS * total))
    bias = bias_ref[0]
    slots = share_slots(text_refs, texts) + share_slots(image_refs, images)
    copies = [pltpu.make_async_copy(source, target, in_sems.at[i]) for i, (source, target) in enumerate(slots)]
    for i in (0, 1, 8, 9, 2, 3, 4, 5, 6, 7, 10, 11, 12, 13, 14, 15):
        copies[i].start()
    waited = set()
    sends = []

    def send(source, target):
        sends.append(pltpu.make_async_copy(source, target, out_sems.at[len(sends)]))
        sends[-1].start()

    loss_acc[...] = jnp.zeros_like(loss_acc)
    for it in range(total // TILE):
        place = pl.ds(it * TILE, TILE)
        for jt in range(total // TILE):
            for i in (8 + 2 * it, 9 + 2 * it, 2 * jt, 2 * jt + 1):
                if i not in waited:
                    copies[i].wait()
                    waited.add(i)
            left = images[place, :]
            right = texts[jt * TILE : (jt + 1) * TILE, :]
            logits = lax.dot_general(left, right, (((1,), (1,)), ((), ())), preferred_element_type=jnp.float32)
            logits = logits * factor + bias
            mixed = it == 0 and jt == 0
            if mixed:
                row = lax.broadcasted_iota(jnp.int32, (TILE, TILE), 0)
                col = lax.broadcasted_iota(jnp.int32, (TILE, TILE), 1)
                positive = jnp.logical_and(row == col, col < rows)
                logits = jnp.where(positive, -logits, logits)
            small = jnp.exp(-jnp.abs(logits))
            log1p = jnp.log(1.0 + small)
            part = jnp.exp(jnp.minimum(logits, 0.0) - log1p) * weight
            if mixed:
                part = jnp.where(positive, -part, part)
            coef[place, jt * TILE : (jt + 1) * TILE] = part.astype(jnp.bfloat16)
            exact = jnp.where(small < 2.0**-9, small * (1.0 - 0.5 * small), log1p)
            terms = jnp.maximum(logits, 0.0) + exact
            loss_acc[...] += jnp.sum(terms.reshape(TILE // 8, 8, TILE), axis=0)
        product = jnp.dot(coef[place, :], texts[...], preferred_element_type=jnp.float32)
        parts = [pl.ds(it * TILE + i * rows, rows) for i in range(2)]
        if it == 0:
            acc[...] = product
            for i in range(2):
                send(acc.at[parts[i], :], wide_refs[i])
        else:
            stage[place, :] = encode(product)
            send(stage.at[place, :], code_refs[it - 1])
    loss = loss_acc[:, : TILE // 2] + loss_acc[:, TILE // 2 :]
    loss_ref[...] = jnp.broadcast_to(loss[None], loss_ref.shape)
    for jt in (2, 3, 1, 0):
        place = pl.ds(jt * TILE, TILE)
        text_acc[place, :] = lax.dot_general(
            coef[:, jt * TILE : (jt + 1) * TILE], images[...], (((0,), (0,)), ((), ())), preferred_element_type=jnp.float32
        )
        for i in (2 * jt, 2 * jt + 1):
            part = text_acc.at[pl.ds(i * rows, rows), :]
            if i == 0:
                send(part, text_own_ref)
            elif i < 4:
                send(part, text_mid_ref.at[pl.ds((i - 1) * rows, rows), :])
            elif i < 7:
                send(part, text_sib_ref.at[pl.ds((i - 4) * rows, rows), :])
            else:
                text_stage[...] = encode(part[...])
                send(text_stage, text_extra_ref)
    for s in sends:
        s.wait()


def pairs_part(logit_scale, logit_bias, image_shares, text_shares):
    rows, width = image_shares[0].shape
    total = 8 * rows

    def wide(count):
        return jax.ShapeDtypeStruct((count, width), jnp.float32)

    def code(count):
        return jax.ShapeDtypeStruct((count, width), jnp.bfloat16)

    return pl.pallas_call(
        pairs_kernel,
        out_shape=[
            jax.ShapeDtypeStruct((lax.axis_size("blk"), 8, TILE // 2), jnp.float32),
            wide(rows),
            wide(rows),
            *[code(TILE)] * 3,
            wide(rows),
            wide(3 * rows),
            wide(3 * rows),
            code(rows),
        ],
        in_specs=[pl.BlockSpec(memory_space=pltpu.SMEM)] * 2 + any_specs(16),
        out_specs=[pl.BlockSpec(memory_space=pltpu.VMEM)] + any_specs(9),
        scratch_shapes=[
            pltpu.VMEM((total, width), jnp.bfloat16),
            pltpu.VMEM((total, width), jnp.bfloat16),
            pltpu.VMEM((total, total), jnp.bfloat16),
            pltpu.VMEM((TILE, width), jnp.float32),
            pltpu.VMEM((total, width), jnp.bfloat16),
            pltpu.VMEM((total, width), jnp.float32),
            pltpu.VMEM((rows, width), jnp.bfloat16),
            pltpu.VMEM((8, TILE), jnp.float32),
            pltpu.SemaphoreType.DMA((16,)),
            pltpu.SemaphoreType.DMA((20,)),
        ],
        compiler_params=params(),
        cost_estimate=HINT,
        name="pairs_part",
    )(logit_scale, logit_bias, *image_shares, *text_shares)


def body(images, texts, logit_scale, logit_bias):
    rows, width = images.shape
    core = lax.axis_index("blk") % 2
    across = swap_y(images, "across")
    behind2 = shift_blk(texts, 4, 4, "behind2")
    behind1 = shift_blk(texts, 2, 2, "behind1")
    near = [images]
    far = [across]
    for name, group in (("near", near), ("far", far)):
        one = ring_x(group[0], 1, f"{name}1")
        group += [one, ring_x(one, 1, f"{name}2"), ring_x(group[0], 3, f"{name}3")]
    extra = shift_blk(jnp.where(core == 0, texts, behind2), 1, 3, "extra")
    behind3 = shift_blk(behind2, 2, 2, "behind3")
    sib2 = swap_core(behind2, "sibling2")
    sib1 = swap_core(after(behind1, far[1], near[2]), "sibling1")
    sib3 = swap_core(after(behind3, far[1], near[2]), "sibling3")
    image_shares = [s for pair in zip(near, far) for s in pair]
    text_shares = [texts, behind1, behind3, behind2, sib1, sib3, sib2, extra]

    loss, own, other, *codes, gt_own, gt_mid, gt_sib, gt_extra = pairs_part(
        logit_scale, logit_bias, image_shares, text_shares
    )

    sibling = swap_core(gt_sib, "back_sib")
    back = [ring_x(c, -(i + 1), f"back_x{i + 1}") for i, c in enumerate(codes)]
    code13 = encode(gt_mid[: 2 * rows] + sibling[: 2 * rows])
    from13 = shift_blk(code13, -2, -2, "back13")
    extra_code = shift_blk(after(gt_extra, code13), -3, -1, "back_extra")
    loss = sum_over(after(loss, extra_code), "blk")
    from_extra = decode(extra_code)
    code2 = encode(
        gt_mid[2 * rows :] + sibling[2 * rows :] + jnp.where(core == 1, from_extra, 0.0) + decode(from13[rows:])
    )
    from2 = shift_blk(code2, -4, -4, "back2")
    for code in back:
        other = other + decode(code[rows:])
    other = encode(other)
    last = swap_y(other, "back_across")
    loss = jnp.broadcast_to(loss[None], (lax.axis_size("group"), *loss.shape))
    loss = jnp.sum(sum_over(after(loss, other, code2), "group"))
    for code in back:
        own = own + decode(code[:rows])
    grad_images = own + decode(last)
    grad_texts = gt_own + jnp.where(core == 0, from_extra, 0.0) + decode(from13[:rows]) + decode(from2)
    pairs = rows * lax.axis_size("group") * lax.axis_size("blk")
    loss = loss.reshape(1) / pairs
    return (grad_images, grad_texts, loss)


def solution(mesh):
    return jax.shard_map(
        body,
        mesh=mesh,
        in_specs=(P(("blk", "group"), None), P(("blk", "group"), None), P(), P()),
        out_specs=(P(("blk", "group"), None), P(("blk", "group"), None), P()),
        check_vma=False,
    )
```

time: 119 us -> 108 us (0.908); the launches traced: 117 us -> 108 us
  waiting for transfers between devices: 37.3 us -> 31.3 us
  Pallas kernels: 19.2 us -> 15.6 us
  starting transfers between devices: 41.7 us -> 44.8 us
  other arithmetic: 12.3 us -> 10.7 us
  local copies, waits for them, and re-layouts: 2.87 us -> 1.39 us
    ppermute x13 -> x11, waiting for transfers between devices: 23.5 us -> 12.5 us  [shift_blk(): return lax.ppermute(value, 'blk', pairs)]
    ppermute x13 -> x11, starting transfers between devices: 16.3 us -> 22.6 us  [shift_blk(): return lax.ppermute(value, 'blk', pairs)]
    ppermute x9, waiting for transfers between devices: 11 us -> 16.1 us  [ring_x(): return lax.ppermute(value, ('blk', 'group'), pairs)]
    pallas_call x2 -> x1, Pallas kernels: 19.2 us -> 15.6 us  [pairs_part(): pl.pallas_call(pairs_kernel, out_shape=[jax.ShapeDtypeStruct((lax.axis_si...]
    all_to_all x2, starting transfers between devices: 11.3 us -> 8.96 us  [sum_over(): return jnp.sum(lax.all_to_all(value, axis, 0, 0), axis=0)]
    convert_element_type x4 -> x3, other arithmetic: 4.32 us -> 6.13 us  [encode(): return (scaled * jnp.abs(scaled)).astype(jnp.bfloat16)]
    ppermute x9, starting transfers between devices: 13.2 us -> 11.5 us  [ring_x(): return lax.ppermute(value, ('blk', 'group'), pairs)]
    reduce_sum x2, other arithmetic: 2.31 us -> 0.64 us  [the longest x1 0.61 us: body(): loss = jnp.sum(sum_over(after(loss, other, code2), 'group'))]
  transfers between devices with their start and end apart: 26 -> 24, of which waited for: 9 -> 11; matrix products, arithmetic and copies ran while one was open for 10% -> 9% of each run, Pallas kernels for 0% -> 0%
where the time goes in v3:
time: 108 us
  starting transfers between devices  44.8 us (41%)
  waiting for transfers between devices  31.3 us (29%)
  Pallas kernels  15.6 us (14%)
  other arithmetic  10.7 us (10%)
  between operations  3.95 us (4%)
  local copies, waits for them, and re-layouts  1.39 us (1%)
    ppermute x11, starting transfers between devices, shift_blk(): return lax.ppermute(value, 'blk', pairs)  22.6 us
    ppermute x9, waiting for transfers between devices, ring_x(): return lax.ppermute(value, ('blk', 'group'), pairs)  16.1 us
    pallas_call x1, Pallas kernels, pairs_part(): pl.pallas_call(pairs_kernel, out_shape=[jax.ShapeDtypeStruct((lax.axis_si...  15.6 us
    ppermute x11, waiting for transfers between devices, shift_blk(): return lax.ppermute(value, 'blk', pairs)  12.5 us
    ppermute x9, starting transfers between devices, ring_x(): return lax.ppermute(value, ('blk', 'group'), pairs)  11.5 us
    all_to_all x2, starting transfers between devices, sum_over(): return jnp.sum(lax.all_to_all(value, axis, 0, 0), axis=0)  8.96 us
    convert_element_type x3, other arithmetic, encode(): return (scaled * jnp.abs(scaled)).astype(jnp.bfloat16)  6.13 us
    all_to_all x2, waiting for transfers between devices, sum_over(): return jnp.sum(lax.all_to_all(value, axis, 0, 0), axis=0)  2.71 us
  transfers between devices with their start and end apart: 24, of which 11 were waited for; matrix products, arithmetic and copies ran while one was open for 9% of the time, Pallas kernels for 0%

profile of v3, /device:TPU:1, one launch (start us, length us, event | category | flops | bytes accessed | tf_op | source)
XLA Modules:
  0.0 107.7 jit_solution(1469655530321134738)
XLA Ops:
  0.6 3.4 %collective-permute-start.1 = (bf16[128,1152]{1,0:T(8,128)(2,1)}, bf16[128,1152]{1,0:T(8,128)(2,1)S(1)}, u32[]{:S(2)}, u32[]{:S(2)}) collective-permute-start(bf16[128,1152]{1,0:T(8,128)(2,1)} %refs_0_.1), channel_id=1, source_target_pairs={{0,1},{1,2},{2,3},{3,0},{4,5},{5,6},{6,7},{7,4},{8,11},{9,8},{10,9... | collective-permute-start | bytes 884744 | tf_op jit(solution)/shard_map/near1/ppermute | solution.py:51
  4.0 1.3 %collective-permute-start = (bf16[128,1152]{1,0:T(8,128)(2,1)}, bf16[128,1152]{1,0:T(8,128)(2,1)S(1)}, u32[]{:S(2)}, u32[]{:S(2)}) collective-permute-start(bf16[128,1152]{1,0:T(8,128)(2,1)} %refs_0_.1), channel_id=1, source_target_pairs={{0,4},{1,5},{2,6},{3,7},{4,0},{5,1},{6,2},{7,3},{8,12},{9,13},{10,... | collective-permute-start | bytes 884744 | tf_op jit(solution)/shard_map/across/ppermute | solution.py:41
  5.3 1.6 %collective-permute-start.8 = (bf16[128,1152]{1,0:T(8,128)(2,1)}, bf16[128,1152]{1,0:T(8,128)(2,1)S(1)}, u32[]{:S(2)}, u32[]{:S(2)}) collective-permute-start(bf16[128,1152]{1,0:T(8,128)(2,1)} %refs_8_.1), channel_id=1, source_target_pairs={{0,32},{8,40},{16,48},{24,56},{32,64},{40,72},{48,80},{56,88},{64,... | collective-permute-start | bytes 884744 | tf_op jit(solution)/shard_map/behind2/ppermute | solution.py:32
  6.9 1.0 collective-permute-done.1.refs_2_
  8.0 3.0 %collective-permute-start.3 = (bf16[128,1152]{1,0:T(8,128)(2,1)S(1)}, bf16[128,1152]{1,0:T(8,128)(2,1)S(1)}, u32[]{:S(2)}, u32[]{:S(2)}) collective-permute-start(bf16[128,1152]{1,0:T(8,128)(2,1)S(1)} %collective-permute-done.1.refs_2_), channel_id=1, source_target_pairs={{0,1},{1,2},{2,3},{3,0},{4,5},{5,6},{6,7},{7,4},{8,11},{9,8},{10,9... | collective-permute-start | bytes 884744 | tf_op jit(solution)/shard_map/near2/ppermute | solution.py:51
  11.0 2.9 %collective-permute-start.7 = (bf16[128,1152]{1,0:T(8,128)(2,1)}, bf16[128,1152]{1,0:T(8,128)(2,1)S(1)}, u32[]{:S(2)}, u32[]{:S(2)}) collective-permute-start(bf16[128,1152]{1,0:T(8,128)(2,1)} %refs_8_.1), channel_id=1, source_target_pairs={{0,16},{8,24},{16,32},{24,40},{32,48},{40,56},{48,64},{56,72},{64,... | collective-permute-start | bytes 884744 | tf_op jit(solution)/shard_map/behind1/ppermute | solution.py:32
  13.9 4.6 %collective-permute-done.8.refs_11_ = bf16[128,1152]{1,0:T(8,128)(2,1)S(1)} collective-permute-done((bf16[128,1152]{1,0:T(8,128)(2,1)}, bf16[128,1152]{1,0:T(8,128)(2,1)S(1)}, u32[]{:S(2)}, u32[]{:S(2)}) %collective-permute-start.8) | collective-permute-done | bytes 294944 | tf_op jit(solution)/shard_map/behind2/ppermute | solution.py:32
  18.5 2.7 %collective-permute-start.9 = (bf16[128,1152]{1,0:T(8,128)(2,1)S(1)}, bf16[128,1152]{1,0:T(8,128)(2,1)S(1)}, u32[]{:S(2)}, u32[]{:S(2)}) collective-permute-start(bf16[128,1152]{1,0:T(8,128)(2,1)S(1)} %collective-permute-done.8.refs_11_), channel_id=1, source_target_pairs={{0,16},{8,24},{16,32},{24,40},{32,48},{40,56},{48,64},{56,72},{64,... | collective-permute-start | bytes 884744 | tf_op jit(solution)/shard_map/behind3/ppermute | solution.py:32
  21.3 5.0 %collective-permute-done.2.refs_3_ = bf16[128,1152]{1,0:T(8,128)(2,1)S(1)} collective-permute-done((bf16[128,1152]{1,0:T(8,128)(2,1)S(1)}, bf16[128,1152]{1,0:T(8,128)(2,1)S(1)}, u32[]{:S(2)}, u32[]{:S(2)}) %collective-permute-start.2) | collective-permute-done | bytes 294944 | tf_op jit(solution)/shard_map/far1/ppermute | solution.py:51
  26.3 3.0 %collective-permute-start.13 = (bf16[128,1152]{1,0:T(8,128)(2,1)S(1)}, bf16[128,1152]{1,0:T(8,128)(2,1)S(1)}, u32[]{:S(2)}, u32[]{:S(2)}) collective-permute-start(bf16[128,1152]{1,0:T(8,128)(2,1)S(1)} %broadcast_select_fusion), channel_id=1, source_target_pairs={{0,8},{8,32},{16,24},{24,48},{32,40},{40,64},{48,56},{56,80},{64,7... | collective-permute-start | bytes 884744 | tf_op jit(solution)/shard_map/extra/ppermute | solution.py:32
  29.3 0.9 collective-permute-done.9.refs_10_
  30.2 4.1 %collective-permute-start.12 = (bf16[128,1152]{1,0:T(8,128)(2,1)S(1)}, bf16[128,1152]{1,0:T(8,128)(2,1)S(1)}, u32[]{:S(2)}, u32[]{:S(2)}) collective-permute-start(bf16[128,1152]{1,0:T(8,128)(2,1)S(1)} %collective-permute-done.8.refs_11_), channel_id=1, source_target_pairs={{0,8},{8,0},{16,24},{24,16},{32,40},{40,32},{48,56},{56,48},{64,72... | collective-permute-start | bytes 884744 | tf_op jit(solution)/shard_map/sibling2/ppermute | solution.py:32
  34.4 2.4 %collective-permute-start.4 = (bf16[128,1152]{1,0:T(8,128)(2,1)S(1)}, bf16[128,1152]{1,0:T(8,128)(2,1)S(1)}, u32[]{:S(2)}, u32[]{:S(2)}) collective-permute-start(bf16[128,1152]{1,0:T(8,128)(2,1)S(1)} %collective-permute-done.2.refs_3_), channel_id=1, source_target_pairs={{0,1},{1,2},{2,3},{3,0},{4,5},{5,6},{6,7},{7,4},{8,11},{9,8},{10,9... | collective-permute-start | bytes 884744 | tf_op jit(solution)/shard_map/far2/ppermute | solution.py:51
  38.2 2.3 %collective-permute-done.4.refs_5_ = bf16[128,1152]{1,0:T(8,128)(2,1)S(1)} collective-permute-done((bf16[128,1152]{1,0:T(8,128)(2,1)S(1)}, bf16[128,1152]{1,0:T(8,128)(2,1)S(1)}, u32[]{:S(2)}, u32[]{:S(2)}) %collective-permute-start.4) | collective-permute-done | bytes 294944 | tf_op jit(solution)/shard_map/far2/ppermute | solution.py:51
  41.4 15.6 %pairs_part.1 = (f32[32,8,128]{2,1,0:T(8,128)}, f32[128,1152]{1,0:T(8,128)}, f32[128,1152]{1,0:T(8,128)}, bf16[256,1152]{1,0:T(8,128)(2,1)}, bf16[256,1152]{1,0:...) custom-call(f32[1]{0:T(128)S(6)} %copy.7.scale, ...), custom_call_target="tpu_custom_call" | custom-call | flops 1 | bytes 1 | tf_op jit(solution)/shard_map/pairs_part/pallas_call | solution.py:172
  57.0 2.3 %collective-permute-start.18 = (f32[384,1152]{1,0:T(8,128)}, f32[384,1152]{1,0:T(8,128)S(1)}, u32[]{:S(2)}, u32[]{:S(2)}) collective-permute-start(f32[384,1152]{1,0:T(8,128)} %get-tuple-element.28), channel_id=1, source_target_pairs={{0,8},{8,0},{16,24},{24,16},{32,40},{40,32},{48,56},{56,48},{64,72... | collective-permute-start | bytes 5308424 | tf_op jit(solution)/shard_map/back_sib/ppermute | solution.py:32
  59.3 2.4 %collective-permute-start.15 = (bf16[256,1152]{1,0:T(8,128)(2,1)}, bf16[256,1152]{1,0:T(8,128)(2,1)}, u32[]{:S(2)}, u32[]{:S(2)}) collective-permute-start(bf16[256,1152]{1,0:T(8,128)(2,1)} %get-tuple-element.22), channel_id=1, source_target_pairs={{0,2},{1,3},{2,0},{3,1},{4,6},{5,7},{6,4},{7,5},{8,10},{9,11},{10,... | collective-permute-start | bytes 1769480 | tf_op jit(solution)/shard_map/back_x2/ppermute | solution.py:51
  62.0 0.8 collective-permute-done.18
  62.8 2.3 %fusion = bf16[256,1152]{1,0:T(8,128)(2,1)} fusion(f32[384,1152]{1,0:T(8,128)S(1)} %collective-permute-done.18, f32[384,1152]{1,0:T(8,128)} %get-tuple-element.27), kind=kLoop, calls=%fused_computation.1 | loop fusion | flops 1474560 | bytes 2949120 | tf_op jit(solution)/shard_map/convert_element_type | solution.py:20
  65.5 3.2 %collective-permute-start.20 = (bf16[256,1152]{1,0:T(8,128)(2,1)}, bf16[256,1152]{1,0:T(8,128)(2,1)S(1)}, u32[]{:S(2)}, u32[]{:S(2)}) collective-permute-start(bf16[256,1152]{1,0:T(8,128)(2,1)} %fusion), channel_id=1, source_target_pairs={{0,240},{8,248},{16,0},{24,8},{32,16},{40,24},{48,32},{56,40},{64,... | collective-permute-start | bytes 1769480 | tf_op jit(solution)/shard_map/back13/ppermute | solution.py:32
  68.7 6.2 %collective-permute-done.19 = bf16[128,1152]{1,0:T(8,128)(2,1)S(1)} collective-permute-done((bf16[128,1152]{1,0:T(8,128)(2,1)S(1)}, bf16[128,1152]{1,0:T(8,128)(2,1)S(1)}, u32[]{:S(2)}, u32[]{:S(2)}) %collective-permute-start.19) | collective-permute-done | bytes 294944 | tf_op jit(solution)/shard_map/back_extra/ppermute | solution.py:32
  74.9 5.6 %all-to-all-start = ((f32[32,8,128]{2,1,0:T(8,128)}), f32[32,8,128]{2,1,0:T(8,128)S(1)}, u32[]{:S(2)}, u32[]{:S(2)}) async-start(f32[32,8,128]{2,1,0:T(8,128)} %get-tuple-element.31), calls=%async_computation | async-start | bytes 262144 | tf_op jit(solution)/shard_map/loss_blk/all_to_all | solution.py:56
  80.5 6.1 %collective-permute-done.14 = bf16[256,1152]{1,0:T(8,128)(2,1)S(1)} collective-permute-done((bf16[256,1152]{1,0:T(8,128)(2,1)}, bf16[256,1152]{1,0:T(8,128)(2,1)S(1)}, u32[]{:S(2)}, u32[]{:S(2)}) %collective-permute-start.14) | collective-permute-done | bytes 589856 | tf_op jit(solution)/shard_map/back_x1/ppermute | solution.py:51
  86.6 1.6 %collective-permute-done.16 = bf16[256,1152]{1,0:T(8,128)(2,1)} collective-permute-done((bf16[256,1152]{1,0:T(8,128)(2,1)}, bf16[256,1152]{1,0:T(8,128)(2,1)}, u32[]{:S(2)}, u32[]{:S(2)}) %collective-permute-start.16) | collective-permute-done | bytes 589856 | tf_op jit(solution)/shard_map/back_x3/ppermute | solution.py:51
  88.2 2.4 %fusion.49 = bf16[128,1152]{1,0:T(8,128)(2,1)} fusion(f32[128,1152]{1,0:T(8,128)} %get-tuple-element.24, bf16[256,1152]{1,0:T(8,128)(2,1)} %collective-permute-done.16, bf16[256,1152]{1,0:T(8,128)(2,1)} %collective-permute-done.15, bf16[256,1152]{1,0:T(8,128)(2,1)S(1)} %collective-permute-done.14), kind=kLoop, calls=%fused_computation.76 | loop fusion | flops 3244032 | bytes 1769472 | tf_op jit(solution)/shard_map/convert_element_type | solution.py:20
  91.4 1.4 %fusion.47 = bf16[128,1152]{1,0:T(8,128)(2,1)S(1)} fusion(f32[384,1152]{1,0:T(8,128)S(1)} %collective-permute-done.18, f32[384,1152]{1,0:T(8,128)} %get-tuple-element.27, bf16[128,1152]{1,0:T(8,128)(2,1)S(1)} %collective-permute-done.19, bf16[256,1152]{1,0:T(8,128)(2,1)S(1)} %collective-permute-done.20, pred[]{:T(512)S(6)} %eq.10), kind=kLoop, calls=%fused_computation.73 | loop fusion | flops 2654208 | bytes 2064385 | tf_op jit(solution)/shard_map/convert_element_type | solution.py:20
  92.9 2.1 %collective-permute-start.21 = (bf16[128,1152]{1,0:T(8,128)(2,1)S(1)}, bf16[128,1152]{1,0:T(8,128)(2,1)S(1)}, u32[]{:S(2)}, u32[]{:S(2)}) collective-permute-start(bf16[128,1152]{1,0:T(8,128)(2,1)S(1)} %fusion.47), channel_id=1, source_target_pairs={{0,224},{8,232},{16,240},{24,248},{32,0},{40,8},{48,16},{56,24},{6... | collective-permute-start | bytes 884744 | tf_op jit(solution)/shard_map/back2/ppermute | solution.py:32
  95.0 0.6 broadcast_in_dim.12
  95.6 3.3 %all-to-all-start.1 = ((f32[8,8,128]{2,1,0:T(8,128)}), f32[8,8,128]{2,1,0:T(8,128)S(1)}, u32[]{:S(2)}, u32[]{:S(2)}) async-start(f32[8,8,128]{2,1,0:T(8,128)} %broadcast_in_dim.12), calls=%async_computation.1 | async-start | bytes 65536 | tf_op jit(solution)/shard_map/loss_group/all_to_all | solution.py:56
  99.0 2.7 %fusion.8 = f32[128,1152]{1,0:T(8,128)} fusion(f32[128,1152]{1,0:T(8,128)} %get-tuple-element.20, bf16[128,1152]{1,0:T(8,128)(2,1)} %collective-permute-done.17, bf16[256,1152]{1,0:T(8,128)(2,1)} %collective-permute-done.16, bf16[256,1152]{1,0:T(8,128)(2,1)} %collective-permute-done.15, bf16[256,1152]{1,0:T(8,128)(2,1)S(1)} %collective-permute-done.14), kind=kLoop, calls=%fused_computation.34 | loop fusion | flops 3538944 | bytes 2359296 | tf_op jit(solution)/shard_map/add | solution.py:246
  101.7 2.4 %all-to-all-done.1 = f32[8,8,128]{2,1,0:T(8,128)S(1)} async-done(((f32[8,8,128]{2,1,0:T(8,128)}), f32[8,8,128]{2,1,0:T(8,128)S(1)}, u32[]{:S(2)}, u32[]{:S(2)}) %all-to-all-start.1) | async-done | bytes 32800 | tf_op jit(solution)/shard_map/loss_group/all_to_all | solution.py:56
  105.3 1.2 %fusion.38 = f32[128,1152]{1,0:T(8,128)} fusion(bf16[128,1152]{1,0:T(8,128)(2,1)S(1)} %collective-permute-done.21, f32[128,1152]{1,0:T(8,128)S(1)} %copy-done.1, bf16[128,1152]{1,0:T(8,128)(2,1)S(1)} %collective-permute-done.19, bf16[256,1152]{1,0:T(8,128)(2,1)S(1)} %collective-permute-done.20, pred[]{:T(512)S(6)} %eq.9), kind=kLoop, calls=%fused_computation.64 | loop fusion | flops 2801664 | bytes 2064385 | tf_op jit(solution)/shard_map/add | solution.py:247
  (56 shorter events, 3.0 us)
Async XLA Ops:
  0.6 7.4 %collective-permute-start.1 = (bf16[128,1152]{1,0:T(8,128)(2,1)}, bf16[128,1152]{1,0:T(8,128)(2,1)S(1)}, u32[]{:S(2)}, u32[]{:S(2)}) collective-permute-start(bf16[128,1152]{1,0:T(8,128)(2,1)} %refs_0_.1), channel_id=1, source_target_pairs={{0,1},{1,2},{2,3},{3,0},{4,5},{5,6},{6,7},{7,4},{8,11},{9,8},{10,9... | collective-permute-start | bytes 884744 | tf_op jit(solution)/shard_map/near1/ppermute | solution.py:51
  4.0 9.9 %collective-permute-start = (bf16[128,1152]{1,0:T(8,128)(2,1)}, bf16[128,1152]{1,0:T(8,128)(2,1)S(1)}, u32[]{:S(2)}, u32[]{:S(2)}) collective-permute-start(bf16[128,1152]{1,0:T(8,128)(2,1)} %refs_0_.1), channel_id=1, source_target_pairs={{0,4},{1,5},{2,6},{3,7},{4,0},{5,1},{6,2},{7,3},{8,12},{9,13},{10,... | collective-permute-start | bytes 884744 | tf_op jit(solution)/shard_map/across/ppermute | solution.py:41
  5.3 13.2 %collective-permute-start.8 = (bf16[128,1152]{1,0:T(8,128)(2,1)}, bf16[128,1152]{1,0:T(8,128)(2,1)S(1)}, u32[]{:S(2)}, u32[]{:S(2)}) collective-permute-start(bf16[128,1152]{1,0:T(8,128)(2,1)} %refs_8_.1), channel_id=1, source_target_pairs={{0,32},{8,40},{16,48},{24,56},{32,64},{40,72},{48,80},{56,88},{64,... | collective-permute-start | bytes 884744 | tf_op jit(solution)/shard_map/behind2/ppermute | solution.py:32
  8.0 32.6 %copy-start.2 = (bf16[128,1152]{1,0:T(8,128)(2,1)}, bf16[128,1152]{1,0:T(8,128)(2,1)S(1)}, u32[]{:S(2)}) copy-start(bf16[128,1152]{1,0:T(8,128)(2,1)S(1)} %collective-permute-done.1.refs_2_) | copy-start | bytes 884740
  8.0 10.5 %collective-permute-start.3 = (bf16[128,1152]{1,0:T(8,128)(2,1)S(1)}, bf16[128,1152]{1,0:T(8,128)(2,1)S(1)}, u32[]{:S(2)}, u32[]{:S(2)}) collective-permute-start(bf16[128,1152]{1,0:T(8,128)(2,1)S(1)} %collective-permute-done.1.refs_2_), channel_id=1, source_target_pairs={{0,1},{1,2},{2,3},{3,0},{4,5},{5,6},{6,7},{7,4},{8,11},{9,8},{10,9... | collective-permute-start | bytes 884744 | tf_op jit(solution)/shard_map/near2/ppermute | solution.py:51
  11.0 23.4 %collective-permute-start.5 = (bf16[128,1152]{1,0:T(8,128)(2,1)}, bf16[128,1152]{1,0:T(8,128)(2,1)S(1)}, u32[]{:S(2)}, u32[]{:S(2)}) collective-permute-start(bf16[128,1152]{1,0:T(8,128)(2,1)} %refs_0_.1), channel_id=1, source_target_pairs={{0,3},{1,0},{2,1},{3,2},{4,7},{5,4},{6,5},{7,6},{8,9},{9,10},{10,1... | collective-permute-start | bytes 884744 | tf_op jit(solution)/shard_map/near3/ppermute | solution.py:51
  11.0 23.3 %collective-permute-start.7 = (bf16[128,1152]{1,0:T(8,128)(2,1)}, bf16[128,1152]{1,0:T(8,128)(2,1)S(1)}, u32[]{:S(2)}, u32[]{:S(2)}) collective-permute-start(bf16[128,1152]{1,0:T(8,128)(2,1)} %refs_8_.1), channel_id=1, source_target_pairs={{0,16},{8,24},{16,32},{24,40},{32,48},{40,56},{48,64},{56,72},{64,... | collective-permute-start | bytes 884744 | tf_op jit(solution)/shard_map/behind1/ppermute | solution.py:32
  13.9 26.6 %copy-start.3 = (bf16[128,1152]{1,0:T(8,128)(2,1)}, bf16[128,1152]{1,0:T(8,128)(2,1)S(1)}, u32[]{:S(2)}) copy-start(bf16[128,1152]{1,0:T(8,128)(2,1)S(1)} %collective-permute-done.refs_1_) | copy-start | bytes 884740
  13.9 22.9 %collective-permute-start.6 = (bf16[128,1152]{1,0:T(8,128)(2,1)S(1)}, bf16[128,1152]{1,0:T(8,128)(2,1)S(1)}, u32[]{:S(2)}, u32[]{:S(2)}) collective-permute-start(bf16[128,1152]{1,0:T(8,128)(2,1)S(1)} %collective-permute-done.refs_1_), channel_id=1, source_target_pairs={{0,3},{1,0},{2,1},{3,2},{4,7},{5,4},{6,5},{7,6},{8,9},{9,10},{10,1... | collective-permute-start | bytes 884744 | tf_op jit(solution)/shard_map/far3/ppermute | solution.py:51
  18.5 22.1 %copy-start = (bf16[128,1152]{1,0:T(8,128)(2,1)}, bf16[128,1152]{1,0:T(8,128)(2,1)S(1)}, u32[]{:S(2)}) copy-start(bf16[128,1152]{1,0:T(8,128)(2,1)S(1)} %collective-permute-done.8.refs_11_) | copy-start | bytes 884740
  18.5 7.8 %collective-permute-start.2 = (bf16[128,1152]{1,0:T(8,128)(2,1)S(1)}, bf16[128,1152]{1,0:T(8,128)(2,1)S(1)}, u32[]{:S(2)}, u32[]{:S(2)}) collective-permute-start(bf16[128,1152]{1,0:T(8,128)(2,1)S(1)} %collective-permute-done.refs_1_), channel_id=1, source_target_pairs={{0,1},{1,2},{2,3},{3,0},{4,5},{5,6},{6,7},{7,4},{8,11},{9,8},{10,9... | collective-permute-start | bytes 884744 | tf_op jit(solution)/shard_map/far1/ppermute | solution.py:51
  18.5 22.1 %copy-start.4 = (bf16[128,1152]{1,0:T(8,128)(2,1)}, bf16[128,1152]{1,0:T(8,128)(2,1)S(1)}, u32[]{:S(2)}) copy-start(bf16[128,1152]{1,0:T(8,128)(2,1)S(1)} %collective-permute-done.3.refs_4_) | copy-start | bytes 884740
  18.5 11.6 %collective-permute-start.9 = (bf16[128,1152]{1,0:T(8,128)(2,1)S(1)}, bf16[128,1152]{1,0:T(8,128)(2,1)S(1)}, u32[]{:S(2)}, u32[]{:S(2)}) collective-permute-start(bf16[128,1152]{1,0:T(8,128)(2,1)S(1)} %collective-permute-done.8.refs_11_), channel_id=1, source_target_pairs={{0,16},{8,24},{16,32},{24,40},{32,48},{40,56},{48,64},{56,72},{64,... | collective-permute-start | bytes 884744 | tf_op jit(solution)/shard_map/behind3/ppermute | solution.py:32
  26.3 14.3 %copy-start.8 = (bf16[128,1152]{1,0:T(8,128)(2,1)}, bf16[128,1152]{1,0:T(8,128)(2,1)S(1)}, u32[]{:S(2)}) copy-start(bf16[128,1152]{1,0:T(8,128)(2,1)S(1)} %collective-permute-done.2.refs_3_) | copy-start | bytes 884740
  26.3 11.9 %collective-permute-start.13 = (bf16[128,1152]{1,0:T(8,128)(2,1)S(1)}, bf16[128,1152]{1,0:T(8,128)(2,1)S(1)}, u32[]{:S(2)}, u32[]{:S(2)}) collective-permute-start(bf16[128,1152]{1,0:T(8,128)(2,1)S(1)} %broadcast_select_fusion), channel_id=1, source_target_pairs={{0,8},{8,32},{16,24},{24,48},{32,40},{40,64},{48,56},{56,80},{64,7... | collective-permute-start | bytes 884744 | tf_op jit(solution)/shard_map/extra/ppermute | solution.py:32
  30.2 10.4 %copy-start.9 = (bf16[128,1152]{1,0:T(8,128)(2,1)}, bf16[128,1152]{1,0:T(8,128)(2,1)S(1)}, u32[]{:S(2)}) copy-start(bf16[128,1152]{1,0:T(8,128)(2,1)S(1)} %collective-permute-done.9.refs_10_) | copy-start | bytes 884740
  30.2 8.0 %collective-permute-start.12 = (bf16[128,1152]{1,0:T(8,128)(2,1)S(1)}, bf16[128,1152]{1,0:T(8,128)(2,1)S(1)}, u32[]{:S(2)}, u32[]{:S(2)}) collective-permute-start(bf16[128,1152]{1,0:T(8,128)(2,1)S(1)} %collective-permute-done.8.refs_11_), channel_id=1, source_target_pairs={{0,8},{8,0},{16,24},{24,16},{32,40},{40,32},{48,56},{56,48},{64,72... | collective-permute-start | bytes 884744 | tf_op jit(solution)/shard_map/sibling2/ppermute | solution.py:32
  34.3 6.2 %collective-permute-start.11 = (bf16[128,1152]{1,0:T(8,128)(2,1)S(1)}, bf16[128,1152]{1,0:T(8,128)(2,1)S(1)}, u32[]{:S(2)}, u32[]{:S(2)}) collective-permute-start(bf16[128,1152]{1,0:T(8,128)(2,1)S(1)} %collective-permute-done.9.refs_10_), channel_id=1, source_target_pairs={{0,8},{8,0},{16,24},{24,16},{32,40},{40,32},{48,56},{56,48},{64,72... | collective-permute-start | bytes 884744 | tf_op jit(solution)/shard_map/sibling3/ppermute | solution.py:32
  34.4 6.1 %collective-permute-start.4 = (bf16[128,1152]{1,0:T(8,128)(2,1)S(1)}, bf16[128,1152]{1,0:T(8,128)(2,1)S(1)}, u32[]{:S(2)}, u32[]{:S(2)}) collective-permute-start(bf16[128,1152]{1,0:T(8,128)(2,1)S(1)} %collective-permute-done.2.refs_3_), channel_id=1, source_target_pairs={{0,1},{1,2},{2,3},{3,0},{4,5},{5,6},{6,7},{7,4},{8,11},{9,8},{10,9... | collective-permute-start | bytes 884744 | tf_op jit(solution)/shard_map/far2/ppermute | solution.py:51
  36.9 3.7 %collective-permute-start.10 = (bf16[128,1152]{1,0:T(8,128)(2,1)S(1)}, bf16[128,1152]{1,0:T(8,128)(2,1)}, u32[]{:S(2)}, u32[]{:S(2)}) collective-permute-start(bf16[128,1152]{1,0:T(8,128)(2,1)S(1)} %collective-permute-done.7.refs_9_), channel_id=1, source_target_pairs={{0,8},{8,0},{16,24},{24,16},{32,40},{40,32},{48,56},{56,48},{64,72... | collective-permute-start | bytes 884744 | tf_op jit(solution)/shard_map/sibling1/ppermute | solution.py:32
  57.0 8.1 %copy-start.14 = (bf16[128,1152]{1,0:T(8,128)(2,1)S(1)}, bf16[128,1152]{1,0:T(8,128)(2,1)}, u32[]{:S(2)}) copy-start(bf16[128,1152]{1,0:T(8,128)(2,1)} %get-tuple-element.29) | copy-start | bytes 884740
  57.0 5.9 %collective-permute-start.18 = (f32[384,1152]{1,0:T(8,128)}, f32[384,1152]{1,0:T(8,128)S(1)}, u32[]{:S(2)}, u32[]{:S(2)}) collective-permute-start(f32[384,1152]{1,0:T(8,128)} %get-tuple-element.28), channel_id=1, source_target_pairs={{0,8},{8,0},{16,24},{24,16},{32,40},{40,32},{48,56},{56,48},{64,72... | collective-permute-start | bytes 5308424 | tf_op jit(solution)/shard_map/back_sib/ppermute | solution.py:32
  59.3 27.3 %collective-permute-start.14 = (bf16[256,1152]{1,0:T(8,128)(2,1)}, bf16[256,1152]{1,0:T(8,128)(2,1)S(1)}, u32[]{:S(2)}, u32[]{:S(2)}) collective-permute-start(bf16[256,1152]{1,0:T(8,128)(2,1)} %get-tuple-element.21), channel_id=1, source_target_pairs={{0,3},{1,0},{2,1},{3,2},{4,7},{5,4},{6,5},{7,6},{8,9},{9,10},{10,1... | collective-permute-start | bytes 1769480 | tf_op jit(solution)/shard_map/back_x1/ppermute | solution.py:51
  59.3 27.3 %collective-permute-start.15 = (bf16[256,1152]{1,0:T(8,128)(2,1)}, bf16[256,1152]{1,0:T(8,128)(2,1)}, u32[]{:S(2)}, u32[]{:S(2)}) collective-permute-start(bf16[256,1152]{1,0:T(8,128)(2,1)} %get-tuple-element.22), channel_id=1, source_target_pairs={{0,2},{1,3},{2,0},{3,1},{4,6},{5,7},{6,4},{7,5},{8,10},{9,11},{10,... | collective-permute-start | bytes 1769480 | tf_op jit(solution)/shard_map/back_x2/ppermute | solution.py:51
  61.7 26.5 %collective-permute-start.16 = (bf16[256,1152]{1,0:T(8,128)(2,1)}, bf16[256,1152]{1,0:T(8,128)(2,1)}, u32[]{:S(2)}, u32[]{:S(2)}) collective-permute-start(bf16[256,1152]{1,0:T(8,128)(2,1)} %get-tuple-element.23), channel_id=1, source_target_pairs={{0,1},{1,2},{2,3},{3,0},{4,5},{5,6},{6,7},{7,4},{8,11},{9,8},{10,9... | collective-permute-start | bytes 1769480 | tf_op jit(solution)/shard_map/back_x3/ppermute | solution.py:51
  65.1 9.8 %collective-permute-start.19 = (bf16[128,1152]{1,0:T(8,128)(2,1)S(1)}, bf16[128,1152]{1,0:T(8,128)(2,1)S(1)}, u32[]{:S(2)}, u32[]{:S(2)}) collective-permute-start(bf16[128,1152]{1,0:T(8,128)(2,1)S(1)} %copy-done.14), channel_id=1, source_target_pairs={{0,232},{8,0},{16,248},{24,16},{32,8},{40,32},{48,24},{56,48},{64,... | collective-permute-start | bytes 884744 | tf_op jit(solution)/shard_map/back_extra/ppermute | solution.py:32
  65.5 25.9 %collective-permute-start.20 = (bf16[256,1152]{1,0:T(8,128)(2,1)}, bf16[256,1152]{1,0:T(8,128)(2,1)S(1)}, u32[]{:S(2)}, u32[]{:S(2)}) collective-permute-start(bf16[256,1152]{1,0:T(8,128)(2,1)} %fusion), channel_id=1, source_target_pairs={{0,240},{8,248},{16,0},{24,8},{32,16},{40,24},{48,32},{56,40},{64,... | collective-permute-start | bytes 1769480 | tf_op jit(solution)/shard_map/back13/ppermute | solution.py:32
  74.9 16.5 %all-to-all-start = ((f32[32,8,128]{2,1,0:T(8,128)}), f32[32,8,128]{2,1,0:T(8,128)S(1)}, u32[]{:S(2)}, u32[]{:S(2)}) async-start(f32[32,8,128]{2,1,0:T(8,128)} %get-tuple-element.31), calls=%async_computation | async-start | bytes 262144 | tf_op jit(solution)/shard_map/loss_blk/all_to_all | solution.py:56
  90.6 8.4 %collective-permute-start.17 = (bf16[128,1152]{1,0:T(8,128)(2,1)}, bf16[128,1152]{1,0:T(8,128)(2,1)}, u32[]{:S(2)}, u32[]{:S(2)}) collective-permute-start(bf16[128,1152]{1,0:T(8,128)(2,1)} %fusion.49), channel_id=1, source_target_pairs={{0,4},{1,5},{2,6},{3,7},{4,0},{5,1},{6,2},{7,3},{8,12},{9,13},{10,... | collective-permute-start | bytes 884744 | tf_op jit(solution)/shard_map/back_across/ppermute | solution.py:41
  92.9 12.4 %copy-start.1 = (f32[128,1152]{1,0:T(8,128)S(1)}, f32[128,1152]{1,0:T(8,128)}, u32[]{:S(2)}) copy-start(f32[128,1152]{1,0:T(8,128)} %get-tuple-element.25) | copy-start | bytes 1769476
  92.9 12.4 %collective-permute-start.21 = (bf16[128,1152]{1,0:T(8,128)(2,1)S(1)}, bf16[128,1152]{1,0:T(8,128)(2,1)S(1)}, u32[]{:S(2)}, u32[]{:S(2)}) collective-permute-start(bf16[128,1152]{1,0:T(8,128)(2,1)S(1)} %fusion.47), channel_id=1, source_target_pairs={{0,224},{8,232},{16,240},{24,248},{32,0},{40,8},{48,16},{56,24},{6... | collective-permute-start | bytes 884744 | tf_op jit(solution)/shard_map/back2/ppermute | solution.py:32
  95.6 8.4 %all-to-all-start.1 = ((f32[8,8,128]{2,1,0:T(8,128)}), f32[8,8,128]{2,1,0:T(8,128)S(1)}, u32[]{:S(2)}, u32[]{:S(2)}) async-start(f32[8,8,128]{2,1,0:T(8,128)} %broadcast_in_dim.12), calls=%async_computation.1 | async-start | bytes 65536 | tf_op jit(solution)/shard_map/loss_group/all_to_all | solution.py:56
  (7 other events, 22.7 us)

commit v4 on v3

--- a/solution.py
+++ b/solution.py
@@ -34,6 +34,11 @@
 
 def swap_core(value, name):
     return shift_blk(value, 1, -1, name)
+
+
+def flip_y(value, name):
+    with jax.named_scope(name):
+        return lax.ppermute(value, "blk", [(s, s ^ 2) for s in range(lax.axis_size("blk"))])
 
 
 def swap_y(value, name):
@@ -204,19 +209,22 @@
 def body(images, texts, logit_scale, logit_bias):
     rows, width = images.shape
     core = lax.axis_index("blk") % 2
+    half = lax.axis_index("blk") // 2 % 2
     across = swap_y(images, "across")
     behind2 = shift_blk(texts, 4, 4, "behind2")
-    behind1 = shift_blk(texts, 2, 2, "behind1")
+    behind1 = flip_y(jnp.where(half == 0, texts, behind2), "behind1")
     near = [images]
     far = [across]
     for name, group in (("near", near), ("far", far)):
         one = ring_x(group[0], 1, f"{name}1")
-        group += [one, ring_x(one, 1, f"{name}2"), ring_x(group[0], 3, f"{name}3")]
+        three = ring_x(group[0], 3, f"{name}3")
+        two = ring_x(one if name == "near" else after(one, near[3]), 1, f"{name}2")
+        group += [one, two, three]
     extra = shift_blk(jnp.where(core == 0, texts, behind2), 1, 3, "extra")
-    behind3 = shift_blk(behind2, 2, 2, "behind3")
+    behind3 = shift_blk(behind1, 4, 4, "behind3")
     sib2 = swap_core(behind2, "sibling2")
-    sib1 = swap_core(after(behind1, far[1], near[2]), "sibling1")
-    sib3 = swap_core(after(behind3, far[1], near[2]), "sibling3")
+    sib1 = swap_core(behind1, "sibling1")
+    sib3 = swap_core(behind3, "sibling3")
     image_shares = [s for pair in zip(near, far) for s in pair]
     text_shares = [texts, behind1, behind3, behind2, sib1, sib3, sib2, extra]
 
@@ -229,7 +237,7 @@
     code13 = encode(gt_mid[: 2 * rows] + sibling[: 2 * rows])
     from13 = shift_blk(code13, -2, -2, "back13")
     extra_code = shift_blk(after(gt_extra, code13), -3, -1, "back_extra")
-    loss = sum_over(after(loss, extra_code), "blk")
+    loss = sum_over(after(loss, code13), "blk")
     from_extra = decode(extra_code)
     code2 = encode(
         gt_mid[2 * rows :] + sibling[2 * rows :] + jnp.where(core == 1, from_extra, 0.0) + decode(from13[rows:])

time: 108 us -> 107 us (level)
  waiting for transfers between devices: 31.3 us -> 26.3 us
  starting transfers between devices: 44.8 us -> 47.9 us
  other arithmetic: 10.7 us -> 11.8 us
    ppermute x11 -> x10, waiting for transfers between devices: 12.5 us -> 7.98 us  [shift_blk(): return lax.ppermute(value, 'blk', pairs)]
    ppermute x11 -> x10, starting transfers between devices: 22.6 us -> 19.3 us  [shift_blk(): return lax.ppermute(value, 'blk', pairs)]
    ppermute x0 -> x1, starting transfers between devices: none -> 3 us  [flip_y(): lax.ppermute(value, 'blk', [(s, s ^ 2) for s in range(lax.axis_size('blk'...]
    ppermute x9, starting transfers between devices: 11.5 us -> 13.4 us  [ring_x(): return lax.ppermute(value, ('blk', 'group'), pairs)]
    all_to_all x2, starting transfers between devices: 8.96 us -> 10.5 us  [sum_over(): return jnp.sum(lax.all_to_all(value, axis, 0, 0), axis=0)]
    select_n x1, other arithmetic: 0.04 us -> 1.13 us  [body(): extra = shift_blk(jnp.where(core == 0, texts, behind2), 1, 3, 'extra')]
  transfers between devices with their start and end apart: 24 -> 24, of which waited for: 11 -> 6; matrix products, arithmetic and copies ran while one was open for 9% -> 10% of each run, Pallas kernels for 0% -> 0%
where the time goes in v4:
time: 107 us
  starting transfers between devices  47.9 us (45%)
  waiting for transfers between devices  26.3 us (25%)
  Pallas kernels  15.6 us (15%)
  other arithmetic  11.8 us (11%)
  between operations  3.94 us (4%)
  local copies, waits for them, and re-layouts  1.55 us (1%)
    ppermute x10, starting transfers between devices, shift_blk(): return lax.ppermute(value, 'blk', pairs)  19.3 us
    ppermute x9, waiting for transfers between devices, ring_x(): return lax.ppermute(value, ('blk', 'group'), pairs)  15.9 us
    pallas_call x1, Pallas kernels, pairs_part(): pl.pallas_call(pairs_kernel, out_shape=[jax.ShapeDtypeStruct((lax.axis_si...  15.6 us
    ppermute x9, starting transfers between devices, ring_x(): return lax.ppermute(value, ('blk', 'group'), pairs)  13.4 us
    all_to_all x2, starting transfers between devices, sum_over(): return jnp.sum(lax.all_to_all(value, axis, 0, 0), axis=0)  10.5 us
    ppermute x10, waiting for transfers between devices, shift_blk(): return lax.ppermute(value, 'blk', pairs)  7.98 us
    convert_element_type x3, other arithmetic, encode(): return (scaled * jnp.abs(scaled)).astype(jnp.bfloat16)  6.13 us
    ppermute x1, starting transfers between devices, flip_y(): lax.ppermute(value, 'blk', [(s, s ^ 2) for s in range(lax.axis_size('blk'...  3 us
  transfers between devices with their start and end apart: 24, of which 6 were waited for; matrix products, arithmetic and copies ran while one was open for 10% of the time, Pallas kernels for 0%

profile of v4, /device:TPU:1, one launch (start us, length us, event | category | flops | bytes accessed | tf_op | source)
XLA Modules:
  0.0 107.1 jit_solution(5695001070416377665)
XLA Ops:
  0.6 2.5 %collective-permute-start.7 = (bf16[128,1152]{1,0:T(8,128)(2,1)}, bf16[128,1152]{1,0:T(8,128)(2,1)S(1)}, u32[]{:S(2)}, u32[]{:S(2)}) collective-permute-start(bf16[128,1152]{1,0:T(8,128)(2,1)} %refs_8_.1), channel_id=1, source_target_pairs={{0,32},{8,40},{16,48},{24,56},{32,64},{40,72},{48,80},{56,88},{64,... | collective-permute-start | bytes 884744 | tf_op jit(solution)/shard_map/behind2/ppermute | solution.py:32
  3.2 2.5 %collective-permute-start.1 = (bf16[128,1152]{1,0:T(8,128)(2,1)}, bf16[128,1152]{1,0:T(8,128)(2,1)S(1)}, u32[]{:S(2)}, u32[]{:S(2)}) collective-permute-start(bf16[128,1152]{1,0:T(8,128)(2,1)} %refs_0_.1), channel_id=1, source_target_pairs={{0,1},{1,2},{2,3},{3,0},{4,5},{5,6},{6,7},{7,4},{8,11},{9,8},{10,9... | collective-permute-start | bytes 884744 | tf_op jit(solution)/shard_map/near1/ppermute | solution.py:56
  5.7 1.3 %collective-permute-start = (bf16[128,1152]{1,0:T(8,128)(2,1)}, bf16[128,1152]{1,0:T(8,128)(2,1)S(1)}, u32[]{:S(2)}, u32[]{:S(2)}) collective-permute-start(bf16[128,1152]{1,0:T(8,128)(2,1)} %refs_0_.1), channel_id=1, source_target_pairs={{0,4},{1,5},{2,6},{3,7},{4,0},{5,1},{6,2},{7,3},{8,12},{9,13},{10,... | collective-permute-start | bytes 884744 | tf_op jit(solution)/shard_map/across/ppermute | solution.py:46
  6.9 7.1 %collective-permute-done.7.refs_11_ = bf16[128,1152]{1,0:T(8,128)(2,1)S(1)} collective-permute-done((bf16[128,1152]{1,0:T(8,128)(2,1)}, bf16[128,1152]{1,0:T(8,128)(2,1)S(1)}, u32[]{:S(2)}, u32[]{:S(2)}) %collective-permute-start.7) | collective-permute-done | bytes 294944 | tf_op jit(solution)/shard_map/behind2/ppermute | solution.py:32
  14.1 1.1 %broadcast_select_fusion = (bf16[128,1152]{1,0:T(8,128)(2,1)S(1)}, bf16[128,1152]{1,0:T(8,128)(2,1)S(1)}) fusion(bf16[128,1152]{1,0:T(8,128)(2,1)} %refs_8_.1, bf16[128,1152]{1,0:T(8,128)(2,1)S(1)} %collective-permute-done.7.refs_11_, pred[]{:T(512)S(6)} %eq.14, pred[]{:T(512)S(6)} %eq.13), kind=kLoop, calls=%fused_computation.77 | loop fusion | flops 294912 | bytes 1179650 | tf_op jit(solution)/shard_map/jit(_where)/select_n | solution.py:223
  15.2 3.0 %collective-permute-start.8 = (bf16[128,1152]{1,0:T(8,128)(2,1)S(1)}, bf16[128,1152]{1,0:T(8,128)(2,1)S(1)}, u32[]{:S(2)}, u32[]{:S(2)}) collective-permute-start(bf16[128,1152]{1,0:T(8,128)(2,1)S(1)} %get-tuple-element.32), channel_id=1, source_target_pairs={{0,16},{8,24},{16,0},{24,8},{32,48},{40,56},{48,32},{56,40},{64,80... | collective-permute-start | bytes 884744 | tf_op jit(solution)/shard_map/behind1/ppermute | solution.py:41
  18.2 1.2 %collective-permute-start.4 = (bf16[128,1152]{1,0:T(8,128)(2,1)}, bf16[128,1152]{1,0:T(8,128)(2,1)S(1)}, u32[]{:S(2)}, u32[]{:S(2)}) collective-permute-start(bf16[128,1152]{1,0:T(8,128)(2,1)} %refs_0_.1), channel_id=1, source_target_pairs={{0,3},{1,0},{2,1},{3,2},{4,7},{5,4},{6,5},{7,6},{8,9},{9,10},{10,1... | collective-permute-start | bytes 884744 | tf_op jit(solution)/shard_map/near3/ppermute | solution.py:56
  19.4 1.5 %collective-permute-start.2 = (bf16[128,1152]{1,0:T(8,128)(2,1)S(1)}, bf16[128,1152]{1,0:T(8,128)(2,1)S(1)}, u32[]{:S(2)}, u32[]{:S(2)}) collective-permute-start(bf16[128,1152]{1,0:T(8,128)(2,1)S(1)} %collective-permute-done.refs_1_), channel_id=1, source_target_pairs={{0,1},{1,2},{2,3},{3,0},{4,5},{5,6},{6,7},{7,4},{8,11},{9,8},{10,9... | collective-permute-start | bytes 884744 | tf_op jit(solution)/shard_map/far1/ppermute | solution.py:56
  20.9 1.7 %collective-permute-start.12 = (bf16[128,1152]{1,0:T(8,128)(2,1)S(1)}, bf16[128,1152]{1,0:T(8,128)(2,1)S(1)}, u32[]{:S(2)}, u32[]{:S(2)}) collective-permute-start(bf16[128,1152]{1,0:T(8,128)(2,1)S(1)} %collective-permute-done.7.refs_11_), channel_id=1, source_target_pairs={{0,8},{8,0},{16,24},{24,16},{32,40},{40,32},{48,56},{56,48},{64,72... | collective-permute-start | bytes 884744 | tf_op jit(solution)/shard_map/sibling2/ppermute | solution.py:32
  22.6 2.9 %collective-permute-start.3 = (bf16[128,1152]{1,0:T(8,128)(2,1)S(1)}, bf16[128,1152]{1,0:T(8,128)(2,1)S(1)}, u32[]{:S(2)}, u32[]{:S(2)}) collective-permute-start(bf16[128,1152]{1,0:T(8,128)(2,1)S(1)} %collective-permute-done.1.refs_2_), channel_id=1, source_target_pairs={{0,1},{1,2},{2,3},{3,0},{4,5},{5,6},{6,7},{7,4},{8,11},{9,8},{10,9... | collective-permute-start | bytes 884744 | tf_op jit(solution)/shard_map/near2/ppermute | solution.py:56
  25.5 2.0 %collective-permute-start.13 = (bf16[128,1152]{1,0:T(8,128)(2,1)S(1)}, bf16[128,1152]{1,0:T(8,128)(2,1)S(1)}, u32[]{:S(2)}, u32[]{:S(2)}) collective-permute-start(bf16[128,1152]{1,0:T(8,128)(2,1)S(1)} %get-tuple-element.31), channel_id=1, source_target_pairs={{0,8},{8,32},{16,24},{24,48},{32,40},{40,64},{48,56},{56,80},{64,7... | collective-permute-start | bytes 884744 | tf_op jit(solution)/shard_map/extra/ppermute | solution.py:32
  27.5 1.2 %collective-permute-start.6 = (bf16[128,1152]{1,0:T(8,128)(2,1)S(1)}, bf16[128,1152]{1,0:T(8,128)(2,1)S(1)}, u32[]{:S(2)}, u32[]{:S(2)}) collective-permute-start(bf16[128,1152]{1,0:T(8,128)(2,1)S(1)} %collective-permute-done.refs_1_), channel_id=1, source_target_pairs={{0,3},{1,0},{2,1},{3,2},{4,7},{5,4},{6,5},{7,6},{8,9},{9,10},{10,1... | collective-permute-start | bytes 884744 | tf_op jit(solution)/shard_map/far3/ppermute | solution.py:56
  28.7 1.5 %collective-permute-start.5 = (bf16[128,1152]{1,0:T(8,128)(2,1)S(1)}, bf16[128,1152]{1,0:T(8,128)(2,1)S(1)}, u32[]{:S(2)}, u32[]{:S(2)}) collective-permute-start(bf16[128,1152]{1,0:T(8,128)(2,1)S(1)} %collective-permute-done.2.refs_3_), channel_id=1, source_target_pairs={{0,1},{1,2},{2,3},{3,0},{4,5},{5,6},{6,7},{7,4},{8,11},{9,8},{10,9... | collective-permute-start | bytes 884744 | tf_op jit(solution)/shard_map/far2/ppermute | solution.py:56
  30.2 1.4 %collective-permute-done.3.refs_4_ = bf16[128,1152]{1,0:T(8,128)(2,1)S(1)} collective-permute-done((bf16[128,1152]{1,0:T(8,128)(2,1)S(1)}, bf16[128,1152]{1,0:T(8,128)(2,1)S(1)}, u32[]{:S(2)}, u32[]{:S(2)}) %collective-permute-start.3) | collective-permute-done | bytes 294944 | tf_op jit(solution)/shard_map/near2/ppermute | solution.py:56
  31.6 3.6 %collective-permute-start.10 = (bf16[128,1152]{1,0:T(8,128)(2,1)S(1)}, bf16[128,1152]{1,0:T(8,128)(2,1)S(1)}, u32[]{:S(2)}, u32[]{:S(2)}) collective-permute-start(bf16[128,1152]{1,0:T(8,128)(2,1)S(1)} %collective-permute-done.8.refs_9_), channel_id=1, source_target_pairs={{0,8},{8,0},{16,24},{24,16},{32,40},{40,32},{48,56},{56,48},{64,72... | collective-permute-start | bytes 884744 | tf_op jit(solution)/shard_map/sibling1/ppermute | solution.py:32
  35.2 2.1 %collective-permute-start.11 = (bf16[128,1152]{1,0:T(8,128)(2,1)S(1)}, bf16[128,1152]{1,0:T(8,128)(2,1)}, u32[]{:S(2)}, u32[]{:S(2)}) collective-permute-start(bf16[128,1152]{1,0:T(8,128)(2,1)S(1)} %collective-permute-done.9.refs_10_), channel_id=1, source_target_pairs={{0,8},{8,0},{16,24},{24,16},{32,40},{40,32},{48,56},{56,48},{64,72... | collective-permute-start | bytes 884744 | tf_op jit(solution)/shard_map/sibling3/ppermute | solution.py:32
  39.7 15.6 %pairs_part.1 = (f32[32,8,128]{2,1,0:T(8,128)}, f32[128,1152]{1,0:T(8,128)}, f32[128,1152]{1,0:T(8,128)}, bf16[256,1152]{1,0:T(8,128)(2,1)}, bf16[256,1152]{1,0:...) custom-call(f32[1]{0:T(128)S(6)} %copy.7.scale, ...), custom_call_target="tpu_custom_call" | custom-call | flops 1 | bytes 1 | tf_op jit(solution)/shard_map/pairs_part/pallas_call | solution.py:177
  55.3 2.7 %collective-permute-start.18 = (f32[384,1152]{1,0:T(8,128)}, f32[384,1152]{1,0:T(8,128)S(1)}, u32[]{:S(2)}, u32[]{:S(2)}) collective-permute-start(f32[384,1152]{1,0:T(8,128)} %get-tuple-element.26), channel_id=1, source_target_pairs={{0,8},{8,0},{16,24},{24,16},{32,40},{40,32},{48,56},{56,48},{64,72... | collective-permute-start | bytes 5308424 | tf_op jit(solution)/shard_map/back_sib/ppermute | solution.py:32
  58.0 1.1 %collective-permute-start.15 = (bf16[256,1152]{1,0:T(8,128)(2,1)}, bf16[256,1152]{1,0:T(8,128)(2,1)}, u32[]{:S(2)}, u32[]{:S(2)}) collective-permute-start(bf16[256,1152]{1,0:T(8,128)(2,1)} %get-tuple-element.20), channel_id=1, source_target_pairs={{0,2},{1,3},{2,0},{3,1},{4,6},{5,7},{6,4},{7,5},{8,10},{9,11},{10,... | collective-permute-start | bytes 1769480 | tf_op jit(solution)/shard_map/back_x2/ppermute | solution.py:56
  59.2 1.5 %collective-permute-start.16 = (bf16[256,1152]{1,0:T(8,128)(2,1)}, bf16[256,1152]{1,0:T(8,128)(2,1)}, u32[]{:S(2)}, u32[]{:S(2)}) collective-permute-start(bf16[256,1152]{1,0:T(8,128)(2,1)} %get-tuple-element.21), channel_id=1, source_target_pairs={{0,1},{1,2},{2,3},{3,0},{4,5},{5,6},{6,7},{7,4},{8,11},{9,8},{10,9... | collective-permute-start | bytes 1769480 | tf_op jit(solution)/shard_map/back_x3/ppermute | solution.py:56
  61.6 2.3 %fusion = bf16[256,1152]{1,0:T(8,128)(2,1)} fusion(f32[384,1152]{1,0:T(8,128)S(1)} %collective-permute-done.18, f32[384,1152]{1,0:T(8,128)} %get-tuple-element.25), kind=kLoop, calls=%fused_computation.1 | loop fusion | flops 1474560 | bytes 2949120 | tf_op jit(solution)/shard_map/convert_element_type | solution.py:20
  63.8 2.1 %collective-permute-start.20 = (bf16[256,1152]{1,0:T(8,128)(2,1)}, bf16[256,1152]{1,0:T(8,128)(2,1)S(1)}, u32[]{:S(2)}, u32[]{:S(2)}) collective-permute-start(bf16[256,1152]{1,0:T(8,128)(2,1)} %fusion), channel_id=1, source_target_pairs={{0,240},{8,248},{16,0},{24,8},{32,16},{40,24},{48,32},{56,40},{64,... | collective-permute-start | bytes 1769480 | tf_op jit(solution)/shard_map/back13/ppermute | solution.py:32
  65.9 6.4 %all-to-all-start = ((f32[32,8,128]{2,1,0:T(8,128)}), f32[32,8,128]{2,1,0:T(8,128)S(1)}, u32[]{:S(2)}, u32[]{:S(2)}) async-start(f32[32,8,128]{2,1,0:T(8,128)} %get-tuple-element.29), calls=%async_computation | async-start | bytes 262144 | tf_op jit(solution)/shard_map/loss_blk/all_to_all | solution.py:61
  72.5 13.4 %collective-permute-done.14 = bf16[256,1152]{1,0:T(8,128)(2,1)S(1)} collective-permute-done((bf16[256,1152]{1,0:T(8,128)(2,1)}, bf16[256,1152]{1,0:T(8,128)(2,1)S(1)}, u32[]{:S(2)}, u32[]{:S(2)}) %collective-permute-start.14) | collective-permute-done | bytes 589856 | tf_op jit(solution)/shard_map/back_x1/ppermute | solution.py:56
  85.9 1.0 collective-permute-done.16
  86.9 2.4 %fusion.49 = bf16[128,1152]{1,0:T(8,128)(2,1)} fusion(f32[128,1152]{1,0:T(8,128)} %get-tuple-element.22, bf16[256,1152]{1,0:T(8,128)(2,1)} %collective-permute-done.16, bf16[256,1152]{1,0:T(8,128)(2,1)} %collective-permute-done.15, bf16[256,1152]{1,0:T(8,128)(2,1)S(1)} %collective-permute-done.14), kind=kLoop, calls=%fused_computation.76 | loop fusion | flops 3244032 | bytes 1769472 | tf_op jit(solution)/shard_map/convert_element_type | solution.py:20
  89.8 1.4 %fusion.47 = bf16[128,1152]{1,0:T(8,128)(2,1)S(1)} fusion(f32[384,1152]{1,0:T(8,128)S(1)} %collective-permute-done.18, f32[384,1152]{1,0:T(8,128)} %get-tuple-element.25, bf16[128,1152]{1,0:T(8,128)(2,1)S(1)} %collective-permute-done.19, bf16[256,1152]{1,0:T(8,128)(2,1)S(1)} %collective-permute-done.20, pred[]{:T(512)S(6)} %eq.15), kind=kLoop, calls=%fused_computation.73 | loop fusion | flops 2654208 | bytes 2064385 | tf_op jit(solution)/shard_map/convert_element_type | solution.py:20
  91.3 2.3 %collective-permute-start.21 = (bf16[128,1152]{1,0:T(8,128)(2,1)S(1)}, bf16[128,1152]{1,0:T(8,128)(2,1)S(1)}, u32[]{:S(2)}, u32[]{:S(2)}) collective-permute-start(bf16[128,1152]{1,0:T(8,128)(2,1)S(1)} %fusion.47), channel_id=1, source_target_pairs={{0,224},{8,232},{16,240},{24,248},{32,0},{40,8},{48,16},{56,24},{6... | collective-permute-start | bytes 884744 | tf_op jit(solution)/shard_map/back2/ppermute | solution.py:32
  94.2 4.1 %all-to-all-start.1 = ((f32[8,8,128]{2,1,0:T(8,128)}), f32[8,8,128]{2,1,0:T(8,128)S(1)}, u32[]{:S(2)}, u32[]{:S(2)}) async-start(f32[8,8,128]{2,1,0:T(8,128)} %broadcast_in_dim.12), calls=%async_computation.1 | async-start | bytes 65536 | tf_op jit(solution)/shard_map/loss_group/all_to_all | solution.py:61
  98.3 2.7 %fusion.8 = f32[128,1152]{1,0:T(8,128)} fusion(f32[128,1152]{1,0:T(8,128)} %get-tuple-element.18, bf16[128,1152]{1,0:T(8,128)(2,1)} %collective-permute-done.17, bf16[256,1152]{1,0:T(8,128)(2,1)} %collective-permute-done.16, bf16[256,1152]{1,0:T(8,128)(2,1)} %collective-permute-done.15, bf16[256,1152]{1,0:T(8,128)(2,1)S(1)} %collective-permute-done.14), kind=kLoop, calls=%fused_computation.34 | loop fusion | flops 3538944 | bytes 2359296 | tf_op jit(solution)/shard_map/add | solution.py:254
  101.0 2.4 %all-to-all-done.1 = f32[8,8,128]{2,1,0:T(8,128)S(1)} async-done(((f32[8,8,128]{2,1,0:T(8,128)}), f32[8,8,128]{2,1,0:T(8,128)S(1)}, u32[]{:S(2)}, u32[]{:S(2)}) %all-to-all-start.1) | async-done | bytes 32800 | tf_op jit(solution)/shard_map/loss_group/all_to_all | solution.py:61
  104.7 1.2 %fusion.38 = f32[128,1152]{1,0:T(8,128)} fusion(bf16[128,1152]{1,0:T(8,128)(2,1)S(1)} %collective-permute-done.21, f32[128,1152]{1,0:T(8,128)S(1)} %copy-done.1, bf16[128,1152]{1,0:T(8,128)(2,1)S(1)} %collective-permute-done.19, bf16[256,1152]{1,0:T(8,128)(2,1)S(1)} %collective-permute-done.20, pred[]{:T(512)S(6)} %eq.14), kind=kLoop, calls=%fused_computation.64 | loop fusion | flops 2801664 | bytes 2064385 | tf_op jit(solution)/shard_map/add | solution.py:255
  (54 shorter events, 3.8 us)
Async XLA Ops:
  0.6 13.4 %collective-permute-start.7 = (bf16[128,1152]{1,0:T(8,128)(2,1)}, bf16[128,1152]{1,0:T(8,128)(2,1)S(1)}, u32[]{:S(2)}, u32[]{:S(2)}) collective-permute-start(bf16[128,1152]{1,0:T(8,128)(2,1)} %refs_8_.1), channel_id=1, source_target_pairs={{0,32},{8,40},{16,48},{24,56},{32,64},{40,72},{48,80},{56,88},{64,... | collective-permute-start | bytes 884744 | tf_op jit(solution)/shard_map/behind2/ppermute | solution.py:32
  3.2 19.4 %collective-permute-start.1 = (bf16[128,1152]{1,0:T(8,128)(2,1)}, bf16[128,1152]{1,0:T(8,128)(2,1)S(1)}, u32[]{:S(2)}, u32[]{:S(2)}) collective-permute-start(bf16[128,1152]{1,0:T(8,128)(2,1)} %refs_0_.1), channel_id=1, source_target_pairs={{0,1},{1,2},{2,3},{3,0},{4,5},{5,6},{6,7},{7,4},{8,11},{9,8},{10,9... | collective-permute-start | bytes 884744 | tf_op jit(solution)/shard_map/near1/ppermute | solution.py:56
  5.7 13.8 %collective-permute-start = (bf16[128,1152]{1,0:T(8,128)(2,1)}, bf16[128,1152]{1,0:T(8,128)(2,1)S(1)}, u32[]{:S(2)}, u32[]{:S(2)}) collective-permute-start(bf16[128,1152]{1,0:T(8,128)(2,1)} %refs_0_.1), channel_id=1, source_target_pairs={{0,4},{1,5},{2,6},{3,7},{4,0},{5,1},{6,2},{7,3},{8,12},{9,13},{10,... | collective-permute-start | bytes 884744 | tf_op jit(solution)/shard_map/across/ppermute | solution.py:46
  14.1 24.7 %copy-start = (bf16[128,1152]{1,0:T(8,128)(2,1)}, bf16[128,1152]{1,0:T(8,128)(2,1)S(1)}, u32[]{:S(2)}) copy-start(bf16[128,1152]{1,0:T(8,128)(2,1)S(1)} %collective-permute-done.7.refs_11_) | copy-start | bytes 884740
  15.2 10.2 %collective-permute-start.8 = (bf16[128,1152]{1,0:T(8,128)(2,1)S(1)}, bf16[128,1152]{1,0:T(8,128)(2,1)S(1)}, u32[]{:S(2)}, u32[]{:S(2)}) collective-permute-start(bf16[128,1152]{1,0:T(8,128)(2,1)S(1)} %get-tuple-element.32), channel_id=1, source_target_pairs={{0,16},{8,24},{16,0},{24,8},{32,48},{40,56},{48,32},{56,40},{64,80... | collective-permute-start | bytes 884744 | tf_op jit(solution)/shard_map/behind1/ppermute | solution.py:41
  18.2 7.3 %collective-permute-start.4 = (bf16[128,1152]{1,0:T(8,128)(2,1)}, bf16[128,1152]{1,0:T(8,128)(2,1)S(1)}, u32[]{:S(2)}, u32[]{:S(2)}) collective-permute-start(bf16[128,1152]{1,0:T(8,128)(2,1)} %refs_0_.1), channel_id=1, source_target_pairs={{0,3},{1,0},{2,1},{3,2},{4,7},{5,4},{6,5},{7,6},{8,9},{9,10},{10,1... | collective-permute-start | bytes 884744 | tf_op jit(solution)/shard_map/near3/ppermute | solution.py:56
  19.4 19.3 %copy-start.3 = (bf16[128,1152]{1,0:T(8,128)(2,1)}, bf16[128,1152]{1,0:T(8,128)(2,1)S(1)}, u32[]{:S(2)}) copy-start(bf16[128,1152]{1,0:T(8,128)(2,1)S(1)} %collective-permute-done.refs_1_) | copy-start | bytes 884740
  19.4 8.1 %collective-permute-start.2 = (bf16[128,1152]{1,0:T(8,128)(2,1)S(1)}, bf16[128,1152]{1,0:T(8,128)(2,1)S(1)}, u32[]{:S(2)}, u32[]{:S(2)}) collective-permute-start(bf16[128,1152]{1,0:T(8,128)(2,1)S(1)} %collective-permute-done.refs_1_), channel_id=1, source_target_pairs={{0,1},{1,2},{2,3},{3,0},{4,5},{5,6},{6,7},{7,4},{8,11},{9,8},{10,9... | collective-permute-start | bytes 884744 | tf_op jit(solution)/shard_map/far1/ppermute | solution.py:56
  20.9 7.8 %collective-permute-start.12 = (bf16[128,1152]{1,0:T(8,128)(2,1)S(1)}, bf16[128,1152]{1,0:T(8,128)(2,1)S(1)}, u32[]{:S(2)}, u32[]{:S(2)}) collective-permute-start(bf16[128,1152]{1,0:T(8,128)(2,1)S(1)} %collective-permute-done.7.refs_11_), channel_id=1, source_target_pairs={{0,8},{8,0},{16,24},{24,16},{32,40},{40,32},{48,56},{56,48},{64,72... | collective-permute-start | bytes 884744 | tf_op jit(solution)/shard_map/sibling2/ppermute | solution.py:32
  22.6 16.2 %copy-start.2 = (bf16[128,1152]{1,0:T(8,128)(2,1)}, bf16[128,1152]{1,0:T(8,128)(2,1)S(1)}, u32[]{:S(2)}) copy-start(bf16[128,1152]{1,0:T(8,128)(2,1)S(1)} %collective-permute-done.1.refs_2_) | copy-start | bytes 884740
  22.6 9.0 %collective-permute-start.3 = (bf16[128,1152]{1,0:T(8,128)(2,1)S(1)}, bf16[128,1152]{1,0:T(8,128)(2,1)S(1)}, u32[]{:S(2)}, u32[]{:S(2)}) collective-permute-start(bf16[128,1152]{1,0:T(8,128)(2,1)S(1)} %collective-permute-done.1.refs_2_), channel_id=1, source_target_pairs={{0,1},{1,2},{2,3},{3,0},{4,5},{5,6},{6,7},{7,4},{8,11},{9,8},{10,9... | collective-permute-start | bytes 884744 | tf_op jit(solution)/shard_map/near2/ppermute | solution.py:56
  25.4 13.3 %copy-start.4 = (bf16[128,1152]{1,0:T(8,128)(2,1)}, bf16[128,1152]{1,0:T(8,128)(2,1)S(1)}, u32[]{:S(2)}) copy-start(bf16[128,1152]{1,0:T(8,128)(2,1)S(1)} %collective-permute-done.8.refs_9_) | copy-start | bytes 884740
  25.4 9.8 %collective-permute-start.9 = (bf16[128,1152]{1,0:T(8,128)(2,1)S(1)}, bf16[128,1152]{1,0:T(8,128)(2,1)S(1)}, u32[]{:S(2)}, u32[]{:S(2)}) collective-permute-start(bf16[128,1152]{1,0:T(8,128)(2,1)S(1)} %collective-permute-done.8.refs_9_), channel_id=1, source_target_pairs={{0,32},{8,40},{16,48},{24,56},{32,64},{40,72},{48,80},{56,88},{64,... | collective-permute-start | bytes 884744 | tf_op jit(solution)/shard_map/behind3/ppermute | solution.py:32
  25.5 13.3 %copy-start.5 = (bf16[128,1152]{1,0:T(8,128)(2,1)}, bf16[128,1152]{1,0:T(8,128)(2,1)S(1)}, u32[]{:S(2)}) copy-start(bf16[128,1152]{1,0:T(8,128)(2,1)S(1)} %collective-permute-done.4.refs_6_) | copy-start | bytes 884740
  25.5 13.2 %collective-permute-start.13 = (bf16[128,1152]{1,0:T(8,128)(2,1)S(1)}, bf16[128,1152]{1,0:T(8,128)(2,1)S(1)}, u32[]{:S(2)}, u32[]{:S(2)}) collective-permute-start(bf16[128,1152]{1,0:T(8,128)(2,1)S(1)} %get-tuple-element.31), channel_id=1, source_target_pairs={{0,8},{8,32},{16,24},{24,48},{32,40},{40,64},{48,56},{56,80},{64,7... | collective-permute-start | bytes 884744 | tf_op jit(solution)/shard_map/extra/ppermute | solution.py:32
  27.5 11.3 %copy-start.6 = (bf16[128,1152]{1,0:T(8,128)(2,1)}, bf16[128,1152]{1,0:T(8,128)(2,1)S(1)}, u32[]{:S(2)}) copy-start(bf16[128,1152]{1,0:T(8,128)(2,1)S(1)} %collective-permute-done.2.refs_3_) | copy-start | bytes 884740
  27.5 11.1 %collective-permute-start.6 = (bf16[128,1152]{1,0:T(8,128)(2,1)S(1)}, bf16[128,1152]{1,0:T(8,128)(2,1)S(1)}, u32[]{:S(2)}, u32[]{:S(2)}) collective-permute-start(bf16[128,1152]{1,0:T(8,128)(2,1)S(1)} %collective-permute-done.refs_1_), channel_id=1, source_target_pairs={{0,3},{1,0},{2,1},{3,2},{4,7},{5,4},{6,5},{7,6},{8,9},{9,10},{10,1... | collective-permute-start | bytes 884744 | tf_op jit(solution)/shard_map/far3/ppermute | solution.py:56
  28.7 10.1 %copy-start.7 = (bf16[128,1152]{1,0:T(8,128)(2,1)}, bf16[128,1152]{1,0:T(8,128)(2,1)S(1)}, u32[]{:S(2)}) copy-start(bf16[128,1152]{1,0:T(8,128)(2,1)S(1)} %collective-permute-done.12.refs_14_) | copy-start | bytes 884740
  28.7 10.0 %collective-permute-start.5 = (bf16[128,1152]{1,0:T(8,128)(2,1)S(1)}, bf16[128,1152]{1,0:T(8,128)(2,1)S(1)}, u32[]{:S(2)}, u32[]{:S(2)}) collective-permute-start(bf16[128,1152]{1,0:T(8,128)(2,1)S(1)} %collective-permute-done.2.refs_3_), channel_id=1, source_target_pairs={{0,1},{1,2},{2,3},{3,0},{4,5},{5,6},{6,7},{7,4},{8,11},{9,8},{10,9... | collective-permute-start | bytes 884744 | tf_op jit(solution)/shard_map/far2/ppermute | solution.py:56
  31.6 7.1 %collective-permute-start.10 = (bf16[128,1152]{1,0:T(8,128)(2,1)S(1)}, bf16[128,1152]{1,0:T(8,128)(2,1)S(1)}, u32[]{:S(2)}, u32[]{:S(2)}) collective-permute-start(bf16[128,1152]{1,0:T(8,128)(2,1)S(1)} %collective-permute-done.8.refs_9_), channel_id=1, source_target_pairs={{0,8},{8,0},{16,24},{24,16},{32,40},{40,32},{48,56},{56,48},{64,72... | collective-permute-start | bytes 884744 | tf_op jit(solution)/shard_map/sibling1/ppermute | solution.py:32
  35.2 3.5 %collective-permute-start.11 = (bf16[128,1152]{1,0:T(8,128)(2,1)S(1)}, bf16[128,1152]{1,0:T(8,128)(2,1)}, u32[]{:S(2)}, u32[]{:S(2)}) collective-permute-start(bf16[128,1152]{1,0:T(8,128)(2,1)S(1)} %collective-permute-done.9.refs_10_), channel_id=1, source_target_pairs={{0,8},{8,0},{16,24},{24,16},{32,40},{40,32},{48,56},{56,48},{64,72... | collective-permute-start | bytes 884744 | tf_op jit(solution)/shard_map/sibling3/ppermute | solution.py:32
  55.3 6.3 %collective-permute-start.18 = (f32[384,1152]{1,0:T(8,128)}, f32[384,1152]{1,0:T(8,128)S(1)}, u32[]{:S(2)}, u32[]{:S(2)}) collective-permute-start(f32[384,1152]{1,0:T(8,128)} %get-tuple-element.26), channel_id=1, source_target_pairs={{0,8},{8,0},{16,24},{24,16},{32,40},{40,32},{48,56},{56,48},{64,72... | collective-permute-start | bytes 5308424 | tf_op jit(solution)/shard_map/back_sib/ppermute | solution.py:32
  58.0 27.9 %collective-permute-start.14 = (bf16[256,1152]{1,0:T(8,128)(2,1)}, bf16[256,1152]{1,0:T(8,128)(2,1)S(1)}, u32[]{:S(2)}, u32[]{:S(2)}) collective-permute-start(bf16[256,1152]{1,0:T(8,128)(2,1)} %get-tuple-element.19), channel_id=1, source_target_pairs={{0,3},{1,0},{2,1},{3,2},{4,7},{5,4},{6,5},{7,6},{8,9},{9,10},{10,1... | collective-permute-start | bytes 1769480 | tf_op jit(solution)/shard_map/back_x1/ppermute | solution.py:56
  58.0 27.9 %collective-permute-start.15 = (bf16[256,1152]{1,0:T(8,128)(2,1)}, bf16[256,1152]{1,0:T(8,128)(2,1)}, u32[]{:S(2)}, u32[]{:S(2)}) collective-permute-start(bf16[256,1152]{1,0:T(8,128)(2,1)} %get-tuple-element.20), channel_id=1, source_target_pairs={{0,2},{1,3},{2,0},{3,1},{4,6},{5,7},{6,4},{7,5},{8,10},{9,11},{10,... | collective-permute-start | bytes 1769480 | tf_op jit(solution)/shard_map/back_x2/ppermute | solution.py:56
  59.2 27.8 %collective-permute-start.16 = (bf16[256,1152]{1,0:T(8,128)(2,1)}, bf16[256,1152]{1,0:T(8,128)(2,1)}, u32[]{:S(2)}, u32[]{:S(2)}) collective-permute-start(bf16[256,1152]{1,0:T(8,128)(2,1)} %get-tuple-element.21), channel_id=1, source_target_pairs={{0,1},{1,2},{2,3},{3,0},{4,5},{5,6},{6,7},{7,4},{8,11},{9,8},{10,9... | collective-permute-start | bytes 1769480 | tf_op jit(solution)/shard_map/back_x3/ppermute | solution.py:56
  63.8 26.0 %collective-permute-start.20 = (bf16[256,1152]{1,0:T(8,128)(2,1)}, bf16[256,1152]{1,0:T(8,128)(2,1)S(1)}, u32[]{:S(2)}, u32[]{:S(2)}) collective-permute-start(bf16[256,1152]{1,0:T(8,128)(2,1)} %fusion), channel_id=1, source_target_pairs={{0,240},{8,248},{16,0},{24,8},{32,16},{40,24},{48,32},{56,40},{64,... | collective-permute-start | bytes 1769480 | tf_op jit(solution)/shard_map/back13/ppermute | solution.py:32
  65.9 23.9 %all-to-all-start = ((f32[32,8,128]{2,1,0:T(8,128)}), f32[32,8,128]{2,1,0:T(8,128)S(1)}, u32[]{:S(2)}, u32[]{:S(2)}) async-start(f32[32,8,128]{2,1,0:T(8,128)} %get-tuple-element.29), calls=%async_computation | async-start | bytes 262144 | tf_op jit(solution)/shard_map/loss_blk/all_to_all | solution.py:61
  72.2 17.6 %collective-permute-start.19 = (bf16[128,1152]{1,0:T(8,128)(2,1)}, bf16[128,1152]{1,0:T(8,128)(2,1)S(1)}, u32[]{:S(2)}, u32[]{:S(2)}) collective-permute-start(bf16[128,1152]{1,0:T(8,128)(2,1)} %get-tuple-element.27), channel_id=1, source_target_pairs={{0,232},{8,0},{16,248},{24,16},{32,8},{40,32},{48,24},{56,48},{64,... | collective-permute-start | bytes 884744 | tf_op jit(solution)/shard_map/back_extra/ppermute | solution.py:32
  89.3 9.0 %collective-permute-start.17 = (bf16[128,1152]{1,0:T(8,128)(2,1)}, bf16[128,1152]{1,0:T(8,128)(2,1)}, u32[]{:S(2)}, u32[]{:S(2)}) collective-permute-start(bf16[128,1152]{1,0:T(8,128)(2,1)} %fusion.49), channel_id=1, source_target_pairs={{0,4},{1,5},{2,6},{3,7},{4,0},{5,1},{6,2},{7,3},{8,12},{9,13},{10,... | collective-permute-start | bytes 884744 | tf_op jit(solution)/shard_map/back_across/ppermute | solution.py:46
  91.3 13.4 %copy-start.1 = (f32[128,1152]{1,0:T(8,128)S(1)}, f32[128,1152]{1,0:T(8,128)}, u32[]{:S(2)}) copy-start(f32[128,1152]{1,0:T(8,128)} %get-tuple-element.23) | copy-start | bytes 1769476
  91.3 13.4 %collective-permute-start.21 = (bf16[128,1152]{1,0:T(8,128)(2,1)S(1)}, bf16[128,1152]{1,0:T(8,128)(2,1)S(1)}, u32[]{:S(2)}, u32[]{:S(2)}) collective-permute-start(bf16[128,1152]{1,0:T(8,128)(2,1)S(1)} %fusion.47), channel_id=1, source_target_pairs={{0,224},{8,232},{16,240},{24,248},{32,0},{40,8},{48,16},{56,24},{6... | collective-permute-start | bytes 884744 | tf_op jit(solution)/shard_map/back2/ppermute | solution.py:32
  94.2 9.3 %all-to-all-start.1 = ((f32[8,8,128]{2,1,0:T(8,128)}), f32[8,8,128]{2,1,0:T(8,128)S(1)}, u32[]{:S(2)}, u32[]{:S(2)}) async-start(f32[8,8,128]{2,1,0:T(8,128)} %broadcast_in_dim.12), calls=%async_computation.1 | async-start | bytes 65536 | tf_op jit(solution)/shard_map/loss_group/all_to_all | solution.py:61
  (6 other events, 14.3 us)

commit v5 on v4

--- a/solution.py
+++ b/solution.py
@@ -126,12 +126,12 @@
                 logits = jnp.where(positive, -logits, logits)
             small = jnp.exp(-jnp.abs(logits))
             log1p = jnp.log(1.0 + small)
-            part = jnp.exp(jnp.minimum(logits, 0.0) - log1p) * weight
+            exact = jnp.where(small < 2.0**-9, small * (1.0 - 0.5 * small), log1p)
+            terms = jnp.maximum(logits, 0.0) + exact
+            part = jnp.exp(logits - terms) * weight
             if mixed:
                 part = jnp.where(positive, -part, part)
             coef[place, jt * TILE : (jt + 1) * TILE] = part.astype(jnp.bfloat16)
-            exact = jnp.where(small < 2.0**-9, small * (1.0 - 0.5 * small), log1p)
-            terms = jnp.maximum(logits, 0.0) + exact
             loss_acc[...] += jnp.sum(terms.reshape(TILE // 8, 8, TILE), axis=0)
         product = jnp.dot(coef[place, :], texts[...], preferred_element_type=jnp.float32)
         parts = [pl.ds(it * TILE + i * rows, rows) for i in range(2)]
@@ -216,9 +216,10 @@
     near = [images]
     far = [across]
     for name, group in (("near", near), ("far", far)):
-        one = ring_x(group[0], 1, f"{name}1")
-        three = ring_x(group[0], 3, f"{name}3")
-        two = ring_x(one if name == "near" else after(one, near[3]), 1, f"{name}2")
+        start = group[0] if name == "near" else after(group[0], near[1], near[3])
+        one = ring_x(start, 1, f"{name}1")
+        three = ring_x(start, 3, f"{name}3")
+        two = ring_x(after(one, three if name == "near" else near[3]), 1, f"{name}2")
         group += [one, two, three]
     extra = shift_blk(jnp.where(core == 0, texts, behind2), 1, 3, "extra")
     behind3 = shift_blk(behind1, 4, 4, "behind3")

time: 107 us -> 105 us (0.981); the launches traced: 107 us -> 104 us
  waiting for transfers between devices: 26.3 us -> 24.3 us
  starting transfers between devices: 47.9 us -> 46.8 us
    ppermute x9, waiting for transfers between devices: 15.9 us -> 12.1 us  [ring_x(): return lax.ppermute(value, ('blk', 'group'), pairs)]
    ppermute x10, starting transfers between devices: 19.3 us -> 15.6 us  [shift_blk(): return lax.ppermute(value, 'blk', pairs)]
    ppermute x9, starting transfers between devices: 13.4 us -> 15.6 us  [ring_x(): return lax.ppermute(value, ('blk', 'group'), pairs)]
    ppermute x1, waiting for transfers between devices: 0.01 us -> 1.53 us  [flip_y(): lax.ppermute(value, 'blk', [(s, s ^ 2) for s in range(lax.axis_size('blk'...]
    ppermute x2, starting transfers between devices: 1.7 us -> 2.99 us  [swap_y(): return lax.ppermute(value, 'group', [(s, (s + 4) % 8) for s in range(8)])]
  transfers between devices with their start and end apart: 24 -> 24, of which waited for: 6 -> 7; matrix products, arithmetic and copies ran while one was open for 10% -> 11% of each run, Pallas kernels for 0% -> 0%
where the time goes in v5:
time: 105 us; the launch traced here: 104 us
  starting transfers between devices  46.8 us (45%)
  waiting for transfers between devices  24.3 us (23%)
  Pallas kernels  15.5 us (15%)
  other arithmetic  11.8 us (11%)
  between operations  3.97 us (4%)
  local copies, waits for them, and re-layouts  1.53 us (1%)
    ppermute x9, starting transfers between devices, ring_x(): return lax.ppermute(value, ('blk', 'group'), pairs)  15.6 us
    ppermute x10, starting transfers between devices, shift_blk(): return lax.ppermute(value, 'blk', pairs)  15.6 us
    pallas_call x1, Pallas kernels, pairs_part(): pl.pallas_call(pairs_kernel, out_shape=[jax.ShapeDtypeStruct((lax.axis_si...  15.5 us
    ppermute x9, waiting for transfers between devices, ring_x(): return lax.ppermute(value, ('blk', 'group'), pairs)  12.1 us
    all_to_all x2, starting transfers between devices, sum_over(): return jnp.sum(lax.all_to_all(value, axis, 0, 0), axis=0)  9.67 us
    ppermute x10, waiting for transfers between devices, shift_blk(): return lax.ppermute(value, 'blk', pairs)  8.27 us
    convert_element_type x3, other arithmetic, encode(): return (scaled * jnp.abs(scaled)).astype(jnp.bfloat16)  6.14 us
    ppermute x1, starting transfers between devices, flip_y(): lax.ppermute(value, 'blk', [(s, s ^ 2) for s in range(lax.axis_size('blk'...  3 us
  transfers between devices with their start and end apart: 24, of which 7 were waited for; matrix products, arithmetic and copies ran while one was open for 11% of the time, Pallas kernels for 0%

profile of v5, /device:TPU:1, one launch (start us, length us, event | category | flops | bytes accessed | tf_op | source)
XLA Modules:
  0.0 103.9 jit_solution(3505063184819981391)
XLA Ops:
  0.6 2.5 %collective-permute-start.7 = (bf16[128,1152]{1,0:T(8,128)(2,1)}, bf16[128,1152]{1,0:T(8,128)(2,1)S(1)}, u32[]{:S(2)}, u32[]{:S(2)}) collective-permute-start(bf16[128,1152]{1,0:T(8,128)(2,1)} %refs_8_.1), channel_id=1, source_target_pairs={{0,32},{8,40},{16,48},{24,56},{32,64},{40,72},{48,80},{56,88},{64,... | collective-permute-start | bytes 884744 | tf_op jit(solution)/shard_map/behind2/ppermute | solution.py:32
  3.2 2.5 %collective-permute-start.1 = (bf16[128,1152]{1,0:T(8,128)(2,1)}, bf16[128,1152]{1,0:T(8,128)(2,1)S(1)}, u32[]{:S(2)}, u32[]{:S(2)}) collective-permute-start(bf16[128,1152]{1,0:T(8,128)(2,1)} %refs_0_.1), channel_id=1, source_target_pairs={{0,1},{1,2},{2,3},{3,0},{4,5},{5,6},{6,7},{7,4},{8,11},{9,8},{10,9... | collective-permute-start | bytes 884744 | tf_op jit(solution)/shard_map/near1/ppermute | solution.py:56
  5.7 1.3 %collective-permute-start = (bf16[128,1152]{1,0:T(8,128)(2,1)}, bf16[128,1152]{1,0:T(8,128)(2,1)S(1)}, u32[]{:S(2)}, u32[]{:S(2)}) collective-permute-start(bf16[128,1152]{1,0:T(8,128)(2,1)} %refs_0_.1), channel_id=1, source_target_pairs={{0,4},{1,5},{2,6},{3,7},{4,0},{5,1},{6,2},{7,3},{8,12},{9,13},{10,... | collective-permute-start | bytes 884744 | tf_op jit(solution)/shard_map/across/ppermute | solution.py:46
  7.0 7.1 %collective-permute-done.7.refs_11_ = bf16[128,1152]{1,0:T(8,128)(2,1)S(1)} collective-permute-done((bf16[128,1152]{1,0:T(8,128)(2,1)}, bf16[128,1152]{1,0:T(8,128)(2,1)S(1)}, u32[]{:S(2)}, u32[]{:S(2)}) %collective-permute-start.7) | collective-permute-done | bytes 294944 | tf_op jit(solution)/shard_map/behind2/ppermute | solution.py:32
  14.1 1.1 %broadcast_select_fusion = (bf16[128,1152]{1,0:T(8,128)(2,1)S(1)}, bf16[128,1152]{1,0:T(8,128)(2,1)S(1)}) fusion(bf16[128,1152]{1,0:T(8,128)(2,1)} %refs_8_.1, bf16[128,1152]{1,0:T(8,128)(2,1)S(1)} %collective-permute-done.7.refs_11_, pred[]{:T(512)S(6)} %eq.14, pred[]{:T(512)S(6)} %eq.13), kind=kLoop, calls=%fused_computation.77 | loop fusion | flops 294912 | bytes 1179650 | tf_op jit(solution)/shard_map/jit(_where)/select_n | solution.py:224
  15.2 3.0 %collective-permute-start.8 = (bf16[128,1152]{1,0:T(8,128)(2,1)S(1)}, bf16[128,1152]{1,0:T(8,128)(2,1)S(1)}, u32[]{:S(2)}, u32[]{:S(2)}) collective-permute-start(bf16[128,1152]{1,0:T(8,128)(2,1)S(1)} %get-tuple-element.36), channel_id=1, source_target_pairs={{0,16},{8,24},{16,0},{24,8},{32,48},{40,56},{48,32},{56,40},{64,80... | collective-permute-start | bytes 884744 | tf_op jit(solution)/shard_map/behind1/ppermute | solution.py:41
  18.2 2.6 %collective-permute-start.3 = (bf16[128,1152]{1,0:T(8,128)(2,1)S(1)}, bf16[128,1152]{1,0:T(8,128)(2,1)S(1)}, u32[]{:S(2)}, u32[]{:S(2)}) collective-permute-start(bf16[128,1152]{1,0:T(8,128)(2,1)S(1)} %collective-permute-done.refs_1_), channel_id=1, source_target_pairs={{0,1},{1,2},{2,3},{3,0},{4,5},{5,6},{6,7},{7,4},{8,11},{9,8},{10,9... | collective-permute-start | bytes 884744 | tf_op jit(solution)/shard_map/far1/ppermute | solution.py:56
  21.3 1.2 %collective-permute-start.6 = (bf16[128,1152]{1,0:T(8,128)(2,1)S(1)}, bf16[128,1152]{1,0:T(8,128)(2,1)S(1)}, u32[]{:S(2)}, u32[]{:S(2)}) collective-permute-start(bf16[128,1152]{1,0:T(8,128)(2,1)S(1)} %collective-permute-done.refs_1_), channel_id=1, source_target_pairs={{0,3},{1,0},{2,1},{3,2},{4,7},{5,4},{6,5},{7,6},{8,9},{9,10},{10,1... | collective-permute-start | bytes 884744 | tf_op jit(solution)/shard_map/far3/ppermute | solution.py:56
  22.5 1.5 %collective-permute-done.8.refs_9_ = bf16[128,1152]{1,0:T(8,128)(2,1)S(1)} collective-permute-done((bf16[128,1152]{1,0:T(8,128)(2,1)S(1)}, bf16[128,1152]{1,0:T(8,128)(2,1)S(1)}, u32[]{:S(2)}, u32[]{:S(2)}) %collective-permute-start.8) | collective-permute-done | bytes 294944 | tf_op jit(solution)/shard_map/behind1/ppermute | solution.py:41
  25.0 1.6 %collective-permute-start.4 = (bf16[128,1152]{1,0:T(8,128)(2,1)S(1)}, bf16[128,1152]{1,0:T(8,128)(2,1)S(1)}, u32[]{:S(2)}, u32[]{:S(2)}) collective-permute-start(bf16[128,1152]{1,0:T(8,128)(2,1)S(1)} %collective-permute-done.1.refs_2_), channel_id=1, source_target_pairs={{0,1},{1,2},{2,3},{3,0},{4,5},{5,6},{6,7},{7,4},{8,11},{9,8},{10,9... | collective-permute-start | bytes 884744 | tf_op jit(solution)/shard_map/near2/ppermute | solution.py:56
  27.5 2.9 %collective-permute-start.5 = (bf16[128,1152]{1,0:T(8,128)(2,1)S(1)}, bf16[128,1152]{1,0:T(8,128)(2,1)S(1)}, u32[]{:S(2)}, u32[]{:S(2)}) collective-permute-start(bf16[128,1152]{1,0:T(8,128)(2,1)S(1)} %collective-permute-done.3.refs_3_), channel_id=1, source_target_pairs={{0,1},{1,2},{2,3},{3,0},{4,5},{5,6},{6,7},{7,4},{8,11},{9,8},{10,9... | collective-permute-start | bytes 884744 | tf_op jit(solution)/shard_map/far2/ppermute | solution.py:56
  30.5 1.1 %collective-permute-done.9.refs_10_ = bf16[128,1152]{1,0:T(8,128)(2,1)S(1)} collective-permute-done((bf16[128,1152]{1,0:T(8,128)(2,1)S(1)}, bf16[128,1152]{1,0:T(8,128)(2,1)S(1)}, u32[]{:S(2)}, u32[]{:S(2)}) %collective-permute-start.9) | collective-permute-done | bytes 294944 | tf_op jit(solution)/shard_map/behind3/ppermute | solution.py:32
  31.6 3.6 %collective-permute-start.11 = (bf16[128,1152]{1,0:T(8,128)(2,1)S(1)}, bf16[128,1152]{1,0:T(8,128)(2,1)}, u32[]{:S(2)}, u32[]{:S(2)}) collective-permute-start(bf16[128,1152]{1,0:T(8,128)(2,1)S(1)} %collective-permute-done.9.refs_10_), channel_id=1, source_target_pairs={{0,8},{8,0},{16,24},{24,16},{32,40},{40,32},{48,56},{56,48},{64,72... | collective-permute-start | bytes 884744 | tf_op jit(solution)/shard_map/sibling3/ppermute | solution.py:32
  37.6 15.5 %pairs_part.1 = (f32[32,8,128]{2,1,0:T(8,128)}, f32[128,1152]{1,0:T(8,128)}, f32[128,1152]{1,0:T(8,128)}, bf16[256,1152]{1,0:T(8,128)(2,1)}, bf16[256,1152]{1,0:...) custom-call(f32[1]{0:T(128)S(6)} %copy.7.scale, ...), custom_call_target="tpu_custom_call" | custom-call | flops 1 | bytes 1 | tf_op jit(solution)/shard_map/pairs_part/pallas_call | solution.py:177
  53.1 1.3 %collective-permute-start.18 = (f32[384,1152]{1,0:T(8,128)}, f32[384,1152]{1,0:T(8,128)S(1)}, u32[]{:S(2)}, u32[]{:S(2)}) collective-permute-start(f32[384,1152]{1,0:T(8,128)} %get-tuple-element.30), channel_id=1, source_target_pairs={{0,8},{8,0},{16,24},{24,16},{32,40},{40,32},{48,56},{56,48},{64,72... | collective-permute-start | bytes 5308424 | tf_op jit(solution)/shard_map/back_sib/ppermute | solution.py:32
  54.3 1.3 %collective-permute-start.14 = (bf16[256,1152]{1,0:T(8,128)(2,1)}, bf16[256,1152]{1,0:T(8,128)(2,1)S(1)}, u32[]{:S(2)}, u32[]{:S(2)}) collective-permute-start(bf16[256,1152]{1,0:T(8,128)(2,1)} %get-tuple-element.23), channel_id=1, source_target_pairs={{0,3},{1,0},{2,1},{3,2},{4,7},{5,4},{6,5},{7,6},{8,9},{9,10},{10,1... | collective-permute-start | bytes 1769480 | tf_op jit(solution)/shard_map/back_x1/ppermute | solution.py:56
  55.7 2.3 %collective-permute-start.15 = (bf16[256,1152]{1,0:T(8,128)(2,1)}, bf16[256,1152]{1,0:T(8,128)(2,1)}, u32[]{:S(2)}, u32[]{:S(2)}) collective-permute-start(bf16[256,1152]{1,0:T(8,128)(2,1)} %get-tuple-element.24), channel_id=1, source_target_pairs={{0,2},{1,3},{2,0},{3,1},{4,6},{5,7},{6,4},{7,5},{8,10},{9,11},{10,... | collective-permute-start | bytes 1769480 | tf_op jit(solution)/shard_map/back_x2/ppermute | solution.py:56
  58.0 1.2 %collective-permute-start.16 = (bf16[256,1152]{1,0:T(8,128)(2,1)}, bf16[256,1152]{1,0:T(8,128)(2,1)}, u32[]{:S(2)}, u32[]{:S(2)}) collective-permute-start(bf16[256,1152]{1,0:T(8,128)(2,1)} %get-tuple-element.25), channel_id=1, source_target_pairs={{0,1},{1,2},{2,3},{3,0},{4,5},{5,6},{6,7},{7,4},{8,11},{9,8},{10,9... | collective-permute-start | bytes 1769480 | tf_op jit(solution)/shard_map/back_x3/ppermute | solution.py:56
  59.2 2.3 %fusion = bf16[256,1152]{1,0:T(8,128)(2,1)} fusion(f32[384,1152]{1,0:T(8,128)S(1)} %collective-permute-done.18, f32[384,1152]{1,0:T(8,128)} %get-tuple-element.29), kind=kLoop, calls=%fused_computation.1 | loop fusion | flops 1474560 | bytes 2949120 | tf_op jit(solution)/shard_map/convert_element_type | solution.py:20
  61.4 3.7 %collective-permute-start.20 = (bf16[256,1152]{1,0:T(8,128)(2,1)}, bf16[256,1152]{1,0:T(8,128)(2,1)S(1)}, u32[]{:S(2)}, u32[]{:S(2)}) collective-permute-start(bf16[256,1152]{1,0:T(8,128)(2,1)} %fusion), channel_id=1, source_target_pairs={{0,240},{8,248},{16,0},{24,8},{32,16},{40,24},{48,32},{56,40},{64,... | collective-permute-start | bytes 1769480 | tf_op jit(solution)/shard_map/back13/ppermute | solution.py:32
  65.1 6.0 %all-to-all-start = ((f32[32,8,128]{2,1,0:T(8,128)}), f32[32,8,128]{2,1,0:T(8,128)S(1)}, u32[]{:S(2)}, u32[]{:S(2)}) async-start(f32[32,8,128]{2,1,0:T(8,128)} %get-tuple-element.33), calls=%async_computation | async-start | bytes 262144 | tf_op jit(solution)/shard_map/loss_blk/all_to_all | solution.py:61
  71.4 5.8 %collective-permute-done.14 = bf16[256,1152]{1,0:T(8,128)(2,1)S(1)} collective-permute-done((bf16[256,1152]{1,0:T(8,128)(2,1)}, bf16[256,1152]{1,0:T(8,128)(2,1)S(1)}, u32[]{:S(2)}, u32[]{:S(2)}) %collective-permute-start.14) | collective-permute-done | bytes 589856 | tf_op jit(solution)/shard_map/back_x1/ppermute | solution.py:56
  77.1 4.8 %collective-permute-done.15 = bf16[256,1152]{1,0:T(8,128)(2,1)} collective-permute-done((bf16[256,1152]{1,0:T(8,128)(2,1)}, bf16[256,1152]{1,0:T(8,128)(2,1)}, u32[]{:S(2)}, u32[]{:S(2)}) %collective-permute-start.15) | collective-permute-done | bytes 589856 | tf_op jit(solution)/shard_map/back_x2/ppermute | solution.py:56
  81.9 1.6 %collective-permute-done.16 = bf16[256,1152]{1,0:T(8,128)(2,1)} collective-permute-done((bf16[256,1152]{1,0:T(8,128)(2,1)}, bf16[256,1152]{1,0:T(8,128)(2,1)}, u32[]{:S(2)}, u32[]{:S(2)}) %collective-permute-start.16) | collective-permute-done | bytes 589856 | tf_op jit(solution)/shard_map/back_x3/ppermute | solution.py:56
  83.4 2.4 %fusion.49 = bf16[128,1152]{1,0:T(8,128)(2,1)} fusion(f32[128,1152]{1,0:T(8,128)} %get-tuple-element.26, bf16[256,1152]{1,0:T(8,128)(2,1)} %collective-permute-done.16, bf16[256,1152]{1,0:T(8,128)(2,1)} %collective-permute-done.15, bf16[256,1152]{1,0:T(8,128)(2,1)S(1)} %collective-permute-done.14), kind=kLoop, calls=%fused_computation.76 | loop fusion | flops 3244032 | bytes 1769472 | tf_op jit(solution)/shard_map/convert_element_type | solution.py:20
  85.9 1.7 %collective-permute-start.17 = (bf16[128,1152]{1,0:T(8,128)(2,1)}, bf16[128,1152]{1,0:T(8,128)(2,1)}, u32[]{:S(2)}, u32[]{:S(2)}) collective-permute-start(bf16[128,1152]{1,0:T(8,128)(2,1)} %fusion.49), channel_id=1, source_target_pairs={{0,4},{1,5},{2,6},{3,7},{4,0},{5,1},{6,2},{7,3},{8,12},{9,13},{10,... | collective-permute-start | bytes 884744 | tf_op jit(solution)/shard_map/back_across/ppermute | solution.py:46
  87.6 1.4 %fusion.47 = bf16[128,1152]{1,0:T(8,128)(2,1)S(1)} fusion(f32[384,1152]{1,0:T(8,128)S(1)} %collective-permute-done.18, f32[384,1152]{1,0:T(8,128)} %get-tuple-element.29, bf16[128,1152]{1,0:T(8,128)(2,1)S(1)} %collective-permute-done.19, bf16[256,1152]{1,0:T(8,128)(2,1)S(1)} %collective-permute-done.20, pred[]{:T(512)S(6)} %eq.15), kind=kLoop, calls=%fused_computation.73 | loop fusion | flops 2654208 | bytes 2064385 | tf_op jit(solution)/shard_map/convert_element_type | solution.py:20
  89.1 1.8 %collective-permute-start.21 = (bf16[128,1152]{1,0:T(8,128)(2,1)S(1)}, bf16[128,1152]{1,0:T(8,128)(2,1)S(1)}, u32[]{:S(2)}, u32[]{:S(2)}) collective-permute-start(bf16[128,1152]{1,0:T(8,128)(2,1)S(1)} %fusion.47), channel_id=1, source_target_pairs={{0,224},{8,232},{16,240},{24,248},{32,0},{40,8},{48,16},{56,24},{6... | collective-permute-start | bytes 884744 | tf_op jit(solution)/shard_map/back2/ppermute | solution.py:32
  91.5 3.7 %all-to-all-start.1 = ((f32[8,8,128]{2,1,0:T(8,128)}), f32[8,8,128]{2,1,0:T(8,128)S(1)}, u32[]{:S(2)}, u32[]{:S(2)}) async-start(f32[8,8,128]{2,1,0:T(8,128)} %broadcast_in_dim.12), calls=%async_computation.1 | async-start | bytes 65536 | tf_op jit(solution)/shard_map/loss_group/all_to_all | solution.py:61
  95.2 2.7 %fusion.8 = f32[128,1152]{1,0:T(8,128)} fusion(f32[128,1152]{1,0:T(8,128)} %get-tuple-element.22, bf16[128,1152]{1,0:T(8,128)(2,1)} %collective-permute-done.17, bf16[256,1152]{1,0:T(8,128)(2,1)} %collective-permute-done.16, bf16[256,1152]{1,0:T(8,128)(2,1)} %collective-permute-done.15, bf16[256,1152]{1,0:T(8,128)(2,1)S(1)} %collective-permute-done.14), kind=kLoop, calls=%fused_computation.34 | loop fusion | flops 3538944 | bytes 2359296 | tf_op jit(solution)/shard_map/add | solution.py:255
  97.9 2.4 %all-to-all-done.1 = f32[8,8,128]{2,1,0:T(8,128)S(1)} async-done(((f32[8,8,128]{2,1,0:T(8,128)}), f32[8,8,128]{2,1,0:T(8,128)S(1)}, u32[]{:S(2)}, u32[]{:S(2)}) %all-to-all-start.1) | async-done | bytes 32800 | tf_op jit(solution)/shard_map/loss_group/all_to_all | solution.py:61
  101.6 1.2 %fusion.38 = f32[128,1152]{1,0:T(8,128)} fusion(bf16[128,1152]{1,0:T(8,128)(2,1)S(1)} %collective-permute-done.21, f32[128,1152]{1,0:T(8,128)S(1)} %copy-done.1, bf16[128,1152]{1,0:T(8,128)(2,1)S(1)} %collective-permute-done.19, bf16[256,1152]{1,0:T(8,128)(2,1)S(1)} %collective-permute-done.20, pred[]{:T(512)S(6)} %eq.14), kind=kLoop, calls=%fused_computation.64 | loop fusion | flops 2801664 | bytes 2064385 | tf_op jit(solution)/shard_map/add | solution.py:256
  (54 shorter events, 4.9 us)
Async XLA Ops:
  0.6 13.4 %collective-permute-start.7 = (bf16[128,1152]{1,0:T(8,128)(2,1)}, bf16[128,1152]{1,0:T(8,128)(2,1)S(1)}, u32[]{:S(2)}, u32[]{:S(2)}) collective-permute-start(bf16[128,1152]{1,0:T(8,128)(2,1)} %refs_8_.1), channel_id=1, source_target_pairs={{0,32},{8,40},{16,48},{24,56},{32,64},{40,72},{48,80},{56,88},{64,... | collective-permute-start | bytes 884744 | tf_op jit(solution)/shard_map/behind2/ppermute | solution.py:32
  3.2 15.0 %collective-permute-start.1 = (bf16[128,1152]{1,0:T(8,128)(2,1)}, bf16[128,1152]{1,0:T(8,128)(2,1)S(1)}, u32[]{:S(2)}, u32[]{:S(2)}) collective-permute-start(bf16[128,1152]{1,0:T(8,128)(2,1)} %refs_0_.1), channel_id=1, source_target_pairs={{0,1},{1,2},{2,3},{3,0},{4,5},{5,6},{6,7},{7,4},{8,11},{9,8},{10,9... | collective-permute-start | bytes 884744 | tf_op jit(solution)/shard_map/near1/ppermute | solution.py:56
  5.7 12.5 %collective-permute-start = (bf16[128,1152]{1,0:T(8,128)(2,1)}, bf16[128,1152]{1,0:T(8,128)(2,1)S(1)}, u32[]{:S(2)}, u32[]{:S(2)}) collective-permute-start(bf16[128,1152]{1,0:T(8,128)(2,1)} %refs_0_.1), channel_id=1, source_target_pairs={{0,4},{1,5},{2,6},{3,7},{4,0},{5,1},{6,2},{7,3},{8,12},{9,13},{10,... | collective-permute-start | bytes 884744 | tf_op jit(solution)/shard_map/across/ppermute | solution.py:46
  6.9 11.3 %collective-permute-start.2 = (bf16[128,1152]{1,0:T(8,128)(2,1)}, bf16[128,1152]{1,0:T(8,128)(2,1)S(1)}, u32[]{:S(2)}, u32[]{:S(2)}) collective-permute-start(bf16[128,1152]{1,0:T(8,128)(2,1)} %refs_0_.1), channel_id=1, source_target_pairs={{0,3},{1,0},{2,1},{3,2},{4,7},{5,4},{6,5},{7,6},{8,9},{9,10},{10,1... | collective-permute-start | bytes 884744 | tf_op jit(solution)/shard_map/near3/ppermute | solution.py:56
  14.1 22.6 %copy-start = (bf16[128,1152]{1,0:T(8,128)(2,1)}, bf16[128,1152]{1,0:T(8,128)(2,1)S(1)}, u32[]{:S(2)}) copy-start(bf16[128,1152]{1,0:T(8,128)(2,1)S(1)} %collective-permute-done.7.refs_11_) | copy-start | bytes 884740
  15.2 8.9 %collective-permute-start.8 = (bf16[128,1152]{1,0:T(8,128)(2,1)S(1)}, bf16[128,1152]{1,0:T(8,128)(2,1)S(1)}, u32[]{:S(2)}, u32[]{:S(2)}) collective-permute-start(bf16[128,1152]{1,0:T(8,128)(2,1)S(1)} %get-tuple-element.36), channel_id=1, source_target_pairs={{0,16},{8,24},{16,0},{24,8},{32,48},{40,56},{48,32},{56,40},{64,80... | collective-permute-start | bytes 884744 | tf_op jit(solution)/shard_map/behind1/ppermute | solution.py:41
  18.2 18.4 %copy-start.2 = (bf16[128,1152]{1,0:T(8,128)(2,1)}, bf16[128,1152]{1,0:T(8,128)(2,1)S(1)}, u32[]{:S(2)}) copy-start(bf16[128,1152]{1,0:T(8,128)(2,1)S(1)} %collective-permute-done.1.refs_2_) | copy-start | bytes 884740
  18.2 18.4 %copy-start.3 = (bf16[128,1152]{1,0:T(8,128)(2,1)}, bf16[128,1152]{1,0:T(8,128)(2,1)S(1)}, u32[]{:S(2)}) copy-start(bf16[128,1152]{1,0:T(8,128)(2,1)S(1)} %collective-permute-done.refs_1_) | copy-start | bytes 884740
  18.2 18.4 %copy-start.4 = (bf16[128,1152]{1,0:T(8,128)(2,1)}, bf16[128,1152]{1,0:T(8,128)(2,1)S(1)}, u32[]{:S(2)}) copy-start(bf16[128,1152]{1,0:T(8,128)(2,1)S(1)} %collective-permute-done.2.refs_6_) | copy-start | bytes 884740
  18.2 8.3 %collective-permute-start.3 = (bf16[128,1152]{1,0:T(8,128)(2,1)S(1)}, bf16[128,1152]{1,0:T(8,128)(2,1)S(1)}, u32[]{:S(2)}, u32[]{:S(2)}) collective-permute-start(bf16[128,1152]{1,0:T(8,128)(2,1)S(1)} %collective-permute-done.refs_1_), channel_id=1, source_target_pairs={{0,1},{1,2},{2,3},{3,0},{4,5},{5,6},{6,7},{7,4},{8,11},{9,8},{10,9... | collective-permute-start | bytes 884744 | tf_op jit(solution)/shard_map/far1/ppermute | solution.py:56
  20.8 6.7 %collective-permute-start.12 = (bf16[128,1152]{1,0:T(8,128)(2,1)S(1)}, bf16[128,1152]{1,0:T(8,128)(2,1)S(1)}, u32[]{:S(2)}, u32[]{:S(2)}) collective-permute-start(bf16[128,1152]{1,0:T(8,128)(2,1)S(1)} %collective-permute-done.7.refs_11_), channel_id=1, source_target_pairs={{0,8},{8,0},{16,24},{24,16},{32,40},{40,32},{48,56},{56,48},{64,72... | collective-permute-start | bytes 884744 | tf_op jit(solution)/shard_map/sibling2/ppermute | solution.py:32
  21.3 9.2 %collective-permute-start.6 = (bf16[128,1152]{1,0:T(8,128)(2,1)S(1)}, bf16[128,1152]{1,0:T(8,128)(2,1)S(1)}, u32[]{:S(2)}, u32[]{:S(2)}) collective-permute-start(bf16[128,1152]{1,0:T(8,128)(2,1)S(1)} %collective-permute-done.refs_1_), channel_id=1, source_target_pairs={{0,3},{1,0},{2,1},{3,2},{4,7},{5,4},{6,5},{7,6},{8,9},{9,10},{10,1... | collective-permute-start | bytes 884744 | tf_op jit(solution)/shard_map/far3/ppermute | solution.py:56
  24.1 12.6 %copy-start.5 = (bf16[128,1152]{1,0:T(8,128)(2,1)}, bf16[128,1152]{1,0:T(8,128)(2,1)S(1)}, u32[]{:S(2)}) copy-start(bf16[128,1152]{1,0:T(8,128)(2,1)S(1)} %collective-permute-done.8.refs_9_) | copy-start | bytes 884740
  24.1 7.6 %collective-permute-start.9 = (bf16[128,1152]{1,0:T(8,128)(2,1)S(1)}, bf16[128,1152]{1,0:T(8,128)(2,1)S(1)}, u32[]{:S(2)}, u32[]{:S(2)}) collective-permute-start(bf16[128,1152]{1,0:T(8,128)(2,1)S(1)} %collective-permute-done.8.refs_9_), channel_id=1, source_target_pairs={{0,32},{8,40},{16,48},{24,56},{32,64},{40,72},{48,80},{56,88},{64,... | collective-permute-start | bytes 884744 | tf_op jit(solution)/shard_map/behind3/ppermute | solution.py:32
  25.0 11.6 %collective-permute-start.4 = (bf16[128,1152]{1,0:T(8,128)(2,1)S(1)}, bf16[128,1152]{1,0:T(8,128)(2,1)S(1)}, u32[]{:S(2)}, u32[]{:S(2)}) collective-permute-start(bf16[128,1152]{1,0:T(8,128)(2,1)S(1)} %collective-permute-done.1.refs_2_), channel_id=1, source_target_pairs={{0,1},{1,2},{2,3},{3,0},{4,5},{5,6},{6,7},{7,4},{8,11},{9,8},{10,9... | collective-permute-start | bytes 884744 | tf_op jit(solution)/shard_map/near2/ppermute | solution.py:56
  26.5 10.1 %copy-start.6 = (bf16[128,1152]{1,0:T(8,128)(2,1)}, bf16[128,1152]{1,0:T(8,128)(2,1)S(1)}, u32[]{:S(2)}) copy-start(bf16[128,1152]{1,0:T(8,128)(2,1)S(1)} %collective-permute-done.3.refs_3_) | copy-start | bytes 884740
  26.5 10.0 %collective-permute-start.13 = (bf16[128,1152]{1,0:T(8,128)(2,1)S(1)}, bf16[128,1152]{1,0:T(8,128)(2,1)S(1)}, u32[]{:S(2)}, u32[]{:S(2)}) collective-permute-start(bf16[128,1152]{1,0:T(8,128)(2,1)S(1)} %get-tuple-element.35), channel_id=1, source_target_pairs={{0,8},{8,32},{16,24},{24,48},{32,40},{40,64},{48,56},{56,80},{64,7... | collective-permute-start | bytes 884744 | tf_op jit(solution)/shard_map/extra/ppermute | solution.py:32
  27.5 9.2 %copy-start.7 = (bf16[128,1152]{1,0:T(8,128)(2,1)}, bf16[128,1152]{1,0:T(8,128)(2,1)S(1)}, u32[]{:S(2)}) copy-start(bf16[128,1152]{1,0:T(8,128)(2,1)S(1)} %collective-permute-done.12.refs_14_) | copy-start | bytes 884740
  27.5 9.1 %collective-permute-start.5 = (bf16[128,1152]{1,0:T(8,128)(2,1)S(1)}, bf16[128,1152]{1,0:T(8,128)(2,1)S(1)}, u32[]{:S(2)}, u32[]{:S(2)}) collective-permute-start(bf16[128,1152]{1,0:T(8,128)(2,1)S(1)} %collective-permute-done.3.refs_3_), channel_id=1, source_target_pairs={{0,1},{1,2},{2,3},{3,0},{4,5},{5,6},{6,7},{7,4},{8,11},{9,8},{10,9... | collective-permute-start | bytes 884744 | tf_op jit(solution)/shard_map/far2/ppermute | solution.py:56
  30.5 6.1 %collective-permute-start.10 = (bf16[128,1152]{1,0:T(8,128)(2,1)S(1)}, bf16[128,1152]{1,0:T(8,128)(2,1)S(1)}, u32[]{:S(2)}, u32[]{:S(2)}) collective-permute-start(bf16[128,1152]{1,0:T(8,128)(2,1)S(1)} %collective-permute-done.8.refs_9_), channel_id=1, source_target_pairs={{0,8},{8,0},{16,24},{24,16},{32,40},{40,32},{48,56},{56,48},{64,72... | collective-permute-start | bytes 884744 | tf_op jit(solution)/shard_map/sibling1/ppermute | solution.py:32
  31.6 5.0 %collective-permute-start.11 = (bf16[128,1152]{1,0:T(8,128)(2,1)S(1)}, bf16[128,1152]{1,0:T(8,128)(2,1)}, u32[]{:S(2)}, u32[]{:S(2)}) collective-permute-start(bf16[128,1152]{1,0:T(8,128)(2,1)S(1)} %collective-permute-done.9.refs_10_), channel_id=1, source_target_pairs={{0,8},{8,0},{16,24},{24,16},{32,40},{40,32},{48,56},{56,48},{64,72... | collective-permute-start | bytes 884744 | tf_op jit(solution)/shard_map/sibling3/ppermute | solution.py:32
  53.1 6.1 %collective-permute-start.18 = (f32[384,1152]{1,0:T(8,128)}, f32[384,1152]{1,0:T(8,128)S(1)}, u32[]{:S(2)}, u32[]{:S(2)}) collective-permute-start(f32[384,1152]{1,0:T(8,128)} %get-tuple-element.30), channel_id=1, source_target_pairs={{0,8},{8,0},{16,24},{24,16},{32,40},{40,32},{48,56},{56,48},{64,72... | collective-permute-start | bytes 5308424 | tf_op jit(solution)/shard_map/back_sib/ppermute | solution.py:32
  54.3 22.8 %collective-permute-start.14 = (bf16[256,1152]{1,0:T(8,128)(2,1)}, bf16[256,1152]{1,0:T(8,128)(2,1)S(1)}, u32[]{:S(2)}, u32[]{:S(2)}) collective-permute-start(bf16[256,1152]{1,0:T(8,128)(2,1)} %get-tuple-element.23), channel_id=1, source_target_pairs={{0,3},{1,0},{2,1},{3,2},{4,7},{5,4},{6,5},{7,6},{8,9},{9,10},{10,1... | collective-permute-start | bytes 1769480 | tf_op jit(solution)/shard_map/back_x1/ppermute | solution.py:56
  55.7 26.2 %collective-permute-start.15 = (bf16[256,1152]{1,0:T(8,128)(2,1)}, bf16[256,1152]{1,0:T(8,128)(2,1)}, u32[]{:S(2)}, u32[]{:S(2)}) collective-permute-start(bf16[256,1152]{1,0:T(8,128)(2,1)} %get-tuple-element.24), channel_id=1, source_target_pairs={{0,2},{1,3},{2,0},{3,1},{4,6},{5,7},{6,4},{7,5},{8,10},{9,11},{10,... | collective-permute-start | bytes 1769480 | tf_op jit(solution)/shard_map/back_x2/ppermute | solution.py:56
  58.0 25.5 %collective-permute-start.16 = (bf16[256,1152]{1,0:T(8,128)(2,1)}, bf16[256,1152]{1,0:T(8,128)(2,1)}, u32[]{:S(2)}, u32[]{:S(2)}) collective-permute-start(bf16[256,1152]{1,0:T(8,128)(2,1)} %get-tuple-element.25), channel_id=1, source_target_pairs={{0,1},{1,2},{2,3},{3,0},{4,5},{5,6},{6,7},{7,4},{8,11},{9,8},{10,9... | collective-permute-start | bytes 1769480 | tf_op jit(solution)/shard_map/back_x3/ppermute | solution.py:56
  61.4 26.2 %collective-permute-start.20 = (bf16[256,1152]{1,0:T(8,128)(2,1)}, bf16[256,1152]{1,0:T(8,128)(2,1)S(1)}, u32[]{:S(2)}, u32[]{:S(2)}) collective-permute-start(bf16[256,1152]{1,0:T(8,128)(2,1)} %fusion), channel_id=1, source_target_pairs={{0,240},{8,248},{16,0},{24,8},{32,16},{40,24},{48,32},{56,40},{64,... | collective-permute-start | bytes 1769480 | tf_op jit(solution)/shard_map/back13/ppermute | solution.py:32
  65.1 22.4 %all-to-all-start = ((f32[32,8,128]{2,1,0:T(8,128)}), f32[32,8,128]{2,1,0:T(8,128)S(1)}, u32[]{:S(2)}, u32[]{:S(2)}) async-start(f32[32,8,128]{2,1,0:T(8,128)} %get-tuple-element.33), calls=%async_computation | async-start | bytes 262144 | tf_op jit(solution)/shard_map/loss_blk/all_to_all | solution.py:61
  71.1 16.5 %collective-permute-start.19 = (bf16[128,1152]{1,0:T(8,128)(2,1)}, bf16[128,1152]{1,0:T(8,128)(2,1)S(1)}, u32[]{:S(2)}, u32[]{:S(2)}) collective-permute-start(bf16[128,1152]{1,0:T(8,128)(2,1)} %get-tuple-element.31), channel_id=1, source_target_pairs={{0,232},{8,0},{16,248},{24,16},{32,8},{40,32},{48,24},{56,48},{64,... | collective-permute-start | bytes 884744 | tf_op jit(solution)/shard_map/back_extra/ppermute | solution.py:32
  85.9 9.3 %collective-permute-start.17 = (bf16[128,1152]{1,0:T(8,128)(2,1)}, bf16[128,1152]{1,0:T(8,128)(2,1)}, u32[]{:S(2)}, u32[]{:S(2)}) collective-permute-start(bf16[128,1152]{1,0:T(8,128)(2,1)} %fusion.49), channel_id=1, source_target_pairs={{0,4},{1,5},{2,6},{3,7},{4,0},{5,1},{6,2},{7,3},{8,12},{9,13},{10,... | collective-permute-start | bytes 884744 | tf_op jit(solution)/shard_map/back_across/ppermute | solution.py:46
  89.1 12.5 %copy-start.1 = (f32[128,1152]{1,0:T(8,128)S(1)}, f32[128,1152]{1,0:T(8,128)}, u32[]{:S(2)}) copy-start(f32[128,1152]{1,0:T(8,128)} %get-tuple-element.27) | copy-start | bytes 1769476
  89.1 12.5 %collective-permute-start.21 = (bf16[128,1152]{1,0:T(8,128)(2,1)S(1)}, bf16[128,1152]{1,0:T(8,128)(2,1)S(1)}, u32[]{:S(2)}, u32[]{:S(2)}) collective-permute-start(bf16[128,1152]{1,0:T(8,128)(2,1)S(1)} %fusion.47), channel_id=1, source_target_pairs={{0,224},{8,232},{16,240},{24,248},{32,0},{40,8},{48,16},{56,24},{6... | collective-permute-start | bytes 884744 | tf_op jit(solution)/shard_map/back2/ppermute | solution.py:32
  91.5 8.8 %all-to-all-start.1 = ((f32[8,8,128]{2,1,0:T(8,128)}), f32[8,8,128]{2,1,0:T(8,128)S(1)}, u32[]{:S(2)}, u32[]{:S(2)}) async-start(f32[8,8,128]{2,1,0:T(8,128)} %broadcast_in_dim.12), calls=%async_computation.1 | async-start | bytes 65536 | tf_op jit(solution)/shard_map/loss_group/all_to_all | solution.py:61
  (6 other events, 14.8 us)

commit v6 on v5

--- a/solution.py
+++ b/solution.py
@@ -249,7 +249,7 @@
     other = encode(other)
     last = swap_y(other, "back_across")
     loss = jnp.broadcast_to(loss[None], (lax.axis_size("group"), *loss.shape))
-    loss = jnp.sum(sum_over(after(loss, other, code2), "group"))
+    loss = jnp.sum(sum_over(after(loss, code2), "group"))
     for code in back:
         own = own + decode(code[:rows])
     grad_images = own + decode(last)

time: 105 us -> 105 us (level)
  no operation moved by 1% of the time
where the time goes in v6:
time: 105 us; the launch traced here: 104 us
  starting transfers between devices  46.8 us (45%)
  waiting for transfers between devices  24.3 us (23%)
  Pallas kernels  15.5 us (15%)
  other arithmetic  11.8 us (11%)
  between operations  3.97 us (4%)
  local copies, waits for them, and re-layouts  1.53 us (1%)
    ppermute x9, starting transfers between devices, ring_x(): return lax.ppermute(value, ('blk', 'group'), pairs)  15.6 us
    ppermute x10, starting transfers between devices, shift_blk(): return lax.ppermute(value, 'blk', pairs)  15.6 us
    pallas_call x1, Pallas kernels, pairs_part(): pl.pallas_call(pairs_kernel, out_shape=[jax.ShapeDtypeStruct((lax.axis_si...  15.5 us
    ppermute x9, waiting for transfers between devices, ring_x(): return lax.ppermute(value, ('blk', 'group'), pairs)  12.1 us
    all_to_all x2, starting transfers between devices, sum_over(): return jnp.sum(lax.all_to_all(value, axis, 0, 0), axis=0)  9.67 us
    ppermute x10, waiting for transfers between devices, shift_blk(): return lax.ppermute(value, 'blk', pairs)  8.27 us
    convert_element_type x3, other arithmetic, encode(): return (scaled * jnp.abs(scaled)).astype(jnp.bfloat16)  6.14 us
    ppermute x1, starting transfers between devices, flip_y(): lax.ppermute(value, 'blk', [(s, s ^ 2) for s in range(lax.axis_size('blk'...  3 us
  transfers between devices with their start and end apart: 24, of which 7 were waited for; matrix products, arithmetic and copies ran while one was open for 11% of the time, Pallas kernels for 0%

profile of v6, /device:TPU:1, one launch (start us, length us, event | category | flops | bytes accessed | tf_op | source)
XLA Modules:
  0.0 103.9 jit_solution(3505063184819981391)
XLA Ops:
  0.6 2.5 %collective-permute-start.7 = (bf16[128,1152]{1,0:T(8,128)(2,1)}, bf16[128,1152]{1,0:T(8,128)(2,1)S(1)}, u32[]{:S(2)}, u32[]{:S(2)}) collective-permute-start(bf16[128,1152]{1,0:T(8,128)(2,1)} %refs_8_.1), channel_id=1, source_target_pairs={{0,32},{8,40},{16,48},{24,56},{32,64},{40,72},{48,80},{56,88},{64,... | collective-permute-start | bytes 884744 | tf_op jit(solution)/shard_map/behind2/ppermute | solution.py:32
  3.2 2.5 %collective-permute-start.1 = (bf16[128,1152]{1,0:T(8,128)(2,1)}, bf16[128,1152]{1,0:T(8,128)(2,1)S(1)}, u32[]{:S(2)}, u32[]{:S(2)}) collective-permute-start(bf16[128,1152]{1,0:T(8,128)(2,1)} %refs_0_.1), channel_id=1, source_target_pairs={{0,1},{1,2},{2,3},{3,0},{4,5},{5,6},{6,7},{7,4},{8,11},{9,8},{10,9... | collective-permute-start | bytes 884744 | tf_op jit(solution)/shard_map/near1/ppermute | solution.py:56
  5.7 1.3 %collective-permute-start = (bf16[128,1152]{1,0:T(8,128)(2,1)}, bf16[128,1152]{1,0:T(8,128)(2,1)S(1)}, u32[]{:S(2)}, u32[]{:S(2)}) collective-permute-start(bf16[128,1152]{1,0:T(8,128)(2,1)} %refs_0_.1), channel_id=1, source_target_pairs={{0,4},{1,5},{2,6},{3,7},{4,0},{5,1},{6,2},{7,3},{8,12},{9,13},{10,... | collective-permute-start | bytes 884744 | tf_op jit(solution)/shard_map/across/ppermute | solution.py:46
  7.0 7.1 %collective-permute-done.7.refs_11_ = bf16[128,1152]{1,0:T(8,128)(2,1)S(1)} collective-permute-done((bf16[128,1152]{1,0:T(8,128)(2,1)}, bf16[128,1152]{1,0:T(8,128)(2,1)S(1)}, u32[]{:S(2)}, u32[]{:S(2)}) %collective-permute-start.7) | collective-permute-done | bytes 294944 | tf_op jit(solution)/shard_map/behind2/ppermute | solution.py:32
  14.1 1.1 %broadcast_select_fusion = (bf16[128,1152]{1,0:T(8,128)(2,1)S(1)}, bf16[128,1152]{1,0:T(8,128)(2,1)S(1)}) fusion(bf16[128,1152]{1,0:T(8,128)(2,1)} %refs_8_.1, bf16[128,1152]{1,0:T(8,128)(2,1)S(1)} %collective-permute-done.7.refs_11_, pred[]{:T(512)S(6)} %eq.14, pred[]{:T(512)S(6)} %eq.13), kind=kLoop, calls=%fused_computation.77 | loop fusion | flops 294912 | bytes 1179650 | tf_op jit(solution)/shard_map/jit(_where)/select_n | solution.py:224
  15.2 3.0 %collective-permute-start.8 = (bf16[128,1152]{1,0:T(8,128)(2,1)S(1)}, bf16[128,1152]{1,0:T(8,128)(2,1)S(1)}, u32[]{:S(2)}, u32[]{:S(2)}) collective-permute-start(bf16[128,1152]{1,0:T(8,128)(2,1)S(1)} %get-tuple-element.36), channel_id=1, source_target_pairs={{0,16},{8,24},{16,0},{24,8},{32,48},{40,56},{48,32},{56,40},{64,80... | collective-permute-start | bytes 884744 | tf_op jit(solution)/shard_map/behind1/ppermute | solution.py:41
  18.2 2.6 %collective-permute-start.3 = (bf16[128,1152]{1,0:T(8,128)(2,1)S(1)}, bf16[128,1152]{1,0:T(8,128)(2,1)S(1)}, u32[]{:S(2)}, u32[]{:S(2)}) collective-permute-start(bf16[128,1152]{1,0:T(8,128)(2,1)S(1)} %collective-permute-done.refs_1_), channel_id=1, source_target_pairs={{0,1},{1,2},{2,3},{3,0},{4,5},{5,6},{6,7},{7,4},{8,11},{9,8},{10,9... | collective-permute-start | bytes 884744 | tf_op jit(solution)/shard_map/far1/ppermute | solution.py:56
  21.3 1.2 %collective-permute-start.6 = (bf16[128,1152]{1,0:T(8,128)(2,1)S(1)}, bf16[128,1152]{1,0:T(8,128)(2,1)S(1)}, u32[]{:S(2)}, u32[]{:S(2)}) collective-permute-start(bf16[128,1152]{1,0:T(8,128)(2,1)S(1)} %collective-permute-done.refs_1_), channel_id=1, source_target_pairs={{0,3},{1,0},{2,1},{3,2},{4,7},{5,4},{6,5},{7,6},{8,9},{9,10},{10,1... | collective-permute-start | bytes 884744 | tf_op jit(solution)/shard_map/far3/ppermute | solution.py:56
  22.5 1.5 %collective-permute-done.8.refs_9_ = bf16[128,1152]{1,0:T(8,128)(2,1)S(1)} collective-permute-done((bf16[128,1152]{1,0:T(8,128)(2,1)S(1)}, bf16[128,1152]{1,0:T(8,128)(2,1)S(1)}, u32[]{:S(2)}, u32[]{:S(2)}) %collective-permute-start.8) | collective-permute-done | bytes 294944 | tf_op jit(solution)/shard_map/behind1/ppermute | solution.py:41
  25.0 1.6 %collective-permute-start.4 = (bf16[128,1152]{1,0:T(8,128)(2,1)S(1)}, bf16[128,1152]{1,0:T(8,128)(2,1)S(1)}, u32[]{:S(2)}, u32[]{:S(2)}) collective-permute-start(bf16[128,1152]{1,0:T(8,128)(2,1)S(1)} %collective-permute-done.1.refs_2_), channel_id=1, source_target_pairs={{0,1},{1,2},{2,3},{3,0},{4,5},{5,6},{6,7},{7,4},{8,11},{9,8},{10,9... | collective-permute-start | bytes 884744 | tf_op jit(solution)/shard_map/near2/ppermute | solution.py:56
  27.5 2.9 %collective-permute-start.5 = (bf16[128,1152]{1,0:T(8,128)(2,1)S(1)}, bf16[128,1152]{1,0:T(8,128)(2,1)S(1)}, u32[]{:S(2)}, u32[]{:S(2)}) collective-permute-start(bf16[128,1152]{1,0:T(8,128)(2,1)S(1)} %collective-permute-done.3.refs_3_), channel_id=1, source_target_pairs={{0,1},{1,2},{2,3},{3,0},{4,5},{5,6},{6,7},{7,4},{8,11},{9,8},{10,9... | collective-permute-start | bytes 884744 | tf_op jit(solution)/shard_map/far2/ppermute | solution.py:56
  30.5 1.1 %collective-permute-done.9.refs_10_ = bf16[128,1152]{1,0:T(8,128)(2,1)S(1)} collective-permute-done((bf16[128,1152]{1,0:T(8,128)(2,1)S(1)}, bf16[128,1152]{1,0:T(8,128)(2,1)S(1)}, u32[]{:S(2)}, u32[]{:S(2)}) %collective-permute-start.9) | collective-permute-done | bytes 294944 | tf_op jit(solution)/shard_map/behind3/ppermute | solution.py:32
  31.6 3.6 %collective-permute-start.11 = (bf16[128,1152]{1,0:T(8,128)(2,1)S(1)}, bf16[128,1152]{1,0:T(8,128)(2,1)}, u32[]{:S(2)}, u32[]{:S(2)}) collective-permute-start(bf16[128,1152]{1,0:T(8,128)(2,1)S(1)} %collective-permute-done.9.refs_10_), channel_id=1, source_target_pairs={{0,8},{8,0},{16,24},{24,16},{32,40},{40,32},{48,56},{56,48},{64,72... | collective-permute-start | bytes 884744 | tf_op jit(solution)/shard_map/sibling3/ppermute | solution.py:32
  37.6 15.5 %pairs_part.1 = (f32[32,8,128]{2,1,0:T(8,128)}, f32[128,1152]{1,0:T(8,128)}, f32[128,1152]{1,0:T(8,128)}, bf16[256,1152]{1,0:T(8,128)(2,1)}, bf16[256,1152]{1,0:...) custom-call(f32[1]{0:T(128)S(6)} %copy.7.scale, ...), custom_call_target="tpu_custom_call" | custom-call | flops 1 | bytes 1 | tf_op jit(solution)/shard_map/pairs_part/pallas_call | solution.py:177
  53.1 1.3 %collective-permute-start.18 = (f32[384,1152]{1,0:T(8,128)}, f32[384,1152]{1,0:T(8,128)S(1)}, u32[]{:S(2)}, u32[]{:S(2)}) collective-permute-start(f32[384,1152]{1,0:T(8,128)} %get-tuple-element.30), channel_id=1, source_target_pairs={{0,8},{8,0},{16,24},{24,16},{32,40},{40,32},{48,56},{56,48},{64,72... | collective-permute-start | bytes 5308424 | tf_op jit(solution)/shard_map/back_sib/ppermute | solution.py:32
  54.3 1.3 %collective-permute-start.14 = (bf16[256,1152]{1,0:T(8,128)(2,1)}, bf16[256,1152]{1,0:T(8,128)(2,1)S(1)}, u32[]{:S(2)}, u32[]{:S(2)}) collective-permute-start(bf16[256,1152]{1,0:T(8,128)(2,1)} %get-tuple-element.23), channel_id=1, source_target_pairs={{0,3},{1,0},{2,1},{3,2},{4,7},{5,4},{6,5},{7,6},{8,9},{9,10},{10,1... | collective-permute-start | bytes 1769480 | tf_op jit(solution)/shard_map/back_x1/ppermute | solution.py:56
  55.7 2.3 %collective-permute-start.15 = (bf16[256,1152]{1,0:T(8,128)(2,1)}, bf16[256,1152]{1,0:T(8,128)(2,1)}, u32[]{:S(2)}, u32[]{:S(2)}) collective-permute-start(bf16[256,1152]{1,0:T(8,128)(2,1)} %get-tuple-element.24), channel_id=1, source_target_pairs={{0,2},{1,3},{2,0},{3,1},{4,6},{5,7},{6,4},{7,5},{8,10},{9,11},{10,... | collective-permute-start | bytes 1769480 | tf_op jit(solution)/shard_map/back_x2/ppermute | solution.py:56
  58.0 1.2 %collective-permute-start.16 = (bf16[256,1152]{1,0:T(8,128)(2,1)}, bf16[256,1152]{1,0:T(8,128)(2,1)}, u32[]{:S(2)}, u32[]{:S(2)}) collective-permute-start(bf16[256,1152]{1,0:T(8,128)(2,1)} %get-tuple-element.25), channel_id=1, source_target_pairs={{0,1},{1,2},{2,3},{3,0},{4,5},{5,6},{6,7},{7,4},{8,11},{9,8},{10,9... | collective-permute-start | bytes 1769480 | tf_op jit(solution)/shard_map/back_x3/ppermute | solution.py:56
  59.2 2.3 %fusion = bf16[256,1152]{1,0:T(8,128)(2,1)} fusion(f32[384,1152]{1,0:T(8,128)S(1)} %collective-permute-done.18, f32[384,1152]{1,0:T(8,128)} %get-tuple-element.29), kind=kLoop, calls=%fused_computation.1 | loop fusion | flops 1474560 | bytes 2949120 | tf_op jit(solution)/shard_map/convert_element_type | solution.py:20
  61.4 3.7 %collective-permute-start.20 = (bf16[256,1152]{1,0:T(8,128)(2,1)}, bf16[256,1152]{1,0:T(8,128)(2,1)S(1)}, u32[]{:S(2)}, u32[]{:S(2)}) collective-permute-start(bf16[256,1152]{1,0:T(8,128)(2,1)} %fusion), channel_id=1, source_target_pairs={{0,240},{8,248},{16,0},{24,8},{32,16},{40,24},{48,32},{56,40},{64,... | collective-permute-start | bytes 1769480 | tf_op jit(solution)/shard_map/back13/ppermute | solution.py:32
  65.1 6.0 %all-to-all-start = ((f32[32,8,128]{2,1,0:T(8,128)}), f32[32,8,128]{2,1,0:T(8,128)S(1)}, u32[]{:S(2)}, u32[]{:S(2)}) async-start(f32[32,8,128]{2,1,0:T(8,128)} %get-tuple-element.33), calls=%async_computation | async-start | bytes 262144 | tf_op jit(solution)/shard_map/loss_blk/all_to_all | solution.py:61
  71.4 5.8 %collective-permute-done.14 = bf16[256,1152]{1,0:T(8,128)(2,1)S(1)} collective-permute-done((bf16[256,1152]{1,0:T(8,128)(2,1)}, bf16[256,1152]{1,0:T(8,128)(2,1)S(1)}, u32[]{:S(2)}, u32[]{:S(2)}) %collective-permute-start.14) | collective-permute-done | bytes 589856 | tf_op jit(solution)/shard_map/back_x1/ppermute | solution.py:56
  77.1 4.8 %collective-permute-done.15 = bf16[256,1152]{1,0:T(8,128)(2,1)} collective-permute-done((bf16[256,1152]{1,0:T(8,128)(2,1)}, bf16[256,1152]{1,0:T(8,128)(2,1)}, u32[]{:S(2)}, u32[]{:S(2)}) %collective-permute-start.15) | collective-permute-done | bytes 589856 | tf_op jit(solution)/shard_map/back_x2/ppermute | solution.py:56
  81.9 1.6 %collective-permute-done.16 = bf16[256,1152]{1,0:T(8,128)(2,1)} collective-permute-done((bf16[256,1152]{1,0:T(8,128)(2,1)}, bf16[256,1152]{1,0:T(8,128)(2,1)}, u32[]{:S(2)}, u32[]{:S(2)}) %collective-permute-start.16) | collective-permute-done | bytes 589856 | tf_op jit(solution)/shard_map/back_x3/ppermute | solution.py:56
  83.4 2.4 %fusion.49 = bf16[128,1152]{1,0:T(8,128)(2,1)} fusion(f32[128,1152]{1,0:T(8,128)} %get-tuple-element.26, bf16[256,1152]{1,0:T(8,128)(2,1)} %collective-permute-done.16, bf16[256,1152]{1,0:T(8,128)(2,1)} %collective-permute-done.15, bf16[256,1152]{1,0:T(8,128)(2,1)S(1)} %collective-permute-done.14), kind=kLoop, calls=%fused_computation.76 | loop fusion | flops 3244032 | bytes 1769472 | tf_op jit(solution)/shard_map/convert_element_type | solution.py:20
  85.9 1.7 %collective-permute-start.17 = (bf16[128,1152]{1,0:T(8,128)(2,1)}, bf16[128,1152]{1,0:T(8,128)(2,1)}, u32[]{:S(2)}, u32[]{:S(2)}) collective-permute-start(bf16[128,1152]{1,0:T(8,128)(2,1)} %fusion.49), channel_id=1, source_target_pairs={{0,4},{1,5},{2,6},{3,7},{4,0},{5,1},{6,2},{7,3},{8,12},{9,13},{10,... | collective-permute-start | bytes 884744 | tf_op jit(solution)/shard_map/back_across/ppermute | solution.py:46
  87.6 1.4 %fusion.47 = bf16[128,1152]{1,0:T(8,128)(2,1)S(1)} fusion(f32[384,1152]{1,0:T(8,128)S(1)} %collective-permute-done.18, f32[384,1152]{1,0:T(8,128)} %get-tuple-element.29, bf16[128,1152]{1,0:T(8,128)(2,1)S(1)} %collective-permute-done.19, bf16[256,1152]{1,0:T(8,128)(2,1)S(1)} %collective-permute-done.20, pred[]{:T(512)S(6)} %eq.15), kind=kLoop, calls=%fused_computation.73 | loop fusion | flops 2654208 | bytes 2064385 | tf_op jit(solution)/shard_map/convert_element_type | solution.py:20
  89.1 1.8 %collective-permute-start.21 = (bf16[128,1152]{1,0:T(8,128)(2,1)S(1)}, bf16[128,1152]{1,0:T(8,128)(2,1)S(1)}, u32[]{:S(2)}, u32[]{:S(2)}) collective-permute-start(bf16[128,1152]{1,0:T(8,128)(2,1)S(1)} %fusion.47), channel_id=1, source_target_pairs={{0,224},{8,232},{16,240},{24,248},{32,0},{40,8},{48,16},{56,24},{6... | collective-permute-start | bytes 884744 | tf_op jit(solution)/shard_map/back2/ppermute | solution.py:32
  91.5 3.7 %all-to-all-start.1 = ((f32[8,8,128]{2,1,0:T(8,128)}), f32[8,8,128]{2,1,0:T(8,128)S(1)}, u32[]{:S(2)}, u32[]{:S(2)}) async-start(f32[8,8,128]{2,1,0:T(8,128)} %broadcast_in_dim.12), calls=%async_computation.1 | async-start | bytes 65536 | tf_op jit(solution)/shard_map/loss_group/all_to_all | solution.py:61
  95.2 2.7 %fusion.8 = f32[128,1152]{1,0:T(8,128)} fusion(f32[128,1152]{1,0:T(8,128)} %get-tuple-element.22, bf16[128,1152]{1,0:T(8,128)(2,1)} %collective-permute-done.17, bf16[256,1152]{1,0:T(8,128)(2,1)} %collective-permute-done.16, bf16[256,1152]{1,0:T(8,128)(2,1)} %collective-permute-done.15, bf16[256,1152]{1,0:T(8,128)(2,1)S(1)} %collective-permute-done.14), kind=kLoop, calls=%fused_computation.34 | loop fusion | flops 3538944 | bytes 2359296 | tf_op jit(solution)/shard_map/add | solution.py:255
  97.9 2.4 %all-to-all-done.1 = f32[8,8,128]{2,1,0:T(8,128)S(1)} async-done(((f32[8,8,128]{2,1,0:T(8,128)}), f32[8,8,128]{2,1,0:T(8,128)S(1)}, u32[]{:S(2)}, u32[]{:S(2)}) %all-to-all-start.1) | async-done | bytes 32800 | tf_op jit(solution)/shard_map/loss_group/all_to_all | solution.py:61
  101.6 1.2 %fusion.38 = f32[128,1152]{1,0:T(8,128)} fusion(bf16[128,1152]{1,0:T(8,128)(2,1)S(1)} %collective-permute-done.21, f32[128,1152]{1,0:T(8,128)S(1)} %copy-done.1, bf16[128,1152]{1,0:T(8,128)(2,1)S(1)} %collective-permute-done.19, bf16[256,1152]{1,0:T(8,128)(2,1)S(1)} %collective-permute-done.20, pred[]{:T(512)S(6)} %eq.14), kind=kLoop, calls=%fused_computation.64 | loop fusion | flops 2801664 | bytes 2064385 | tf_op jit(solution)/shard_map/add | solution.py:256
  (54 shorter events, 4.9 us)
Async XLA Ops:
  0.6 13.4 %collective-permute-start.7 = (bf16[128,1152]{1,0:T(8,128)(2,1)}, bf16[128,1152]{1,0:T(8,128)(2,1)S(1)}, u32[]{:S(2)}, u32[]{:S(2)}) collective-permute-start(bf16[128,1152]{1,0:T(8,128)(2,1)} %refs_8_.1), channel_id=1, source_target_pairs={{0,32},{8,40},{16,48},{24,56},{32,64},{40,72},{48,80},{56,88},{64,... | collective-permute-start | bytes 884744 | tf_op jit(solution)/shard_map/behind2/ppermute | solution.py:32
  3.2 15.0 %collective-permute-start.1 = (bf16[128,1152]{1,0:T(8,128)(2,1)}, bf16[128,1152]{1,0:T(8,128)(2,1)S(1)}, u32[]{:S(2)}, u32[]{:S(2)}) collective-permute-start(bf16[128,1152]{1,0:T(8,128)(2,1)} %refs_0_.1), channel_id=1, source_target_pairs={{0,1},{1,2},{2,3},{3,0},{4,5},{5,6},{6,7},{7,4},{8,11},{9,8},{10,9... | collective-permute-start | bytes 884744 | tf_op jit(solution)/shard_map/near1/ppermute | solution.py:56
  5.7 12.5 %collective-permute-start = (bf16[128,1152]{1,0:T(8,128)(2,1)}, bf16[128,1152]{1,0:T(8,128)(2,1)S(1)}, u32[]{:S(2)}, u32[]{:S(2)}) collective-permute-start(bf16[128,1152]{1,0:T(8,128)(2,1)} %refs_0_.1), channel_id=1, source_target_pairs={{0,4},{1,5},{2,6},{3,7},{4,0},{5,1},{6,2},{7,3},{8,12},{9,13},{10,... | collective-permute-start | bytes 884744 | tf_op jit(solution)/shard_map/across/ppermute | solution.py:46
  6.9 11.3 %collective-permute-start.2 = (bf16[128,1152]{1,0:T(8,128)(2,1)}, bf16[128,1152]{1,0:T(8,128)(2,1)S(1)}, u32[]{:S(2)}, u32[]{:S(2)}) collective-permute-start(bf16[128,1152]{1,0:T(8,128)(2,1)} %refs_0_.1), channel_id=1, source_target_pairs={{0,3},{1,0},{2,1},{3,2},{4,7},{5,4},{6,5},{7,6},{8,9},{9,10},{10,1... | collective-permute-start | bytes 884744 | tf_op jit(solution)/shard_map/near3/ppermute | solution.py:56
  14.1 22.6 %copy-start = (bf16[128,1152]{1,0:T(8,128)(2,1)}, bf16[128,1152]{1,0:T(8,128)(2,1)S(1)}, u32[]{:S(2)}) copy-start(bf16[128,1152]{1,0:T(8,128)(2,1)S(1)} %collective-permute-done.7.refs_11_) | copy-start | bytes 884740
  15.2 8.9 %collective-permute-start.8 = (bf16[128,1152]{1,0:T(8,128)(2,1)S(1)}, bf16[128,1152]{1,0:T(8,128)(2,1)S(1)}, u32[]{:S(2)}, u32[]{:S(2)}) collective-permute-start(bf16[128,1152]{1,0:T(8,128)(2,1)S(1)} %get-tuple-element.36), channel_id=1, source_target_pairs={{0,16},{8,24},{16,0},{24,8},{32,48},{40,56},{48,32},{56,40},{64,80... | collective-permute-start | bytes 884744 | tf_op jit(solution)/shard_map/behind1/ppermute | solution.py:41
  18.2 18.4 %copy-start.2 = (bf16[128,1152]{1,0:T(8,128)(2,1)}, bf16[128,1152]{1,0:T(8,128)(2,1)S(1)}, u32[]{:S(2)}) copy-start(bf16[128,1152]{1,0:T(8,128)(2,1)S(1)} %collective-permute-done.1.refs_2_) | copy-start | bytes 884740
  18.2 18.4 %copy-start.3 = (bf16[128,1152]{1,0:T(8,128)(2,1)}, bf16[128,1152]{1,0:T(8,128)(2,1)S(1)}, u32[]{:S(2)}) copy-start(bf16[128,1152]{1,0:T(8,128)(2,1)S(1)} %collective-permute-done.refs_1_) | copy-start | bytes 884740
  18.2 18.4 %copy-start.4 = (bf16[128,1152]{1,0:T(8,128)(2,1)}, bf16[128,1152]{1,0:T(8,128)(2,1)S(1)}, u32[]{:S(2)}) copy-start(bf16[128,1152]{1,0:T(8,128)(2,1)S(1)} %collective-permute-done.2.refs_6_) | copy-start | bytes 884740
  18.2 8.3 %collective-permute-start.3 = (bf16[128,1152]{1,0:T(8,128)(2,1)S(1)}, bf16[128,1152]{1,0:T(8,128)(2,1)S(1)}, u32[]{:S(2)}, u32[]{:S(2)}) collective-permute-start(bf16[128,1152]{1,0:T(8,128)(2,1)S(1)} %collective-permute-done.refs_1_), channel_id=1, source_target_pairs={{0,1},{1,2},{2,3},{3,0},{4,5},{5,6},{6,7},{7,4},{8,11},{9,8},{10,9... | collective-permute-start | bytes 884744 | tf_op jit(solution)/shard_map/far1/ppermute | solution.py:56
  20.8 6.7 %collective-permute-start.12 = (bf16[128,1152]{1,0:T(8,128)(2,1)S(1)}, bf16[128,1152]{1,0:T(8,128)(2,1)S(1)}, u32[]{:S(2)}, u32[]{:S(2)}) collective-permute-start(bf16[128,1152]{1,0:T(8,128)(2,1)S(1)} %collective-permute-done.7.refs_11_), channel_id=1, source_target_pairs={{0,8},{8,0},{16,24},{24,16},{32,40},{40,32},{48,56},{56,48},{64,72... | collective-permute-start | bytes 884744 | tf_op jit(solution)/shard_map/sibling2/ppermute | solution.py:32
  21.3 9.2 %collective-permute-start.6 = (bf16[128,1152]{1,0:T(8,128)(2,1)S(1)}, bf16[128,1152]{1,0:T(8,128)(2,1)S(1)}, u32[]{:S(2)}, u32[]{:S(2)}) collective-permute-start(bf16[128,1152]{1,0:T(8,128)(2,1)S(1)} %collective-permute-done.refs_1_), channel_id=1, source_target_pairs={{0,3},{1,0},{2,1},{3,2},{4,7},{5,4},{6,5},{7,6},{8,9},{9,10},{10,1... | collective-permute-start | bytes 884744 | tf_op jit(solution)/shard_map/far3/ppermute | solution.py:56
  24.1 12.6 %copy-start.5 = (bf16[128,1152]{1,0:T(8,128)(2,1)}, bf16[128,1152]{1,0:T(8,128)(2,1)S(1)}, u32[]{:S(2)}) copy-start(bf16[128,1152]{1,0:T(8,128)(2,1)S(1)} %collective-permute-done.8.refs_9_) | copy-start | bytes 884740
  24.1 7.6 %collective-permute-start.9 = (bf16[128,1152]{1,0:T(8,128)(2,1)S(1)}, bf16[128,1152]{1,0:T(8,128)(2,1)S(1)}, u32[]{:S(2)}, u32[]{:S(2)}) collective-permute-start(bf16[128,1152]{1,0:T(8,128)(2,1)S(1)} %collective-permute-done.8.refs_9_), channel_id=1, source_target_pairs={{0,32},{8,40},{16,48},{24,56},{32,64},{40,72},{48,80},{56,88},{64,... | collective-permute-start | bytes 884744 | tf_op jit(solution)/shard_map/behind3/ppermute | solution.py:32
  25.0 11.6 %collective-permute-start.4 = (bf16[128,1152]{1,0:T(8,128)(2,1)S(1)}, bf16[128,1152]{1,0:T(8,128)(2,1)S(1)}, u32[]{:S(2)}, u32[]{:S(2)}) collective-permute-start(bf16[128,1152]{1,0:T(8,128)(2,1)S(1)} %collective-permute-done.1.refs_2_), channel_id=1, source_target_pairs={{0,1},{1,2},{2,3},{3,0},{4,5},{5,6},{6,7},{7,4},{8,11},{9,8},{10,9... | collective-permute-start | bytes 884744 | tf_op jit(solution)/shard_map/near2/ppermute | solution.py:56
  26.5 10.1 %copy-start.6 = (bf16[128,1152]{1,0:T(8,128)(2,1)}, bf16[128,1152]{1,0:T(8,128)(2,1)S(1)}, u32[]{:S(2)}) copy-start(bf16[128,1152]{1,0:T(8,128)(2,1)S(1)} %collective-permute-done.3.refs_3_) | copy-start | bytes 884740
  26.5 10.0 %collective-permute-start.13 = (bf16[128,1152]{1,0:T(8,128)(2,1)S(1)}, bf16[128,1152]{1,0:T(8,128)(2,1)S(1)}, u32[]{:S(2)}, u32[]{:S(2)}) collective-permute-start(bf16[128,1152]{1,0:T(8,128)(2,1)S(1)} %get-tuple-element.35), channel_id=1, source_target_pairs={{0,8},{8,32},{16,24},{24,48},{32,40},{40,64},{48,56},{56,80},{64,7... | collective-permute-start | bytes 884744 | tf_op jit(solution)/shard_map/extra/ppermute | solution.py:32
  27.5 9.2 %copy-start.7 = (bf16[128,1152]{1,0:T(8,128)(2,1)}, bf16[128,1152]{1,0:T(8,128)(2,1)S(1)}, u32[]{:S(2)}) copy-start(bf16[128,1152]{1,0:T(8,128)(2,1)S(1)} %collective-permute-done.12.refs_14_) | copy-start | bytes 884740
  27.5 9.1 %collective-permute-start.5 = (bf16[128,1152]{1,0:T(8,128)(2,1)S(1)}, bf16[128,1152]{1,0:T(8,128)(2,1)S(1)}, u32[]{:S(2)}, u32[]{:S(2)}) collective-permute-start(bf16[128,1152]{1,0:T(8,128)(2,1)S(1)} %collective-permute-done.3.refs_3_), channel_id=1, source_target_pairs={{0,1},{1,2},{2,3},{3,0},{4,5},{5,6},{6,7},{7,4},{8,11},{9,8},{10,9... | collective-permute-start | bytes 884744 | tf_op jit(solution)/shard_map/far2/ppermute | solution.py:56
  30.5 6.1 %collective-permute-start.10 = (bf16[128,1152]{1,0:T(8,128)(2,1)S(1)}, bf16[128,1152]{1,0:T(8,128)(2,1)S(1)}, u32[]{:S(2)}, u32[]{:S(2)}) collective-permute-start(bf16[128,1152]{1,0:T(8,128)(2,1)S(1)} %collective-permute-done.8.refs_9_), channel_id=1, source_target_pairs={{0,8},{8,0},{16,24},{24,16},{32,40},{40,32},{48,56},{56,48},{64,72... | collective-permute-start | bytes 884744 | tf_op jit(solution)/shard_map/sibling1/ppermute | solution.py:32
  31.6 5.0 %collective-permute-start.11 = (bf16[128,1152]{1,0:T(8,128)(2,1)S(1)}, bf16[128,1152]{1,0:T(8,128)(2,1)}, u32[]{:S(2)}, u32[]{:S(2)}) collective-permute-start(bf16[128,1152]{1,0:T(8,128)(2,1)S(1)} %collective-permute-done.9.refs_10_), channel_id=1, source_target_pairs={{0,8},{8,0},{16,24},{24,16},{32,40},{40,32},{48,56},{56,48},{64,72... | collective-permute-start | bytes 884744 | tf_op jit(solution)/shard_map/sibling3/ppermute | solution.py:32
  53.1 6.1 %collective-permute-start.18 = (f32[384,1152]{1,0:T(8,128)}, f32[384,1152]{1,0:T(8,128)S(1)}, u32[]{:S(2)}, u32[]{:S(2)}) collective-permute-start(f32[384,1152]{1,0:T(8,128)} %get-tuple-element.30), channel_id=1, source_target_pairs={{0,8},{8,0},{16,24},{24,16},{32,40},{40,32},{48,56},{56,48},{64,72... | collective-permute-start | bytes 5308424 | tf_op jit(solution)/shard_map/back_sib/ppermute | solution.py:32
  54.3 22.8 %collective-permute-start.14 = (bf16[256,1152]{1,0:T(8,128)(2,1)}, bf16[256,1152]{1,0:T(8,128)(2,1)S(1)}, u32[]{:S(2)}, u32[]{:S(2)}) collective-permute-start(bf16[256,1152]{1,0:T(8,128)(2,1)} %get-tuple-element.23), channel_id=1, source_target_pairs={{0,3},{1,0},{2,1},{3,2},{4,7},{5,4},{6,5},{7,6},{8,9},{9,10},{10,1... | collective-permute-start | bytes 1769480 | tf_op jit(solution)/shard_map/back_x1/ppermute | solution.py:56
  55.7 26.2 %collective-permute-start.15 = (bf16[256,1152]{1,0:T(8,128)(2,1)}, bf16[256,1152]{1,0:T(8,128)(2,1)}, u32[]{:S(2)}, u32[]{:S(2)}) collective-permute-start(bf16[256,1152]{1,0:T(8,128)(2,1)} %get-tuple-element.24), channel_id=1, source_target_pairs={{0,2},{1,3},{2,0},{3,1},{4,6},{5,7},{6,4},{7,5},{8,10},{9,11},{10,... | collective-permute-start | bytes 1769480 | tf_op jit(solution)/shard_map/back_x2/ppermute | solution.py:56
  58.0 25.5 %collective-permute-start.16 = (bf16[256,1152]{1,0:T(8,128)(2,1)}, bf16[256,1152]{1,0:T(8,128)(2,1)}, u32[]{:S(2)}, u32[]{:S(2)}) collective-permute-start(bf16[256,1152]{1,0:T(8,128)(2,1)} %get-tuple-element.25), channel_id=1, source_target_pairs={{0,1},{1,2},{2,3},{3,0},{4,5},{5,6},{6,7},{7,4},{8,11},{9,8},{10,9... | collective-permute-start | bytes 1769480 | tf_op jit(solution)/shard_map/back_x3/ppermute | solution.py:56
  61.4 26.2 %collective-permute-start.20 = (bf16[256,1152]{1,0:T(8,128)(2,1)}, bf16[256,1152]{1,0:T(8,128)(2,1)S(1)}, u32[]{:S(2)}, u32[]{:S(2)}) collective-permute-start(bf16[256,1152]{1,0:T(8,128)(2,1)} %fusion), channel_id=1, source_target_pairs={{0,240},{8,248},{16,0},{24,8},{32,16},{40,24},{48,32},{56,40},{64,... | collective-permute-start | bytes 1769480 | tf_op jit(solution)/shard_map/back13/ppermute | solution.py:32
  65.1 22.4 %all-to-all-start = ((f32[32,8,128]{2,1,0:T(8,128)}), f32[32,8,128]{2,1,0:T(8,128)S(1)}, u32[]{:S(2)}, u32[]{:S(2)}) async-start(f32[32,8,128]{2,1,0:T(8,128)} %get-tuple-element.33), calls=%async_computation | async-start | bytes 262144 | tf_op jit(solution)/shard_map/loss_blk/all_to_all | solution.py:61
  71.1 16.5 %collective-permute-start.19 = (bf16[128,1152]{1,0:T(8,128)(2,1)}, bf16[128,1152]{1,0:T(8,128)(2,1)S(1)}, u32[]{:S(2)}, u32[]{:S(2)}) collective-permute-start(bf16[128,1152]{1,0:T(8,128)(2,1)} %get-tuple-element.31), channel_id=1, source_target_pairs={{0,232},{8,0},{16,248},{24,16},{32,8},{40,32},{48,24},{56,48},{64,... | collective-permute-start | bytes 884744 | tf_op jit(solution)/shard_map/back_extra/ppermute | solution.py:32
  85.9 9.3 %collective-permute-start.17 = (bf16[128,1152]{1,0:T(8,128)(2,1)}, bf16[128,1152]{1,0:T(8,128)(2,1)}, u32[]{:S(2)}, u32[]{:S(2)}) collective-permute-start(bf16[128,1152]{1,0:T(8,128)(2,1)} %fusion.49), channel_id=1, source_target_pairs={{0,4},{1,5},{2,6},{3,7},{4,0},{5,1},{6,2},{7,3},{8,12},{9,13},{10,... | collective-permute-start | bytes 884744 | tf_op jit(solution)/shard_map/back_across/ppermute | solution.py:46
  89.1 12.5 %copy-start.1 = (f32[128,1152]{1,0:T(8,128)S(1)}, f32[128,1152]{1,0:T(8,128)}, u32[]{:S(2)}) copy-start(f32[128,1152]{1,0:T(8,128)} %get-tuple-element.27) | copy-start | bytes 1769476
  89.1 12.5 %collective-permute-start.21 = (bf16[128,1152]{1,0:T(8,128)(2,1)S(1)}, bf16[128,1152]{1,0:T(8,128)(2,1)S(1)}, u32[]{:S(2)}, u32[]{:S(2)}) collective-permute-start(bf16[128,1152]{1,0:T(8,128)(2,1)S(1)} %fusion.47), channel_id=1, source_target_pairs={{0,224},{8,232},{16,240},{24,248},{32,0},{40,8},{48,16},{56,24},{6... | collective-permute-start | bytes 884744 | tf_op jit(solution)/shard_map/back2/ppermute | solution.py:32
  91.5 8.8 %all-to-all-start.1 = ((f32[8,8,128]{2,1,0:T(8,128)}), f32[8,8,128]{2,1,0:T(8,128)S(1)}, u32[]{:S(2)}, u32[]{:S(2)}) async-start(f32[8,8,128]{2,1,0:T(8,128)} %broadcast_in_dim.12), calls=%async_computation.1 | async-start | bytes 65536 | tf_op jit(solution)/shard_map/loss_group/all_to_all | solution.py:61
  (6 other events, 14.8 us)
